TPU v7x, 128 devices: a whole 4x4x4 slice. The times are simulated.
128 devices in a mesh: row: 2 (over y_lo), col: 8 (over x, core), layer: 8 (over y_hi, z).
Axes of the slice: x: 4, y: 4 (y_hi: 2, y_lo: 2; y = y_hi * 2 + y_lo), z: 4, core: 2. Of those that a mesh axis runs over, the one named last changes fastest.
Arguments:
- left: float32 [1024, 8192], P('row', ('layer', 'col')), may hold values from -6 to 6
- right: float32 [8192, 16384], P(('layer', 'row'), 'col'), may hold values from -0.125 to 0.125
- left_mask: int32 [2, 16], replicated, may hold values 0 or 1
- right_mask: int32 [16, 32], replicated, may hold values 0 or 1
- result_mask: int32 [2, 32], replicated, may hold values 0 or 1
Outputs:
- ladder: float32 [1024, 16384], P('row', ('col', 'layer'))
Inputs may be any that keep to these rules, and one draw needn't show every extreme that they name: `left_mask`: 1 marks a present tile, 0 an absent one. `right_mask`: 1 marks a present tile, 0 an absent one. `result_mask`: 1 marks a present tile, 0 an absent one.
All inputs are finite; a program needn't handle non-finite values.
Results may differ from a plain program's by a relative error of at most 0.0003.
Values sent between devices are 32-bit elements; how exact they have to be, the bound alone decides.
No kernel may reach another device: no remote copies, remote signals or barrier semaphores. Data moves between devices by JAX's collectives and lax.ppermute only.
A program may use at most 64 MiB of HBM per device.

v0:
```python
import jax
import jax.numpy as jnp
from jax import lax
from jax.sharding import Mesh
from jax.sharding import PartitionSpec as P

TILE = 512
LAYER = ("layer_0", "layer_1")
LAYER_COL = ("layer_0", "layer_1", "col")
LAYER_ROW = ("layer_0", "layer_1", "row")
COL_LAYER = ("col", "layer_0", "layer_1")


def in_order(tiles, dim):
    tiles = jnp.moveaxis(tiles, 0, dim)
    lengths = tiles.shape
    return tiles.reshape(*lengths[:dim], lengths[dim] * lengths[dim + 1], *lengths[dim + 2 :])


def copy_for_each(value, axis):
    length = lax.axis_size(axis)
    return lax.all_to_all(
        jnp.broadcast_to(value[None], (length, *value.shape)), axis, 0, 0, tiled=True
    )


def gather_directly(value, axis, dim):
    return in_order(copy_for_each(value, axis), dim)


def sum_in_order(tiles, axes, turns):
    lengths = [lax.axis_size(a) for a in axes]
    tiles = tiles.reshape(*lengths, *tiles.shape[1:])
    tiles = tiles.transpose(*turns, *range(len(axes), tiles.ndim))
    tiles = tiles.reshape(-1, *tiles.shape[len(axes) :])
    for k in turns:
        tiles = lax.psum_scatter(tiles, axes[k], scatter_dimension=0, tiled=True)
    return tiles[0]


def split_up(value, dim, length):
    before, after = (value.shape[:dim], value.shape[dim + 1 :])
    return jnp.moveaxis(value.reshape(*before, length, -1, *after), dim, 0)


def scatter_axes(value, axes, turns, dim):
    length = lax.axis_size(axes)
    return sum_in_order(split_up(value, dim, length), axes, turns)


def expand(table, row_start, rows, col_start, cols):
    row_ids = (row_start + jnp.arange(rows, dtype=jnp.int32)) // TILE
    col_ids = (col_start + jnp.arange(cols, dtype=jnp.int32)) // TILE
    row_sel = (row_ids[:, None] == jnp.arange(table.shape[0], dtype=jnp.int32)[None, :]).astype(
        jnp.float32
    )
    col_sel = (col_ids[:, None] == jnp.arange(table.shape[1], dtype=jnp.int32)[None, :]).astype(
        jnp.float32
    )
    inner = jnp.dot(row_sel, table.astype(jnp.float32), precision=lax.Precision.HIGHEST)
    return jnp.dot(inner, col_sel.T, precision=lax.Precision.HIGHEST)


def shards(left, right, left_mask, right_mask, result_mask):
    rows, left_cols = left.shape
    right_rows, right_cols = right.shape
    row_pos = lax.axis_index("row")
    col_pos = lax.axis_index("col")
    layer_pos = lax.axis_index(LAYER)
    col_count = lax.axis_size("col")
    row_count = lax.axis_size("row")
    layer_count = lax.axis_size(LAYER)
    left_start = (layer_pos * col_count + col_pos) * left_cols
    right_start = (layer_pos * row_count + row_pos) * right_rows
    left_used = left * expand(left_mask, row_pos * rows, rows, left_start, left_cols)
    right_used = right * expand(
        right_mask, right_start, right_rows, col_pos * right_cols, right_cols
    )
    out_cols = right_cols // layer_count
    slab = lax.all_gather(right_used, "row", axis=0, tiled=True)
    partial_sum = jnp.dot(
        gather_directly(left_used, "col", 1),
        slab,
        precision=lax.Precision.HIGHEST,
        preferred_element_type=jnp.float32,
    )
    product = scatter_axes(partial_sum, LAYER, (1, 0), 1)
    keep = expand(
        result_mask, row_pos * rows, rows, (col_pos * layer_count + layer_pos) * out_cols, out_cols
    )
    return product * keep


def solution(mesh):
    torus = Mesh(
        mesh.devices.reshape(mesh.shape["row"], mesh.shape["col"], 2, 4),
        ("row", "col", "layer_0", "layer_1"),
    )
    in_specs = (P("row", LAYER_COL), P(LAYER_ROW, "col"), P(), P(), P())
    out_specs = P("row", COL_LAYER)
    return jax.shard_map(
        shards, mesh=torus, in_specs=in_specs, out_specs=out_specs, check_vma=False
    )
```

profile of v0, /device:TPU:0, one launch (start us, length us, event | category | flops | bytes accessed | tf_op | source)
XLA Modules:
  0.0 233.0 jit_solution(13741390561035306401)
XLA Ops:
  6.6 1.0 fusion.3
  7.6 5.1 %convolution_multiply_fusion = f32[512,2048]{1,0:T(8,128)} fusion(f32[512,2048]{1,0:T(8,128)} %param.6, f32[512,32]{1,0:T(8,128)S(1)} %fusion.3, s32[2048]{0:T(1024)S(1)} %add_select_fusion), kind=kOutput, calls=%fused_computation | convolution fusion | flops 403767296 | bytes 8462336 | tf_op jit(solution)/shard_map/dot_general | solution.py:61
  12.7 0.0 all-gather.2.cloned.1.call-update
  12.8 0.0 reduce-scatter.3.cloned.1.call-start
  12.8 0.6 copy-done.2
  13.4 0.3 fusion.2
  13.7 0.0 copy-done.1
  13.7 0.4 convolution_multiply_fusion.2
  14.1 0.1 broadcast_in_dim.2
  14.2 31.7 %all_to_all.5 = f32[8,512,128]{2,1,0:T(8,128)S(1)} all-to-all(f32[8,512,128]{2,1,0:T(8,128)S(1)} %broadcast_in_dim.2), channel_id=1, replica_groups=mesh['row'=2,'col'=8,'layer_0'=2,'layer_1'=4] {'col'}, dimensions={0} | all-to-all | bytes 4194304 | tf_op jit(solution)/shard_map/all_to_all | solution.py:22
  45.9 1.2 copy.8
  47.2 1.5 reshape.110
  48.7 73.2 %all-gather.2.cloned.1.call-done = f32[1024,2048]{1,0:T(8,128)} async-done(((f32[512,2048]{1,0:T(8,128)}), f32[1024,2048]{1,0:T(8,128)}) %all-gather.2.cloned.1.call-update) | async-done | bytes 8388624 | tf_op jit(solution)/shard_map/all_gather | solution.py:80
  121.9 9.4 %copy.11 = f32[2048,1024]{1,0:T(8,128)} copy(f32[2048,1024]{0,1:T(8,128)} %bitcast.17) | data formatting | bytes 16777216 | tf_op jit(solution)/shard_map/dot_general | solution.py:81
  131.3 0.0 copy-done
  131.3 16.1 %fusion.21 = f32[512,8,256]{2,0,1:T(8,128)S(1)} fusion(f32[512,1024,1]{1,0,2:T(8,128)S(1)} %copy-done, f32[8,256,1024]{2,1,0:T(8,128)} %bitcast.18), kind=kOutput, calls=%fused_computation.55 | convolution fusion | flops 12884901888 | bytes 14680064 | tf_op jit(solution)/shard_map/dot_general | solution.py:81
  147.4 2.2 copy.10
  149.6 0.0 reduce-scatter.3.cloned.1.call-update
  149.6 0.0 reduce-scatter.5.cloned.1.call-start
  149.7 48.1 %reduce-scatter.3.cloned.1.call-done = f32[2,512,256]{2,1,0:T(8,128)} async-done(((f32[8,512,256]{2,1,0:T(8,128)}), f32[2,512,256]{2,1,0:T(8,128)}) %reduce-scatter.3.cloned.1.call-update) | async-done | bytes 1048592 | tf_op jit(solution)/shard_map/reduce_scatter | solution.py:37
  197.8 0.0 reduce-scatter.5.cloned.1.call-update
  197.8 0.3 fusion.1
  198.2 26.0 %reduce-scatter.5.cloned.1.call-done = f32[1,512,256]{2,1,0:T(8,128)} async-done(((f32[2,512,256]{2,1,0:T(8,128)}), f32[1,512,256]{2,1,0:T(8,128)}) %reduce-scatter.5.cloned.1.call-update) | async-done | bytes 524304 | tf_op jit(solution)/shard_map/reduce_scatter | solution.py:37
  224.2 2.3 convolution_multiply_fusion.1
  (11 shorter events, 0.1 us)
Async XLA Ops:
  6.5 115.4 %all-gather.2.cloned.1.call-start = ((), (), s32[]{:S(2)}) async-start(), calls=%async_computation.3 | async-start | bytes 12582912 | tf_op jit(solution)/shard_map/all_gather | solution.py:80
  12.7 0.7 copy-start.2
  12.7 1.0 copy-start.1
  12.8 185.0 %reduce-scatter.3.cloned.1.call-start = ((), (), s32[]{:S(2)}) async-start(), calls=%async_computation.4 | async-start | bytes 5242880 | tf_op jit(solution)/shard_map/reduce_scatter | solution.py:37
  121.9 9.4 %copy-start = (f32[512,1024,1]{1,0,2:T(8,128)S(1)}, f32[512,1024,1]{1,0,2:T(8,128)}, u32[]{:S(2)}) copy-start(f32[512,1024,1]{1,0,2:T(8,128)} %reshape.110) | copy-start | bytes 6291460
  149.6 48.2 %copy-start.3 = (s32[2,32]{1,0:T(2,128)S(1)}, s32[2,32]{1,0:T(2,128)}, u32[]{:S(2)}) copy-start(s32[2,32]{1,0:T(2,128)} %param.9) | copy-start | bytes 772
  149.6 74.6 %reduce-scatter.5.cloned.1.call-start = ((), (), s32[]{:S(2)}) async-start(), calls=%async_computation.5 | async-start | bytes 1572864 | tf_op jit(solution)/shard_map/reduce_scatter | solution.py:37
Sparse Core Ops, SparseCore 0:
  12.9 108.9 all-gather.1
  149.7 47.9 reduce-scatter.2
  200.2 23.9 reduce-scatter.4
where the time goes:
time: 234 us; the launch traced here: 233 us
  waiting for transfers between devices  147 us (63%)
  blocking collectives  31.7 us (14%)
  matrix products  25.5 us (11%)
  local copies, waits for them, and re-layouts  15.1 us (6%)
  between operations  13.2 us (6%)
    reduce_scatter x2, waiting for transfers between devices, sum_in_order(): tiles = lax.psum_scatter(tiles, axes[k], scatter_dimension=0, tiled=True)  74.2 us
    all_gather x1, waiting for transfers between devices, shards(): slab = lax.all_gather(right_used, 'row', axis=0, tiled=True)  73.2 us
    all_to_all x1, blocking collectives, copy_for_each(): lax.all_to_all(jnp.broadcast_to(value[None], (length, *value.shape)), axi...  31.7 us
    dot_general x1, matrix products, shards(): jnp.dot(gather_directly(left_used, 'col', 1), slab, precision=lax.Precisi...  16.1 us
    dot_general x1, local copies, waits for them, and re-layouts, shards(): jnp.dot(gather_directly(left_used, 'col', 1), slab, precision=lax.Precisi...  9.39 us
    dot_general x3, matrix products, expand(): return jnp.dot(inner, col_sel.T, precision=lax.Precision.HIGHEST)  7.77 us
  transfers between devices with their start and end apart: 3, of which 3 were waited for; matrix products, arithmetic and copies ran while one was open for 2% of the time, Pallas kernels for 0%

commit v1 on v0

v1 whole, which is shorter than its diff:
```python
import jax
import jax.numpy as jnp
from jax import lax
from jax.experimental import pallas as pl
from jax.experimental.pallas import tpu as pltpu
from jax.sharding import Mesh
from jax.sharding import PartitionSpec as P

TILE = 512
PART = 256
AXES = ("yl", "x", "c", "yh", "z")
SIZES = (2, 4, 2, 2, 4)
UP, DOWN = (1, 2), (0, 3)
OWN_ROW, OTHER_ROW = (0, 2), (1, 3)


def everyone():
    for yl in range(2):
        for x in range(4):
            for c in range(2):
                for yh in range(2):
                    for z in range(4):
                        yield yl, x, c, yh, z


def number(yl, x, c, yh, z):
    return (((yl * 4 + x) * 2 + c) * 2 + yh) * 4 + z


def permute(value, target):
    pairs = []
    for place in everyone():
        there = target(*place)
        if there is not None:
            pairs.append((number(*place), number(*there)))
    return lax.ppermute(value, AXES, pairs)


def along_y(value, step):
    def target(yl, x, c, yh, z):
        y = (2 * yh + yl + step) % 4
        return y % 2, x, c, y // 2, z

    return permute(value, target)


def along_z(value, step):
    return permute(value, lambda yl, x, c, yh, z: (yl, x, c, yh, (z + step) % 4))


def swap_cores(value):
    return permute(value, lambda yl, x, c, yh, z: (yl, x, 1 - c, yh, z))


def swap_rows(value):
    def target(yl, x, c, yh, z):
        return (1 - yl, x, c, yh, z) if x // 2 != yl else None

    return permute(value, target)


def spread(value, yl, x):
    def up(yl, x, c, yh, z):
        return (yl, (x + 1) % 4, c, yh, z) if x // 2 == yl else None

    def down(yl, x, c, yh, z):
        return (yl, (x - 1) % 4, c, yh, z) if x // 2 == yl else None

    def across(yl, x, c, yh, z):
        return (yl, (x + 2) % 4, c, yh, z) if x // 2 == yl else None

    from_below = permute(value, up)
    from_above = permute(value, down)
    from_across = permute(value, across)
    place = (x - 2 * yl) % 4
    low = jnp.where(
        place == 0, value, jnp.where(place == 1, from_below, jnp.where(place == 2, from_across, from_above))
    )
    high = jnp.where(
        place == 1, value, jnp.where(place == 0, from_above, jnp.where(place == 2, from_below, from_across))
    )
    return jnp.stack([low, high])


def product_kernel(turns, plan, spots, left_mask, right_mask, result_mask, mine, other, right, *rest):
    outs, (hi_ref, lo_ref) = rest[:-2], rest[-2:]
    yl, x, c, yh, z = (spots[n] for n in range(5))
    y = 2 * yh + yl
    k = (yh * 4 + z) * 2 + yl
    first = (x * 2 + c) * 4
    for s in range(2):
        for block, core in ((mine, c), (other, 1 - c)):
            piece = block[s]
            hi = piece.astype(jnp.bfloat16)
            where = pl.ds(pl.multiple_of(s * 256 + core * 128, 128), 128)
            hi_ref[:, where] = hi
            lo_ref[:, where] = (piece - hi.astype(jnp.float32)).astype(jnp.bfloat16)
    for dy in turns:
        there = lax.rem(y + dy, 4)
        i, half = lax.rem(there, 2), lax.div(there, 2)
        for dz in range(4):
            chunk = half * 4 + lax.rem(z + dz, 4)
            j = first + lax.div(chunk, 2)
            used = left_mask[i, k] * right_mask[k, j] * result_mask[i, j]
            (top, t), (bottom, b) = plan[dy, dz]

            @pl.when(used > 0)
            def _():
                tile = right[:, pl.ds(pl.multiple_of(chunk * 256, 256), 256)]
                hi = tile.astype(jnp.bfloat16)
                lo = (tile - hi.astype(jnp.float32)).astype(jnp.bfloat16)
                total = jnp.dot(hi_ref[...], hi, preferred_element_type=jnp.float32)
                total += jnp.dot(hi_ref[...], lo, preferred_element_type=jnp.float32)
                total += jnp.dot(lo_ref[...], hi, preferred_element_type=jnp.float32)
                outs[top][t] = total[:PART]
                outs[bottom][b] = total[PART:]

            @pl.when(used == 0)
            def _():
                outs[top][t] = jnp.zeros((PART, 256), jnp.float32)
                outs[bottom][b] = jnp.zeros((PART, 256), jnp.float32)


def product(turns, names, spots, masks, mine, right):
    plan = {}
    for dy in turns:
        for dz in range(4):
            slots = []
            for half in "AB":
                for n, blocks in enumerate(names.values()):
                    if (half, dy, dz) in blocks:
                        slots.append((n, blocks.index((half, dy, dz))))
            plan[dy, dz] = slots
    smem = pl.BlockSpec(memory_space=pltpu.SMEM)
    vmem = pl.BlockSpec(memory_space=pltpu.VMEM)
    outs = pl.pallas_call(
        lambda *refs: product_kernel(turns, plan, *refs),
        out_shape=[jax.ShapeDtypeStruct((len(b), PART, 256), jnp.float32) for b in names.values()],
        in_specs=[smem] * 4 + [vmem] * 3,
        out_specs=[vmem] * len(names),
        scratch_shapes=[pltpu.VMEM((TILE, TILE), jnp.bfloat16)] * 2,
        compiler_params=pltpu.CompilerParams(vmem_limit_bytes=32 * 2**20),
        cost_estimate=pl.CostEstimate(
            flops=3 * 2 * TILE * TILE * 2048, bytes_accessed=9 * 2**20, transcendentals=0
        ),
    )(spots, *masks, mine, swap_cores(mine), right)
    return dict(zip(names, outs))


def shards(left, right, left_mask, right_mask, result_mask):
    yl, x, c, yh, z = (lax.axis_index(a) for a in AXES)
    spots = jnp.stack([yl, x, c, yh, z]).astype(jnp.int32)
    masks = (left_mask, right_mask, result_mask)

    mine = spread(left, yl, x)
    theirs = spread(swap_rows(left), yl, x)
    p = product(
        OWN_ROW,
        {
            "a1_up": [("A", 2, d) for d in UP],
            "a1_down": [("A", 2, d) for d in DOWN],
            "b1_up": [("B", d, 2) for d in OWN_ROW],
            "b2_down": [("B", d, 3) for d in OWN_ROW],
            "b3_up": [("B", d, 1) for d in OWN_ROW],
            "a_up": [("A", 0, d) for d in UP],
            "a_down": [("A", 0, d) for d in DOWN],
            "b_own": [("B", d, 0) for d in OWN_ROW],
        },
        spots,
        masks,
        mine,
        right,
    )
    a1_up = along_y(p["a1_up"], 1)
    a1_down = along_y(p["a1_down"], -1)
    b1_up = along_z(p["b1_up"], 1)
    b2_down = along_z(p["b2_down"], -1)
    q = product(
        OTHER_ROW,
        {
            "a2_up": [("A", 1, d) for d in DOWN],
            "a2_down": [("A", 3, d) for d in UP],
            "b1_down": [("B", d, 2) for d in OTHER_ROW],
            "b2_up": [("B", d, 1) for d in OTHER_ROW],
            "a3_up": [("A", 1, d) for d in UP],
            "a3_down": [("A", 3, d) for d in DOWN],
            "b3_down": [("B", d, 3) for d in OTHER_ROW],
            "b_other": [("B", d, 0) for d in OTHER_ROW],
        },
        spots,
        masks,
        theirs,
        right,
    )
    b1_down = along_z(q["b1_down"], -1)
    a2_up = along_y(q["a2_up"], 1)
    a2_down = along_y(q["a2_down"], -1)
    b2_up = along_z(q["b2_up"], 1)
    a3_up = along_y(q["a3_up"] + a1_up, 1)
    a3_down = along_y(q["a3_down"] + a1_down, -1)
    b3_up = along_z(p["b3_up"] + b1_up, 1)
    b3_down = along_z(q["b3_down"] + b1_down, -1)
    a = dict(zip(UP, p["a_up"] + a2_down + a3_up)) | dict(zip(DOWN, p["a_down"] + a2_up + a3_down))
    b = dict(zip(OWN_ROW, p["b_own"] + b2_down + b3_up)) | dict(
        zip(OTHER_ROW, q["b_other"] + b2_up + b3_down)
    )
    top = a[0] + along_z(a[1], 1) + along_z(a[2], 2) + along_z(a[3], -1)
    bottom = b[0] + along_y(b[1], 1) + along_y(b[2], 2) + along_y(b[3], -1)
    return jnp.concatenate([top, bottom])


def solution(mesh):
    torus = Mesh(mesh.devices.reshape(SIZES), AXES)
    in_specs = (
        P("yl", ("yh", "z", "x", "c")),
        P(("yh", "z", "yl"), ("x", "c")),
        P(),
        P(),
        P(),
    )
    return jax.shard_map(
        shards, mesh=torus, in_specs=in_specs, out_specs=P("yl", ("x", "c", "yh", "z")), check_vma=False
    )
```

time: 234 us -> 112 us (0.48)
  waiting for transfers between devices: 147 us -> 52.7 us
  starting transfers between devices: 0.09 us -> 49.8 us
  blocking collectives: 31.7 us -> 0 us
  matrix products: 25.5 us -> 0 us
  between operations: 13.2 us -> 0.35 us
  local copies, waits for them, and re-layouts: 15.1 us -> 2.4 us
  Pallas kernels: 0 us -> 4.89 us
  other arithmetic: 0.05 us -> 2.78 us
    reduce_scatter x2 -> x0, waiting for transfers between devices: 74.2 us -> none  [sum_in_order(): tiles = lax.psum_scatter(tiles, axes[k], scatter_dimension=0, tiled=True)]
    all_gather x1 -> x0, waiting for transfers between devices: 73.2 us -> none  [shards(): slab = lax.all_gather(right_used, 'row', axis=0, tiled=True)]
    ppermute x0 -> x27, waiting for transfers between devices: none -> 52.7 us  [permute(): return lax.ppermute(value, AXES, pairs)]
    ppermute x0 -> x27, starting transfers between devices: none -> 49.8 us  [permute(): return lax.ppermute(value, AXES, pairs)]
    all_to_all x1 -> x0, blocking collectives: 31.7 us -> none  [copy_for_each(): lax.all_to_all(jnp.broadcast_to(value[None], (length, *value.shape)), axi...]
    dot_general x7 -> x0, matrix products: 25.5 us -> none  [the longest x1 16.1 us: shards(): jnp.dot(gather_directly(left_used, 'col', 1), slab, precision=lax.Precisi...]
    dot_general x1 -> x0, local copies, waits for them, and re-layouts: 9.39 us -> none  [shards(): jnp.dot(gather_directly(left_used, 'col', 1), slab, precision=lax.Precisi...]
    pallas_call x0 -> x2, Pallas kernels: none -> 4.89 us  [product(): pl.pallas_call(lambda *refs: product_kernel(turns, plan, *refs), out_shap...]
  transfers between devices with their start and end apart: 3 -> 27, of which waited for: 3 -> 11; matrix products, arithmetic and copies ran while one was open for 2% -> 2% of each run, Pallas kernels for 0% -> 4%
where the time goes in v1:
time: 112 us; the launch traced here: 113 us
  waiting for transfers between devices  52.7 us (47%)
  starting transfers between devices  49.8 us (44%)
  Pallas kernels  4.89 us (4%)
  other arithmetic  2.78 us (2%)
  local copies, waits for them, and re-layouts  2.4 us (2%)
    ppermute x27, waiting for transfers between devices, permute(): return lax.ppermute(value, AXES, pairs)  52.7 us
    ppermute x27, starting transfers between devices, permute(): return lax.ppermute(value, AXES, pairs)  49.8 us
    pallas_call x2, Pallas kernels, product(): pl.pallas_call(lambda *refs: product_kernel(turns, plan, *refs), out_shap...  4.89 us
  transfers between devices with their start and end apart: 27, of which 11 were waited for; matrix products, arithmetic and copies ran while one was open for 2% of the time, Pallas kernels for 4%

profile of v1, /device:TPU:0, one launch (start us, length us, event | category | flops | bytes accessed | tf_op | source)
XLA Modules:
  0.0 112.9 jit_solution(2879986511198852185)
XLA Ops:
  1.4 3.5 %collective-permute-start = (f32[512,128]{1,0:T(8,128)}, f32[512,128]{1,0:T(8,128)S(1)}, u32[]{:S(2)}, u32[]{:S(2)}) collective-permute-start(f32[512,128]{1,0:T(8,128)} %param.5), channel_id=1, source_target_pairs={{0,16},{1,17},{2,18},{3,19},{4,20},{5,21},{6,22},{7,23},{8,24},{9,... | collective-permute-start | bytes 786440 | tf_op jit(solution)/shard_map/ppermute | solution.py:36
  4.9 5.0 %collective-permute-start.1 = (f32[512,128]{1,0:T(8,128)}, f32[512,128]{1,0:T(8,128)S(1)}, u32[]{:S(2)}, u32[]{:S(2)}) collective-permute-start(f32[512,128]{1,0:T(8,128)} %param.5), channel_id=1, source_target_pairs={{0,32},{1,33},{2,34},{3,35},{4,36},{5,37},{6,38},{7,39},{8,40},{9,... | collective-permute-start | bytes 786440 | tf_op jit(solution)/shard_map/ppermute | solution.py:36
  10.0 1.9 %collective-permute-start.2 = (f32[512,128]{1,0:T(8,128)}, f32[512,128]{1,0:T(8,128)S(1)}, u32[]{:S(2)}, u32[]{:S(2)}) collective-permute-start(f32[512,128]{1,0:T(8,128)} %param.5), channel_id=1, source_target_pairs={{0,48},{1,49},{2,50},{3,51},{4,52},{5,53},{6,54},{7,55},{8,56},{9,... | collective-permute-start | bytes 786440 | tf_op jit(solution)/shard_map/ppermute | solution.py:36
  11.9 3.9 %collective-permute-start.5 = (f32[512,128]{1,0:T(8,128)S(1)}, f32[512,128]{1,0:T(8,128)S(1)}, u32[]{:S(2)}, u32[]{:S(2)}) collective-permute-start(f32[512,128]{1,0:T(8,128)S(1)} %collective-permute-done.4), channel_id=1, source_target_pairs={{0,16},{1,17},{2,18},{3,19},{4,20},{5,21},{6,22},{7,23},{8,24},{9,... | collective-permute-start | bytes 786440 | tf_op jit(solution)/shard_map/ppermute | solution.py:36
  17.2 1.9 %collective-permute-start.7 = (f32[512,128]{1,0:T(8,128)S(1)}, f32[512,128]{1,0:T(8,128)S(1)}, u32[]{:S(2)}, u32[]{:S(2)}) collective-permute-start(f32[512,128]{1,0:T(8,128)S(1)} %collective-permute-done.4), channel_id=1, source_target_pairs={{0,48},{1,49},{2,50},{3,51},{4,52},{5,53},{6,54},{7,55},{8,56},{9,... | collective-permute-start | bytes 786440 | tf_op jit(solution)/shard_map/ppermute | solution.py:36
  19.2 3.8 %collective-permute-done.2 = f32[512,128]{1,0:T(8,128)S(1)} collective-permute-done((f32[512,128]{1,0:T(8,128)}, f32[512,128]{1,0:T(8,128)S(1)}, u32[]{:S(2)}, u32[]{:S(2)}) %collective-permute-start.2) | collective-permute-done | bytes 262176 | tf_op jit(solution)/shard_map/ppermute | solution.py:36
  24.1 3.5 %collective-permute-done.6 = f32[512,128]{1,0:T(8,128)S(1)} collective-permute-done((f32[512,128]{1,0:T(8,128)S(1)}, f32[512,128]{1,0:T(8,128)S(1)}, u32[]{:S(2)}, u32[]{:S(2)}) %collective-permute-start.6) | collective-permute-done | bytes 262176 | tf_op jit(solution)/shard_map/ppermute | solution.py:36
  27.6 5.2 %collective-permute-done.7 = f32[512,128]{1,0:T(8,128)S(1)} collective-permute-done((f32[512,128]{1,0:T(8,128)S(1)}, f32[512,128]{1,0:T(8,128)S(1)}, u32[]{:S(2)}, u32[]{:S(2)}) %collective-permute-start.7) | collective-permute-done | bytes 262176 | tf_op jit(solution)/shard_map/ppermute | solution.py:36
  33.1 2.2 %copy-done = f32[512,2048]{1,0:T(8,128)S(1)} copy-done((f32[512,2048]{1,0:T(8,128)S(1)}, f32[512,2048]{1,0:T(8,128)}, u32[]{:S(2)}) %copy-start) | copy-done | bytes 4194328
  35.3 2.4 %shard_map.55 = (f32[2,256,256]{2,1,0:T(8,128)S(1)}, f32[2,256,256]{2,1,0:T(8,128)S(1)}, f32[2,256,256]{2,1,0:T(8,128)S(1)}, f32[2,256,256]{2,1,0:T(8,128)S(1)},...) custom-call(s32[5]{0:T(128)S(1)} %stack.41.refs_0_, ...), custom_call_target="tpu_custom_call" | custom-call | flops 3221225472 | bytes 9437184 | tf_op jit(solution)/shard_map/pallas_call | solution.py:136
  38.6 2.2 %collective-permute-start.10 = (f32[2,256,256]{2,1,0:T(8,128)S(1)}, f32[2,256,256]{2,1,0:T(8,128)S(1)}, u32[]{:S(2)}, u32[]{:S(2)}) collective-permute-start(f32[2,256,256]{2,1,0:T(8,128)S(1)} %get-tuple-element.24), channel_id=1, source_target_pairs={{0,68},{1,69},{2,70},{3,71},{4,64},{5,65},{6,66},{7,67},{8,76},{9,... | collective-permute-start | bytes 1572872 | tf_op jit(solution)/shard_map/ppermute | solution.py:36
  40.8 2.4 %shard_map.56 = (f32[2,256,256]{2,1,0:T(8,128)S(1)}, f32[2,256,256]{2,1,0:T(8,128)S(1)}, f32[2,256,256]{2,1,0:T(8,128)S(1)}, f32[2,256,256]{2,1,0:T(8,128)S(1)},...) custom-call(s32[5]{0:T(128)S(1)} %stack.41.refs_0_, ...), custom_call_target="tpu_custom_call" | custom-call | flops 3221225472 | bytes 9437184 | tf_op jit(solution)/shard_map/pallas_call | solution.py:136
  44.5 5.7 %collective-permute-start.18 = (f32[2,256,256]{2,1,0:T(8,128)S(1)}, f32[2,256,256]{2,1,0:T(8,128)S(1)}, u32[]{:S(2)}, u32[]{:S(2)}) collective-permute-start(f32[2,256,256]{2,1,0:T(8,128)S(1)} %get-tuple-element.30), channel_id=1, source_target_pairs={{0,3},{1,0},{2,1},{3,2},{4,7},{5,4},{6,5},{7,6},{8,11},{9,8},{10,9... | collective-permute-start | bytes 1572872 | tf_op jit(solution)/shard_map/ppermute | solution.py:36
  50.2 3.1 %collective-permute-done.19 = f32[2,256,256]{2,1,0:T(8,128)S(1)} collective-permute-done((f32[2,256,256]{2,1,0:T(8,128)S(1)}, f32[2,256,256]{2,1,0:T(8,128)S(1)}, u32[]{:S(2)}, u32[]{:S(2)}) %collective-permute-start.19) | collective-permute-done | bytes 524320 | tf_op jit(solution)/shard_map/ppermute | solution.py:36
  57.2 2.6 %collective-permute-done.22 = f32[2,256,256]{2,1,0:T(8,128)S(1)} collective-permute-done((f32[2,256,256]{2,1,0:T(8,128)S(1)}, f32[2,256,256]{2,1,0:T(8,128)S(1)}, u32[]{:S(2)}, u32[]{:S(2)}) %collective-permute-start.22) | collective-permute-done | bytes 524320 | tf_op jit(solution)/shard_map/ppermute | solution.py:36
  59.8 2.7 %collective-permute-start.21 = (f32[2,256,256]{2,1,0:T(8,128)S(1)}, f32[2,256,256]{2,1,0:T(8,128)S(1)}, u32[]{:S(2)}, u32[]{:S(2)}) collective-permute-start(f32[2,256,256]{2,1,0:T(8,128)S(1)} %get-tuple-element.34), channel_id=1, source_target_pairs={{0,1},{1,2},{2,3},{3,0},{4,5},{5,6},{6,7},{7,4},{8,9},{9,10},{10,1... | collective-permute-start | bytes 1572872 | tf_op jit(solution)/shard_map/ppermute | solution.py:36
  62.5 8.5 %collective-permute-done.18 = f32[2,256,256]{2,1,0:T(8,128)S(1)} collective-permute-done((f32[2,256,256]{2,1,0:T(8,128)S(1)}, f32[2,256,256]{2,1,0:T(8,128)S(1)}, u32[]{:S(2)}, u32[]{:S(2)}) %collective-permute-start.18) | collective-permute-done | bytes 524320 | tf_op jit(solution)/shard_map/ppermute | solution.py:36
  73.3 3.4 %collective-permute-start.25 = (f32[256,256]{1,0:T(8,128)S(1)}, f32[256,256]{1,0:T(8,128)S(1)}, u32[]{:S(2)}, u32[]{:S(2)}) collective-permute-start(f32[256,256]{1,0:T(8,128)S(1)} %slice_bitcast_fusion.1), channel_id=1, source_target_pairs={{0,4},{1,5},{2,6},{3,7},{4,0},{5,1},{6,2},{7,3},{8,12},{9,13},{10,... | collective-permute-start | bytes 786440 | tf_op jit(solution)/shard_map/ppermute | solution.py:36
  76.9 8.9 %collective-permute-done.12 = f32[2,256,256]{2,1,0:T(8,128)S(1)} collective-permute-done((f32[2,256,256]{2,1,0:T(8,128)S(1)}, f32[2,256,256]{2,1,0:T(8,128)S(1)}, u32[]{:S(2)}, u32[]{:S(2)}) %collective-permute-start.12) | collective-permute-done | bytes 524320 | tf_op jit(solution)/shard_map/ppermute | solution.py:36
  85.7 5.0 %collective-permute-start.17 = (f32[256,256]{1,0:T(8,128)S(1)}, f32[256,256]{1,0:T(8,128)S(1)}, u32[]{:S(2)}, u32[]{:S(2)}) collective-permute-start(f32[256,256]{1,0:T(8,128)S(1)} %slice_bitcast_fusion.4), channel_id=1, source_target_pairs={{0,3},{1,0},{2,1},{3,2},{4,7},{5,4},{6,5},{7,6},{8,11},{9,8},{10,9... | collective-permute-start | bytes 786440 | tf_op jit(solution)/shard_map/ppermute | solution.py:36
  91.0 4.6 %collective-permute-start.15 = (f32[256,256]{1,0:T(8,128)S(1)}, f32[256,256]{1,0:T(8,128)S(1)}, u32[]{:S(2)}, u32[]{:S(2)}) collective-permute-start(f32[256,256]{1,0:T(8,128)S(1)} %get-tuple-element.41), channel_id=1, source_target_pairs={{0,1},{1,2},{2,3},{3,0},{4,5},{5,6},{6,7},{7,4},{8,9},{9,10},{10,1... | collective-permute-start | bytes 786440 | tf_op jit(solution)/shard_map/ppermute | solution.py:36
  95.9 6.6 %collective-permute-done.17 = f32[256,256]{1,0:T(8,128)S(1)} collective-permute-done((f32[256,256]{1,0:T(8,128)S(1)}, f32[256,256]{1,0:T(8,128)S(1)}, u32[]{:S(2)}, u32[]{:S(2)}) %collective-permute-start.17) | collective-permute-done | bytes 262176 | tf_op jit(solution)/shard_map/ppermute | solution.py:36
  102.5 3.9 %collective-permute-done.15 = f32[256,256]{1,0:T(8,128)S(1)} collective-permute-done((f32[256,256]{1,0:T(8,128)S(1)}, f32[256,256]{1,0:T(8,128)S(1)}, u32[]{:S(2)}, u32[]{:S(2)}) %collective-permute-start.15) | collective-permute-done | bytes 262176 | tf_op jit(solution)/shard_map/ppermute | solution.py:36
  106.5 5.5 %collective-permute-done.24 = f32[256,256]{1,0:T(8,128)S(1)} collective-permute-done((f32[256,256]{1,0:T(8,128)S(1)}, f32[256,256]{1,0:T(8,128)S(1)}, u32[]{:S(2)}, u32[]{:S(2)}) %collective-permute-start.24) | collective-permute-done | bytes 262176 | tf_op jit(solution)/shard_map/ppermute | solution.py:36
  (62 shorter events, 14.0 us)
Async XLA Ops:
  0.0 11.9 %collective-permute-start.4 = (f32[512,128]{1,0:T(8,128)}, f32[512,128]{1,0:T(8,128)S(1)}, u32[]{:S(2)}, u32[]{:S(2)}) collective-permute-start(f32[512,128]{1,0:T(8,128)} %param.5), channel_id=1, source_target_pairs={{32,96},{33,97},{34,98},{35,99},{36,100},{37,101},{38,102},{39,103... | collective-permute-start | bytes 786440 | tf_op jit(solution)/shard_map/ppermute | solution.py:36
  1.4 15.8 %collective-permute-start = (f32[512,128]{1,0:T(8,128)}, f32[512,128]{1,0:T(8,128)S(1)}, u32[]{:S(2)}, u32[]{:S(2)}) collective-permute-start(f32[512,128]{1,0:T(8,128)} %param.5), channel_id=1, source_target_pairs={{0,16},{1,17},{2,18},{3,19},{4,20},{5,21},{6,22},{7,23},{8,24},{9,... | collective-permute-start | bytes 786440 | tf_op jit(solution)/shard_map/ppermute | solution.py:36
  4.9 14.2 %collective-permute-start.1 = (f32[512,128]{1,0:T(8,128)}, f32[512,128]{1,0:T(8,128)S(1)}, u32[]{:S(2)}, u32[]{:S(2)}) collective-permute-start(f32[512,128]{1,0:T(8,128)} %param.5), channel_id=1, source_target_pairs={{0,32},{1,33},{2,34},{3,35},{4,36},{5,37},{6,38},{7,39},{8,40},{9,... | collective-permute-start | bytes 786440 | tf_op jit(solution)/shard_map/ppermute | solution.py:36
  10.0 13.0 %collective-permute-start.2 = (f32[512,128]{1,0:T(8,128)}, f32[512,128]{1,0:T(8,128)S(1)}, u32[]{:S(2)}, u32[]{:S(2)}) collective-permute-start(f32[512,128]{1,0:T(8,128)} %param.5), channel_id=1, source_target_pairs={{0,48},{1,49},{2,50},{3,51},{4,52},{5,53},{6,54},{7,55},{8,56},{9,... | collective-permute-start | bytes 786440 | tf_op jit(solution)/shard_map/ppermute | solution.py:36
  11.9 12.2 %collective-permute-start.5 = (f32[512,128]{1,0:T(8,128)S(1)}, f32[512,128]{1,0:T(8,128)S(1)}, u32[]{:S(2)}, u32[]{:S(2)}) collective-permute-start(f32[512,128]{1,0:T(8,128)S(1)} %collective-permute-done.4), channel_id=1, source_target_pairs={{0,16},{1,17},{2,18},{3,19},{4,20},{5,21},{6,22},{7,23},{8,24},{9,... | collective-permute-start | bytes 786440 | tf_op jit(solution)/shard_map/ppermute | solution.py:36
  15.9 11.7 %collective-permute-start.6 = (f32[512,128]{1,0:T(8,128)S(1)}, f32[512,128]{1,0:T(8,128)S(1)}, u32[]{:S(2)}, u32[]{:S(2)}) collective-permute-start(f32[512,128]{1,0:T(8,128)S(1)} %collective-permute-done.4), channel_id=1, source_target_pairs={{0,32},{1,33},{2,34},{3,35},{4,36},{5,37},{6,38},{7,39},{8,40},{9,... | collective-permute-start | bytes 786440 | tf_op jit(solution)/shard_map/ppermute | solution.py:36
  17.2 15.6 %collective-permute-start.7 = (f32[512,128]{1,0:T(8,128)S(1)}, f32[512,128]{1,0:T(8,128)S(1)}, u32[]{:S(2)}, u32[]{:S(2)}) collective-permute-start(f32[512,128]{1,0:T(8,128)S(1)} %collective-permute-done.4), channel_id=1, source_target_pairs={{0,48},{1,49},{2,50},{3,51},{4,52},{5,53},{6,54},{7,55},{8,56},{9,... | collective-permute-start | bytes 786440 | tf_op jit(solution)/shard_map/ppermute | solution.py:36
  37.7 15.6 %collective-permute-start.19 = (f32[2,256,256]{2,1,0:T(8,128)S(1)}, f32[2,256,256]{2,1,0:T(8,128)S(1)}, u32[]{:S(2)}, u32[]{:S(2)}) collective-permute-start(f32[2,256,256]{2,1,0:T(8,128)S(1)} %get-tuple-element.32), channel_id=1, source_target_pairs={{0,1},{1,2},{2,3},{3,0},{4,5},{5,6},{6,7},{7,4},{8,9},{9,10},{10,1... | collective-permute-start | bytes 1572872 | tf_op jit(solution)/shard_map/ppermute | solution.py:36
  38.6 15.0 %collective-permute-start.10 = (f32[2,256,256]{2,1,0:T(8,128)S(1)}, f32[2,256,256]{2,1,0:T(8,128)S(1)}, u32[]{:S(2)}, u32[]{:S(2)}) collective-permute-start(f32[2,256,256]{2,1,0:T(8,128)S(1)} %get-tuple-element.24), channel_id=1, source_target_pairs={{0,68},{1,69},{2,70},{3,71},{4,64},{5,65},{6,66},{7,67},{8,76},{9,... | collective-permute-start | bytes 1572872 | tf_op jit(solution)/shard_map/ppermute | solution.py:36
  40.8 14.8 %collective-permute-start.13 = (f32[2,256,256]{2,1,0:T(8,128)S(1)}, f32[2,256,256]{2,1,0:T(8,128)S(1)}, u32[]{:S(2)}, u32[]{:S(2)}) collective-permute-start(f32[2,256,256]{2,1,0:T(8,128)S(1)} %get-tuple-element.28), channel_id=1, source_target_pairs={{0,64},{1,65},{2,66},{3,67},{4,68},{5,69},{6,70},{7,71},{8,72},{9,... | collective-permute-start | bytes 1572872 | tf_op jit(solution)/shard_map/ppermute | solution.py:36
  43.3 16.5 %collective-permute-start.22 = (f32[2,256,256]{2,1,0:T(8,128)S(1)}, f32[2,256,256]{2,1,0:T(8,128)S(1)}, u32[]{:S(2)}, u32[]{:S(2)}) collective-permute-start(f32[2,256,256]{2,1,0:T(8,128)S(1)} %get-tuple-element.36), channel_id=1, source_target_pairs={{0,3},{1,0},{2,1},{3,2},{4,7},{5,4},{6,5},{7,6},{8,11},{9,8},{10,9... | collective-permute-start | bytes 1572872 | tf_op jit(solution)/shard_map/ppermute | solution.py:36
  44.5 26.5 %collective-permute-start.18 = (f32[2,256,256]{2,1,0:T(8,128)S(1)}, f32[2,256,256]{2,1,0:T(8,128)S(1)}, u32[]{:S(2)}, u32[]{:S(2)}) collective-permute-start(f32[2,256,256]{2,1,0:T(8,128)S(1)} %get-tuple-element.30), channel_id=1, source_target_pairs={{0,3},{1,0},{2,1},{3,2},{4,7},{5,4},{6,5},{7,6},{8,11},{9,8},{10,9... | collective-permute-start | bytes 1572872 | tf_op jit(solution)/shard_map/ppermute | solution.py:36
  53.4 19.0 %collective-permute-start.20 = (f32[2,256,256]{2,1,0:T(8,128)S(1)}, f32[2,256,256]{2,1,0:T(8,128)S(1)}, u32[]{:S(2)}, u32[]{:S(2)}) collective-permute-start(f32[2,256,256]{2,1,0:T(8,128)S(1)} %add.70), channel_id=1, source_target_pairs={{0,1},{1,2},{2,3},{3,0},{4,5},{5,6},{6,7},{7,4},{8,9},{9,10},{10,1... | collective-permute-start | bytes 1572872 | tf_op jit(solution)/shard_map/ppermute | solution.py:36
  53.7 19.5 %collective-permute-start.9 = (f32[2,256,256]{2,1,0:T(8,128)S(1)}, f32[2,256,256]{2,1,0:T(8,128)S(1)}, u32[]{:S(2)}, u32[]{:S(2)}) collective-permute-start(f32[2,256,256]{2,1,0:T(8,128)S(1)} %get-tuple-element.22), channel_id=1, source_target_pairs={{0,64},{1,65},{2,66},{3,67},{4,68},{5,69},{6,70},{7,71},{8,72},{9,... | collective-permute-start | bytes 1572872 | tf_op jit(solution)/shard_map/ppermute | solution.py:36
  55.6 17.7 %collective-permute-start.11 = (f32[2,256,256]{2,1,0:T(8,128)S(1)}, f32[2,256,256]{2,1,0:T(8,128)S(1)}, u32[]{:S(2)}, u32[]{:S(2)}) collective-permute-start(f32[2,256,256]{2,1,0:T(8,128)S(1)} %add.61), channel_id=1, source_target_pairs={{0,68},{1,69},{2,70},{3,71},{4,64},{5,65},{6,66},{7,67},{8,76},{9,... | collective-permute-start | bytes 1572872 | tf_op jit(solution)/shard_map/ppermute | solution.py:36
  59.8 31.3 %collective-permute-start.21 = (f32[2,256,256]{2,1,0:T(8,128)S(1)}, f32[2,256,256]{2,1,0:T(8,128)S(1)}, u32[]{:S(2)}, u32[]{:S(2)}) collective-permute-start(f32[2,256,256]{2,1,0:T(8,128)S(1)} %get-tuple-element.34), channel_id=1, source_target_pairs={{0,1},{1,2},{2,3},{3,0},{4,5},{5,6},{6,7},{7,4},{8,9},{9,10},{10,1... | collective-permute-start | bytes 1572872 | tf_op jit(solution)/shard_map/ppermute | solution.py:36
  71.0 14.7 %collective-permute-start.12 = (f32[2,256,256]{2,1,0:T(8,128)S(1)}, f32[2,256,256]{2,1,0:T(8,128)S(1)}, u32[]{:S(2)}, u32[]{:S(2)}) collective-permute-start(f32[2,256,256]{2,1,0:T(8,128)S(1)} %get-tuple-element.26), channel_id=1, source_target_pairs={{0,68},{1,69},{2,70},{3,71},{4,64},{5,65},{6,66},{7,67},{8,76},{9,... | collective-permute-start | bytes 1572872 | tf_op jit(solution)/shard_map/ppermute | solution.py:36
  72.4 18.4 %collective-permute-start.14 = (f32[2,256,256]{2,1,0:T(8,128)S(1)}, f32[2,256,256]{2,1,0:T(8,128)S(1)}, u32[]{:S(2)}, u32[]{:S(2)}) collective-permute-start(f32[2,256,256]{2,1,0:T(8,128)S(1)} %add.64), channel_id=1, source_target_pairs={{0,64},{1,65},{2,66},{3,67},{4,68},{5,69},{6,70},{7,71},{8,72},{9,... | collective-permute-start | bytes 1572872 | tf_op jit(solution)/shard_map/ppermute | solution.py:36
  73.2 22.4 %collective-permute-start.23 = (f32[2,256,256]{2,1,0:T(8,128)S(1)}, f32[2,256,256]{2,1,0:T(8,128)S(1)}, u32[]{:S(2)}, u32[]{:S(2)}) collective-permute-start(f32[2,256,256]{2,1,0:T(8,128)S(1)} %add.73), channel_id=1, source_target_pairs={{0,3},{1,0},{2,1},{3,2},{4,7},{5,4},{6,5},{7,6},{8,11},{9,8},{10,9... | collective-permute-start | bytes 1572872 | tf_op jit(solution)/shard_map/ppermute | solution.py:36
  73.3 33.2 %collective-permute-start.25 = (f32[256,256]{1,0:T(8,128)S(1)}, f32[256,256]{1,0:T(8,128)S(1)}, u32[]{:S(2)}, u32[]{:S(2)}) collective-permute-start(f32[256,256]{1,0:T(8,128)S(1)} %slice_bitcast_fusion.1), channel_id=1, source_target_pairs={{0,4},{1,5},{2,6},{3,7},{4,0},{5,1},{6,2},{7,3},{8,12},{9,13},{10,... | collective-permute-start | bytes 786440 | tf_op jit(solution)/shard_map/ppermute | solution.py:36
  85.7 16.8 %collective-permute-start.17 = (f32[256,256]{1,0:T(8,128)S(1)}, f32[256,256]{1,0:T(8,128)S(1)}, u32[]{:S(2)}, u32[]{:S(2)}) collective-permute-start(f32[256,256]{1,0:T(8,128)S(1)} %slice_bitcast_fusion.4), channel_id=1, source_target_pairs={{0,3},{1,0},{2,1},{3,2},{4,7},{5,4},{6,5},{7,6},{8,11},{9,8},{10,9... | collective-permute-start | bytes 786440 | tf_op jit(solution)/shard_map/ppermute | solution.py:36
  90.9 11.6 %collective-permute-start.16 = (f32[256,256]{1,0:T(8,128)S(1)}, f32[256,256]{1,0:T(8,128)S(1)}, u32[]{:S(2)}, u32[]{:S(2)}) collective-permute-start(f32[256,256]{1,0:T(8,128)S(1)} %get-tuple-element.42), channel_id=1, source_target_pairs={{0,2},{1,3},{2,0},{3,1},{4,6},{5,7},{6,4},{7,5},{8,10},{9,11},{10,... | collective-permute-start | bytes 786440 | tf_op jit(solution)/shard_map/ppermute | solution.py:36
  91.0 15.4 %collective-permute-start.15 = (f32[256,256]{1,0:T(8,128)S(1)}, f32[256,256]{1,0:T(8,128)S(1)}, u32[]{:S(2)}, u32[]{:S(2)}) collective-permute-start(f32[256,256]{1,0:T(8,128)S(1)} %get-tuple-element.41), channel_id=1, source_target_pairs={{0,1},{1,2},{2,3},{3,0},{4,5},{5,6},{6,7},{7,4},{8,9},{9,10},{10,1... | collective-permute-start | bytes 786440 | tf_op jit(solution)/shard_map/ppermute | solution.py:36
  95.7 10.8 %collective-permute-start.26 = (f32[256,256]{1,0:T(8,128)S(1)}, f32[256,256]{1,0:T(8,128)S(1)}, u32[]{:S(2)}, u32[]{:S(2)}) collective-permute-start(f32[256,256]{1,0:T(8,128)S(1)} %get-tuple-element.44), channel_id=1, source_target_pairs={{0,68},{1,69},{2,70},{3,71},{4,64},{5,65},{6,66},{7,67},{8,76},{9,... | collective-permute-start | bytes 786440 | tf_op jit(solution)/shard_map/ppermute | solution.py:36
  (8 other events, 133.4 us)

commit v2 on v0

v2 whole, which is shorter than its diff:
```python
import jax
import jax.numpy as jnp
from jax import lax
from jax.experimental import pallas as pl
from jax.experimental.pallas import tpu as pltpu
from jax.sharding import Mesh
from jax.sharding import PartitionSpec as P

TILE = 512
WIDTH = 256
AXES = ("yl", "x", "c", "yh", "z")
SIZES = (2, 4, 2, 2, 4)
ROWS = {"A": 320, "B": 192}
SMEM = pl.BlockSpec(memory_space=pltpu.SMEM)
VMEM = pl.BlockSpec(memory_space=pltpu.VMEM)


def permute(value, yl=0, x=0, c=0, yh=0, z=0, senders=lambda yl, x: True):
    pairs = []
    for a in range(2):
        for b in range(4):
            if senders(a, b):
                for d in range(2):
                    for e in range(2):
                        for f in range(4):
                            pairs.append((number(a, b, d, e, f), number(a ^ yl, b ^ x, d ^ c, e ^ yh, f ^ z)))
    return lax.ppermute(value, AXES, pairs)


def number(yl, x, c, yh, z):
    return (((yl * 4 + x) * 2 + c) * 2 + yh) * 4 + z


def along_y(value, bits):
    return permute(value, yl=bits % 2, yh=bits // 2)


def along_z(value, bits):
    return permute(value, z=bits)


def source(yl, x):
    return x // 2 == yl


def split_kernel(right, hi_ref, lo_ref):
    @pl.loop(0, 2048, step=WIDTH)
    def _(start):
        where = pl.ds(pl.multiple_of(start, WIDTH), WIDTH)
        tile = right[:, where]
        hi = tile.astype(jnp.bfloat16)
        hi_ref[:, where] = hi
        lo_ref[:, where] = (tile - hi.astype(jnp.float32)).astype(jnp.bfloat16)


def split(right):
    return pl.pallas_call(
        split_kernel,
        out_shape=[jax.ShapeDtypeStruct(right.shape, jnp.bfloat16)] * 2,
        in_specs=[VMEM],
        out_specs=[VMEM] * 2,
        compiler_params=pltpu.CompilerParams(vmem_limit_bytes=32 * 2**20),
        cost_estimate=pl.CostEstimate(flops=3 * right.size, bytes_accessed=8 * right.size, transcendentals=0),
    )(right)


def product_kernel(rows, plan, spots, left_mask, right_mask, result_mask, *rest):
    pieces, (right_hi, right_lo), outs, (hi_ref, lo_ref) = rest[:4], rest[4:6], rest[6:-2], rest[-2:]
    yl, x, c, yh, z = (spots[n] for n in range(5))
    k = (yh * 4 + z) * 2 + yl
    first = (x * 2 + c) * 4
    near = 1 - lax.rem(x, 2)
    for piece, chip, core in zip(pieces, (near, 1 - near, near, 1 - near), (c, c, 1 - c, 1 - c)):
        value = piece[...]
        hi = value.astype(jnp.bfloat16)
        where = pl.ds(pl.multiple_of(chip * 256 + core * 128, 128), 128)
        hi_ref[:, where] = hi
        lo_ref[:, where] = (value - hi.astype(jnp.float32)).astype(jnp.bfloat16)
    for dy, (start, stop) in rows.items():
        i = lax.rem(yl + dy % 2, 2)
        half = lax.rem(yh + dy // 2, 2)
        for dz in range(4):
            chunk = half * 4 + jnp.bitwise_xor(z, dz)
            j = first + lax.div(chunk, 2)
            used = left_mask[i, k] * right_mask[k, j] * result_mask[i, j]

            @pl.when(used > 0)
            def _():
                where = pl.ds(pl.multiple_of(chunk * WIDTH, WIDTH), WIDTH)
                hi, lo = right_hi[:, where], right_lo[:, where]
                total = jnp.dot(hi_ref[start:stop], hi, preferred_element_type=jnp.float32)
                total += jnp.dot(hi_ref[start:stop], lo, preferred_element_type=jnp.float32)
                total += jnp.dot(lo_ref[start:stop], hi, preferred_element_type=jnp.float32)
                done = 0
                for half, n, slot in plan[dy, dz]:
                    outs[n][slot] = total[done : done + ROWS[half]]
                    done += ROWS[half]

            @pl.when(used == 0)
            def _():
                for half, n, slot in plan[dy, dz]:
                    outs[n][slot] = jnp.zeros((ROWS[half], WIDTH), jnp.float32)


def product(rows, names, spots, masks, pieces, right):
    plan = {
        (dy, dz): [
            (half, n, blocks.index((half, dy, dz)))
            for half in "AB"
            for n, blocks in enumerate(names.values())
            if (half, dy, dz) in blocks
        ]
        for dy in rows
        for dz in range(4)
    }
    work = 3 * 2 * TILE * WIDTH * 4 * sum(stop - start for start, stop in rows.values())
    outs = pl.pallas_call(
        lambda *refs: product_kernel(rows, plan, *refs),
        out_shape=[jax.ShapeDtypeStruct((len(b), ROWS[b[0][0]], WIDTH), jnp.float32) for b in names.values()],
        in_specs=[SMEM] * 4 + [VMEM] * 6,
        out_specs=[VMEM] * len(names),
        scratch_shapes=[pltpu.VMEM((pieces[0].shape[0], TILE), jnp.bfloat16)] * 2,
        compiler_params=pltpu.CompilerParams(vmem_limit_bytes=32 * 2**20),
        cost_estimate=pl.CostEstimate(flops=work, bytes_accessed=4 * 2**20, transcendentals=0),
    )(spots, *masks, *pieces, *right)
    return dict(zip(names, outs))


def join(value, first, arrived):
    def kernel(value_ref, arrived_ref, out_ref):
        del value_ref
        for n in range(arrived.shape[0]):
            out_ref[first + n] += arrived_ref[n]

    return pl.pallas_call(
        kernel,
        out_shape=jax.ShapeDtypeStruct(value.shape, value.dtype),
        in_specs=[VMEM] * 2,
        out_specs=VMEM,
        input_output_aliases={0: 0},
        compiler_params=pltpu.CompilerParams(vmem_limit_bytes=32 * 2**20),
        cost_estimate=pl.CostEstimate(flops=arrived.size, bytes_accessed=12 * arrived.size, transcendentals=0),
    )(value, arrived)


def gather(value, here):
    between, beside, across = (permute(value, x=bits, senders=source) for bits in (1, 3, 2))
    near = jnp.where(here, between, beside)
    far = jnp.where(here, value, across)
    return near, far


def both_cores(near, far):
    return near, far, permute(near, c=1), permute(far, c=1)


def shards(left, right, left_mask, right_mask, result_mask):
    yl, x, c, yh, z = (lax.axis_index(a) for a in AXES)
    spots = jnp.stack([yl, x, c, yh, z]).astype(jnp.int32)
    masks = (left_mask, right_mask, result_mask)
    here = source(yl, x)
    rows_a = ROWS["A"]

    own = gather(left[:rows_a], here)
    other_row = permute(left, yl=1, senders=lambda yl, x: not source(yl, x))
    rest = gather(jnp.concatenate([left[rows_a:], other_row]), here)
    right = split(right)
    p = product(
        {0: (0, rows_a), 2: (0, rows_a)},
        {
            "via1": [("A", 2, 0), ("A", 2, 1)],
            "via3": [("A", 2, 2), ("A", 2, 3)],
            "own": [("A", 0, d) for d in range(4)],
        },
        spots,
        masks,
        both_cores(*own),
        right,
    )
    from1 = along_y(p["via1"], 1)
    from3 = along_y(p["via3"], 3)
    rest, a_own = lax.optimization_barrier((rest, p["own"]))
    own_rows, other_rows = (0, ROWS["B"]), (ROWS["B"], ROWS["B"] + TILE)
    q = product(
        {1: other_rows, 3: other_rows, 0: own_rows, 2: own_rows},
        {
            "a1": [("A", 1, d) for d in range(4)],
            "a3": [("A", 3, d) for d in range(4)],
            "via1": [("B", 0, 2), ("B", 1, 2)],
            "via3": [("B", 2, 2), ("B", 3, 2)],
            "b1": [("B", d, 1) for d in range(4)],
            "b3": [("B", d, 3) for d in range(4)],
            "own": [("B", d, 0) for d in range(4)],
        },
        spots,
        masks,
        both_cores(*rest),
        right,
    )
    top_parts = (along_y(join(q["a1"], 2, from3), 1), along_y(join(q["a3"], 0, from1), 3))
    from1 = along_z(q["via1"], 1)
    from3 = along_z(q["via3"], 3)
    bottom_parts = (along_z(join(q["b1"], 2, from3), 1), along_z(join(q["b3"], 0, from1), 3))

    a = [a_own[d] + top_parts[0][d] + top_parts[1][d] for d in range(4)]
    b = [q["own"][d] + bottom_parts[0][d] + bottom_parts[1][d] for d in range(4)]
    top = a[0] + along_z(a[2], 2) + along_z(a[1], 1) + along_z(a[3], 3)
    bottom = b[0] + along_y(b[2], 2) + along_y(b[1], 1) + along_y(b[3], 3)
    return jnp.concatenate([top, bottom])


def solution(mesh):
    torus = Mesh(mesh.devices.reshape(SIZES), AXES)
    in_specs = (
        P("yl", ("yh", "z", "x", "c")),
        P(("yh", "z", "yl"), ("x", "c")),
        P(),
        P(),
        P(),
    )
    return jax.shard_map(
        shards, mesh=torus, in_specs=in_specs, out_specs=P("yl", ("x", "c", "yh", "z")), check_vma=False
    )
```

time: 234 us -> 107 us (0.46)
  waiting for transfers between devices: 147 us -> 47 us
  starting transfers between devices: 0.09 us -> 47.4 us
  blocking collectives: 31.7 us -> 0 us
  matrix products: 25.5 us -> 0 us
  between operations: 13.2 us -> 0.29 us
  local copies, waits for them, and re-layouts: 15.1 us -> 4.11 us
  Pallas kernels: 0 us -> 5.32 us
  other arithmetic: 0.05 us -> 2.41 us
    reduce_scatter x2 -> x0, waiting for transfers between devices: 74.2 us -> none  [sum_in_order(): tiles = lax.psum_scatter(tiles, axes[k], scatter_dimension=0, tiled=True)]
    all_gather x1 -> x0, waiting for transfers between devices: 73.2 us -> none  [shards(): slab = lax.all_gather(right_used, 'row', axis=0, tiled=True)]
    ppermute x0 -> x25, starting transfers between devices: none -> 47.4 us  [permute(): return lax.ppermute(value, AXES, pairs)]
    ppermute x0 -> x25, waiting for transfers between devices: none -> 47 us  [permute(): return lax.ppermute(value, AXES, pairs)]
    all_to_all x1 -> x0, blocking collectives: 31.7 us -> none  [copy_for_each(): lax.all_to_all(jnp.broadcast_to(value[None], (length, *value.shape)), axi...]
    dot_general x7 -> x0, matrix products: 25.5 us -> none  [the longest x1 16.1 us: shards(): jnp.dot(gather_directly(left_used, 'col', 1), slab, precision=lax.Precisi...]
    dot_general x1 -> x0, local copies, waits for them, and re-layouts: 9.39 us -> none  [shards(): jnp.dot(gather_directly(left_used, 'col', 1), slab, precision=lax.Precisi...]
    pallas_call x0 -> x7, Pallas kernels: none -> 5.32 us  [the longest x2 4.27 us: product(): pl.pallas_call(lambda *refs: product_kernel(rows, plan, *refs), out_shape...]
  transfers between devices with their start and end apart: 3 -> 25, of which waited for: 3 -> 11; matrix products, arithmetic and copies ran while one was open for 2% -> 2% of each run, Pallas kernels for 0% -> 5%
where the time goes in v2:
time: 107 us; the launch traced here: 106 us
  starting transfers between devices  47.4 us (44%)
  waiting for transfers between devices  47 us (44%)
  Pallas kernels  5.32 us (5%)
  local copies, waits for them, and re-layouts  4.11 us (4%)
  other arithmetic  2.41 us (2%)
    ppermute x25, starting transfers between devices, permute(): return lax.ppermute(value, AXES, pairs)  47.4 us
    ppermute x25, waiting for transfers between devices, permute(): return lax.ppermute(value, AXES, pairs)  47 us
    pallas_call x2, Pallas kernels, product(): pl.pallas_call(lambda *refs: product_kernel(rows, plan, *refs), out_shape...  4.27 us
    unnamed x8, local copies, waits for them, and re-layouts  2.2 us
  transfers between devices with their start and end apart: 25, of which 11 were waited for; matrix products, arithmetic and copies ran while one was open for 2% of the time, Pallas kernels for 5%

profile of v2, /device:TPU:0, one launch (start us, length us, event | category | flops | bytes accessed | tf_op | source)
XLA Modules:
  0.0 106.5 jit_solution(12028842269024924553)
XLA Ops:
  0.9 5.0 %collective-permute-start.6 = (f32[320,128]{1,0:T(8,128)S(1)}, f32[320,128]{1,0:T(8,128)S(1)}, u32[]{:S(2)}, u32[]{:S(2)}) collective-permute-start(f32[320,128]{1,0:T(8,128)S(1)} %slice.79), channel_id=1, source_target_pairs={{0,32},{1,33},{2,34},{3,35},{4,36},{5,37},{6,38},{7,39},{8,40},{9,... | collective-permute-start | bytes 491528 | tf_op jit(solution)/shard_map/ppermute | solution.py:27
  7.3 5.3 %collective-permute-start.5 = (f32[320,128]{1,0:T(8,128)S(1)}, f32[320,128]{1,0:T(8,128)S(1)}, u32[]{:S(2)}, u32[]{:S(2)}) collective-permute-start(f32[320,128]{1,0:T(8,128)S(1)} %slice.79), channel_id=1, source_target_pairs={{0,48},{1,49},{2,50},{3,51},{4,52},{5,53},{6,54},{7,55},{8,56},{9,... | collective-permute-start | bytes 491528 | tf_op jit(solution)/shard_map/ppermute | solution.py:27
  12.5 1.9 %collective-permute-start.4 = (f32[320,128]{1,0:T(8,128)S(1)}, f32[320,128]{1,0:T(8,128)S(1)}, u32[]{:S(2)}, u32[]{:S(2)}) collective-permute-start(f32[320,128]{1,0:T(8,128)S(1)} %slice.79), channel_id=1, source_target_pairs={{0,16},{1,17},{2,18},{3,19},{4,20},{5,21},{6,22},{7,23},{8,24},{9,... | collective-permute-start | bytes 491528 | tf_op jit(solution)/shard_map/ppermute | solution.py:27
  17.8 2.0 %collective-permute-done.4 = f32[320,128]{1,0:T(8,128)S(1)} collective-permute-done((f32[320,128]{1,0:T(8,128)S(1)}, f32[320,128]{1,0:T(8,128)S(1)}, u32[]{:S(2)}, u32[]{:S(2)}) %collective-permute-start.4) | collective-permute-done | bytes 163872 | tf_op jit(solution)/shard_map/ppermute | solution.py:27
  19.9 2.2 %copy-done = f32[512,2048]{1,0:T(8,128)S(1)} copy-done((f32[512,2048]{1,0:T(8,128)S(1)}, f32[512,2048]{1,0:T(8,128)}, u32[]{:S(2)}) %copy-start) | copy-done | bytes 4194328
  24.3 2.4 %collective-permute-start.1 = (f32[704,128]{1,0:T(8,128)S(1)}, f32[704,128]{1,0:T(8,128)S(1)}, u32[]{:S(2)}, u32[]{:S(2)}) collective-permute-start(f32[704,128]{1,0:T(8,128)S(1)} %pad_maximum_fusion.1), channel_id=1, source_target_pairs={{0,16},{1,17},{2,18},{3,19},{4,20},{5,21},{6,22},{7,23},{8,24},{9,... | collective-permute-start | bytes 1081352 | tf_op jit(solution)/shard_map/ppermute | solution.py:27
  26.8 1.9 %shard_map.56 = (f32[2,320,256]{2,1,0:T(8,128)S(1)}, f32[2,320,256]{2,1,0:T(8,128)S(1)}, f32[4,320,256]{2,1,0:T(8,128)S(1)}) custom-call(s32[5]{0:T(128)S(1)} %stack.23.refs_0_, s32[2,16]{1,0:T(2,128)S(1)} %copy-done.2, s32[16,32]{1,0:T(8,128)S(1)} %copy-done.1, s32[2,32]{1,0:T(2,128)S(1)} %copy-done.3, f32[320,128]{1,0:T(8,128)S(1)} %broadcast_select_fusion.3.refs_4_, ...), custom_call_target="tpu_custom_call" | custom-call | flops 2013265920 | bytes 4194304 | tf_op jit(solution)/shard_map/pallas_call | solution.py:117
  28.8 6.7 %collective-permute-done.2 = f32[704,128]{1,0:T(8,128)S(1)} collective-permute-done((f32[704,128]{1,0:T(8,128)S(1)}, f32[704,128]{1,0:T(8,128)S(1)}, u32[]{:S(2)}, u32[]{:S(2)}) %collective-permute-start.2) | collective-permute-done | bytes 360480 | tf_op jit(solution)/shard_map/ppermute | solution.py:27
  39.1 2.0 %collective-permute-start.11 = (f32[2,320,256]{2,1,0:T(8,128)S(1)}, f32[2,320,256]{2,1,0:T(8,128)S(1)}, u32[]{:S(2)}, u32[]{:S(2)}) collective-permute-start(f32[2,320,256]{2,1,0:T(8,128)S(1)} %get-tuple-element.27), channel_id=1, source_target_pairs={{0,68},{1,69},{2,70},{3,71},{4,64},{5,65},{6,66},{7,67},{8,76},{9,... | collective-permute-start | bytes 1966088 | tf_op jit(solution)/shard_map/ppermute | solution.py:27
  41.1 2.3 %shard_map.57 = (f32[4,320,256]{2,1,0:T(8,128)S(1)}, f32[4,320,256]{2,1,0:T(8,128)S(1)}, f32[2,192,256]{2,1,0:T(8,128)S(1)}, f32[2,192,256]{2,1,0:T(8,128)S(1)},...) custom-call(s32[5]{0:T(128)S(1)} %stack.23.refs_0_, s32[2,16]{1,0:T(2,128)S(1)} %copy-done.2, ...), custom_call_target="tpu_custom_call" | custom-call | flops 4429185024 | bytes 4194304 | tf_op jit(solution)/shard_map/pallas_call | solution.py:117
  43.4 3.5 %collective-permute-start.20 = (f32[2,192,256]{2,1,0:T(8,128)S(1)}, f32[2,192,256]{2,1,0:T(8,128)S(1)}, u32[]{:S(2)}, u32[]{:S(2)}) collective-permute-start(f32[2,192,256]{2,1,0:T(8,128)S(1)} %get-tuple-element.34), channel_id=1, source_target_pairs={{0,1},{1,0},{2,3},{3,2},{4,5},{5,4},{6,7},{7,6},{8,9},{9,8},{10,11... | collective-permute-start | bytes 1179656 | tf_op jit(solution)/shard_map/ppermute | solution.py:27
  47.0 2.5 %collective-permute-start.18 = (f32[2,192,256]{2,1,0:T(8,128)S(1)}, f32[2,192,256]{2,1,0:T(8,128)S(1)}, u32[]{:S(2)}, u32[]{:S(2)}) collective-permute-start(f32[2,192,256]{2,1,0:T(8,128)S(1)} %get-tuple-element.32), channel_id=1, source_target_pairs={{0,3},{1,2},{2,1},{3,0},{4,7},{5,6},{6,5},{7,4},{8,11},{9,10},{10,... | collective-permute-start | bytes 1179656 | tf_op jit(solution)/shard_map/ppermute | solution.py:27
  49.5 4.9 %collective-permute-done.13.arrived_ref = f32[2,320,256]{2,1,0:T(8,128)S(1)} collective-permute-done((f32[2,320,256]{2,1,0:T(8,128)S(1)}, f32[2,320,256]{2,1,0:T(8,128)S(1)}, u32[]{:S(2)}, u32[]{:S(2)}) %collective-permute-start.13) | collective-permute-done | bytes 655392 | tf_op jit(solution)/shard_map/ppermute | solution.py:27
  54.4 3.3 %collective-permute-start.14 = (f32[4,320,256]{2,1,0:T(8,128)S(1)}, f32[4,320,256]{2,1,0:T(8,128)S(1)}, u32[]{:S(2)}, u32[]{:S(2)}) collective-permute-start(f32[4,320,256]{2,1,0:T(8,128)S(1)} %shard_map.59), channel_id=1, source_target_pairs={{0,68},{1,69},{2,70},{3,71},{4,64},{5,65},{6,66},{7,67},{8,76},{9,... | collective-permute-start | bytes 3932168 | tf_op jit(solution)/shard_map/ppermute | solution.py:27
  58.0 4.1 %collective-permute-start.21 = (f32[4,192,256]{2,1,0:T(8,128)S(1)}, f32[4,192,256]{2,1,0:T(8,128)S(1)}, u32[]{:S(2)}, u32[]{:S(2)}) collective-permute-start(f32[4,192,256]{2,1,0:T(8,128)S(1)} %shard_map.61), channel_id=1, source_target_pairs={{0,3},{1,2},{2,1},{3,0},{4,7},{5,6},{6,5},{7,4},{8,11},{9,10},{10,... | collective-permute-start | bytes 2359304 | tf_op jit(solution)/shard_map/ppermute | solution.py:27
  62.3 16.5 %collective-permute-done.21 = f32[4,192,256]{2,1,0:T(8,128)S(1)} collective-permute-done((f32[4,192,256]{2,1,0:T(8,128)S(1)}, f32[4,192,256]{2,1,0:T(8,128)S(1)}, u32[]{:S(2)}, u32[]{:S(2)}) %collective-permute-start.21) | collective-permute-done | bytes 786464 | tf_op jit(solution)/shard_map/ppermute | solution.py:27
  78.8 1.6 %collective-permute-done.19 = f32[4,192,256]{2,1,0:T(8,128)S(1)} collective-permute-done((f32[4,192,256]{2,1,0:T(8,128)S(1)}, f32[4,192,256]{2,1,0:T(8,128)S(1)}, u32[]{:S(2)}, u32[]{:S(2)}) %collective-permute-start.19) | collective-permute-done | bytes 786464 | tf_op jit(solution)/shard_map/ppermute | solution.py:27
  80.5 2.3 %collective-permute-start.22 = (f32[192,256]{1,0:T(8,128)S(1)}, f32[192,256]{1,0:T(8,128)S(1)}, u32[]{:S(2)}, u32[]{:S(2)}) collective-permute-start(f32[192,256]{1,0:T(8,128)S(1)} %get-tuple-element.38), channel_id=1, source_target_pairs={{0,4},{1,5},{2,6},{3,7},{4,0},{5,1},{6,2},{7,3},{8,12},{9,13},{10,... | collective-permute-start | bytes 589832 | tf_op jit(solution)/shard_map/ppermute | solution.py:27
  82.8 2.1 %collective-permute-start.24 = (f32[192,256]{1,0:T(8,128)S(1)}, f32[192,256]{1,0:T(8,128)S(1)}, u32[]{:S(2)}, u32[]{:S(2)}) collective-permute-start(f32[192,256]{1,0:T(8,128)S(1)} %get-tuple-element.39), channel_id=1, source_target_pairs={{0,68},{1,69},{2,70},{3,71},{4,64},{5,65},{6,66},{7,67},{8,76},{9,... | collective-permute-start | bytes 589832 | tf_op jit(solution)/shard_map/ppermute | solution.py:27
  85.0 3.9 %collective-permute-done.14 = f32[4,320,256]{2,1,0:T(8,128)S(1)} collective-permute-done((f32[4,320,256]{2,1,0:T(8,128)S(1)}, f32[4,320,256]{2,1,0:T(8,128)S(1)}, u32[]{:S(2)}, u32[]{:S(2)}) %collective-permute-start.14) | collective-permute-done | bytes 1310752 | tf_op jit(solution)/shard_map/ppermute | solution.py:27
  89.8 4.0 %collective-permute-start.15 = (f32[320,256]{1,0:T(8,128)S(1)}, f32[320,256]{1,0:T(8,128)S(1)}, u32[]{:S(2)}, u32[]{:S(2)}) collective-permute-start(f32[320,256]{1,0:T(8,128)S(1)} %get-tuple-element.35), channel_id=1, source_target_pairs={{0,2},{1,3},{2,0},{3,1},{4,6},{5,7},{6,4},{7,5},{8,10},{9,11},{10,... | collective-permute-start | bytes 983048 | tf_op jit(solution)/shard_map/ppermute | solution.py:27
  94.5 1.8 %collective-permute-start.16 = (f32[320,256]{1,0:T(8,128)S(1)}, f32[320,256]{1,0:T(8,128)S(1)}, u32[]{:S(2)}, u32[]{:S(2)}) collective-permute-start(f32[320,256]{1,0:T(8,128)S(1)} %get-tuple-element.37), channel_id=1, source_target_pairs={{0,1},{1,0},{2,3},{3,2},{4,5},{5,4},{6,7},{7,6},{8,9},{9,8},{10,11... | collective-permute-start | bytes 983048 | tf_op jit(solution)/shard_map/ppermute | solution.py:27
  96.3 4.9 %collective-permute-done.15 = f32[320,256]{1,0:T(8,128)S(1)} collective-permute-done((f32[320,256]{1,0:T(8,128)S(1)}, f32[320,256]{1,0:T(8,128)S(1)}, u32[]{:S(2)}, u32[]{:S(2)}) %collective-permute-start.15) | collective-permute-done | bytes 327712 | tf_op jit(solution)/shard_map/ppermute | solution.py:27
  101.3 3.4 %collective-permute-done.17 = f32[320,256]{1,0:T(8,128)S(1)} collective-permute-done((f32[320,256]{1,0:T(8,128)S(1)}, f32[320,256]{1,0:T(8,128)S(1)}, u32[]{:S(2)}, u32[]{:S(2)}) %collective-permute-start.17) | collective-permute-done | bytes 327712 | tf_op jit(solution)/shard_map/ppermute | solution.py:27
  (54 shorter events, 15.5 us)
Async XLA Ops:
  0.9 14.4 %collective-permute-start.6 = (f32[320,128]{1,0:T(8,128)S(1)}, f32[320,128]{1,0:T(8,128)S(1)}, u32[]{:S(2)}, u32[]{:S(2)}) collective-permute-start(f32[320,128]{1,0:T(8,128)S(1)} %slice.79), channel_id=1, source_target_pairs={{0,32},{1,33},{2,34},{3,35},{4,36},{5,37},{6,38},{7,39},{8,40},{9,... | collective-permute-start | bytes 491528 | tf_op jit(solution)/shard_map/ppermute | solution.py:27
  6.0 10.4 %collective-permute-start = (f32[512,128]{1,0:T(8,128)}, f32[512,128]{1,0:T(8,128)S(1)}, u32[]{:S(2)}, u32[]{:S(2)}) collective-permute-start(f32[512,128]{1,0:T(8,128)} %param.5), channel_id=1, source_target_pairs={{32,96},{33,97},{34,98},{35,99},{36,100},{37,101},{38,102},{39,103... | collective-permute-start | bytes 786440 | tf_op jit(solution)/shard_map/ppermute | solution.py:27
  7.3 10.5 %collective-permute-start.5 = (f32[320,128]{1,0:T(8,128)S(1)}, f32[320,128]{1,0:T(8,128)S(1)}, u32[]{:S(2)}, u32[]{:S(2)}) collective-permute-start(f32[320,128]{1,0:T(8,128)S(1)} %slice.79), channel_id=1, source_target_pairs={{0,48},{1,49},{2,50},{3,51},{4,52},{5,53},{6,54},{7,55},{8,56},{9,... | collective-permute-start | bytes 491528 | tf_op jit(solution)/shard_map/ppermute | solution.py:27
  12.5 7.2 %collective-permute-start.4 = (f32[320,128]{1,0:T(8,128)S(1)}, f32[320,128]{1,0:T(8,128)S(1)}, u32[]{:S(2)}, u32[]{:S(2)}) collective-permute-start(f32[320,128]{1,0:T(8,128)S(1)} %slice.79), channel_id=1, source_target_pairs={{0,16},{1,17},{2,18},{3,19},{4,20},{5,21},{6,22},{7,23},{8,24},{9,... | collective-permute-start | bytes 491528 | tf_op jit(solution)/shard_map/ppermute | solution.py:27
  16.3 10.4 %collective-permute-start.8 = (f32[320,128]{1,0:T(8,128)S(1)}, f32[320,128]{1,0:T(8,128)S(1)}, u32[]{:S(2)}, u32[]{:S(2)}) collective-permute-start(f32[320,128]{1,0:T(8,128)S(1)} %broadcast_select_fusion.2.refs_5_), channel_id=1, source_target_pairs={{0,8},{1,9},{2,10},{3,11},{4,12},{5,13},{6,14},{7,15},{8,0},{9,1},... | collective-permute-start | bytes 491528 | tf_op jit(solution)/shard_map/ppermute | solution.py:27
  16.4 12.3 %collective-permute-start.3 = (f32[704,128]{1,0:T(8,128)S(1)}, f32[704,128]{1,0:T(8,128)S(1)}, u32[]{:S(2)}, u32[]{:S(2)}) collective-permute-start(f32[704,128]{1,0:T(8,128)S(1)} %pad_maximum_fusion.1), channel_id=1, source_target_pairs={{0,32},{1,33},{2,34},{3,35},{4,36},{5,37},{6,38},{7,39},{8,40},{9,... | collective-permute-start | bytes 1081352 | tf_op jit(solution)/shard_map/ppermute | solution.py:27
  19.8 7.0 %collective-permute-start.7 = (f32[320,128]{1,0:T(8,128)S(1)}, f32[320,128]{1,0:T(8,128)S(1)}, u32[]{:S(2)}, u32[]{:S(2)}) collective-permute-start(f32[320,128]{1,0:T(8,128)S(1)} %broadcast_select_fusion.3.refs_4_), channel_id=1, source_target_pairs={{0,8},{1,9},{2,10},{3,11},{4,12},{5,13},{6,14},{7,15},{8,0},{9,1},... | collective-permute-start | bytes 491528 | tf_op jit(solution)/shard_map/ppermute | solution.py:27
  23.0 12.5 %collective-permute-start.2 = (f32[704,128]{1,0:T(8,128)S(1)}, f32[704,128]{1,0:T(8,128)S(1)}, u32[]{:S(2)}, u32[]{:S(2)}) collective-permute-start(f32[704,128]{1,0:T(8,128)S(1)} %pad_maximum_fusion.1), channel_id=1, source_target_pairs={{0,48},{1,49},{2,50},{3,51},{4,52},{5,53},{6,54},{7,55},{8,56},{9,... | collective-permute-start | bytes 1081352 | tf_op jit(solution)/shard_map/ppermute | solution.py:27
  24.3 12.7 %collective-permute-start.1 = (f32[704,128]{1,0:T(8,128)S(1)}, f32[704,128]{1,0:T(8,128)S(1)}, u32[]{:S(2)}, u32[]{:S(2)}) collective-permute-start(f32[704,128]{1,0:T(8,128)S(1)} %pad_maximum_fusion.1), channel_id=1, source_target_pairs={{0,16},{1,17},{2,18},{3,19},{4,20},{5,21},{6,22},{7,23},{8,24},{9,... | collective-permute-start | bytes 1081352 | tf_op jit(solution)/shard_map/ppermute | solution.py:27
  37.0 4.1 %collective-permute-start.9 = (f32[704,128]{1,0:T(8,128)S(1)}, f32[704,128]{1,0:T(8,128)S(1)}, u32[]{:S(2)}, u32[]{:S(2)}) collective-permute-start(f32[704,128]{1,0:T(8,128)S(1)} %broadcast_select_fusion.1.refs_4_), channel_id=1, source_target_pairs={{0,8},{1,9},{2,10},{3,11},{4,12},{5,13},{6,14},{7,15},{8,0},{9,1},... | collective-permute-start | bytes 1081352 | tf_op jit(solution)/shard_map/ppermute | solution.py:27
  37.6 16.7 %collective-permute-start.13 = (f32[2,320,256]{2,1,0:T(8,128)S(1)}, f32[2,320,256]{2,1,0:T(8,128)S(1)}, u32[]{:S(2)}, u32[]{:S(2)}) collective-permute-start(f32[2,320,256]{2,1,0:T(8,128)S(1)} %get-tuple-element.29), channel_id=1, source_target_pairs={{0,64},{1,65},{2,66},{3,67},{4,68},{5,69},{6,70},{7,71},{8,72},{9,... | collective-permute-start | bytes 1966088 | tf_op jit(solution)/shard_map/ppermute | solution.py:27
  39.1 18.6 %collective-permute-start.11 = (f32[2,320,256]{2,1,0:T(8,128)S(1)}, f32[2,320,256]{2,1,0:T(8,128)S(1)}, u32[]{:S(2)}, u32[]{:S(2)}) collective-permute-start(f32[2,320,256]{2,1,0:T(8,128)S(1)} %get-tuple-element.27), channel_id=1, source_target_pairs={{0,68},{1,69},{2,70},{3,71},{4,64},{5,65},{6,66},{7,67},{8,76},{9,... | collective-permute-start | bytes 1966088 | tf_op jit(solution)/shard_map/ppermute | solution.py:27
  43.4 14.5 %collective-permute-start.20 = (f32[2,192,256]{2,1,0:T(8,128)S(1)}, f32[2,192,256]{2,1,0:T(8,128)S(1)}, u32[]{:S(2)}, u32[]{:S(2)}) collective-permute-start(f32[2,192,256]{2,1,0:T(8,128)S(1)} %get-tuple-element.34), channel_id=1, source_target_pairs={{0,1},{1,0},{2,3},{3,2},{4,5},{5,4},{6,7},{7,6},{8,9},{9,8},{10,11... | collective-permute-start | bytes 1179656 | tf_op jit(solution)/shard_map/ppermute | solution.py:27
  47.0 15.1 %collective-permute-start.18 = (f32[2,192,256]{2,1,0:T(8,128)S(1)}, f32[2,192,256]{2,1,0:T(8,128)S(1)}, u32[]{:S(2)}, u32[]{:S(2)}) collective-permute-start(f32[2,192,256]{2,1,0:T(8,128)S(1)} %get-tuple-element.32), channel_id=1, source_target_pairs={{0,3},{1,2},{2,1},{3,0},{4,7},{5,6},{6,5},{7,4},{8,11},{9,10},{10,... | collective-permute-start | bytes 1179656 | tf_op jit(solution)/shard_map/ppermute | solution.py:27
  54.4 34.5 %collective-permute-start.14 = (f32[4,320,256]{2,1,0:T(8,128)S(1)}, f32[4,320,256]{2,1,0:T(8,128)S(1)}, u32[]{:S(2)}, u32[]{:S(2)}) collective-permute-start(f32[4,320,256]{2,1,0:T(8,128)S(1)} %shard_map.59), channel_id=1, source_target_pairs={{0,68},{1,69},{2,70},{3,71},{4,64},{5,65},{6,66},{7,67},{8,76},{9,... | collective-permute-start | bytes 3932168 | tf_op jit(solution)/shard_map/ppermute | solution.py:27
  57.8 31.8 %collective-permute-start.12 = (f32[4,320,256]{2,1,0:T(8,128)S(1)}, f32[4,320,256]{2,1,0:T(8,128)S(1)}, u32[]{:S(2)}, u32[]{:S(2)}) collective-permute-start(f32[4,320,256]{2,1,0:T(8,128)S(1)} %shard_map.58), channel_id=1, source_target_pairs={{0,64},{1,65},{2,66},{3,67},{4,68},{5,69},{6,70},{7,71},{8,72},{9,... | collective-permute-start | bytes 3932168 | tf_op jit(solution)/shard_map/ppermute | solution.py:27
  58.0 20.8 %collective-permute-start.21 = (f32[4,192,256]{2,1,0:T(8,128)S(1)}, f32[4,192,256]{2,1,0:T(8,128)S(1)}, u32[]{:S(2)}, u32[]{:S(2)}) collective-permute-start(f32[4,192,256]{2,1,0:T(8,128)S(1)} %shard_map.61), channel_id=1, source_target_pairs={{0,3},{1,2},{2,1},{3,0},{4,7},{5,6},{6,5},{7,4},{8,11},{9,10},{10,... | collective-permute-start | bytes 2359304 | tf_op jit(solution)/shard_map/ppermute | solution.py:27
  62.2 18.2 %collective-permute-start.19 = (f32[4,192,256]{2,1,0:T(8,128)S(1)}, f32[4,192,256]{2,1,0:T(8,128)S(1)}, u32[]{:S(2)}, u32[]{:S(2)}) collective-permute-start(f32[4,192,256]{2,1,0:T(8,128)S(1)} %shard_map.60), channel_id=1, source_target_pairs={{0,1},{1,0},{2,3},{3,2},{4,5},{5,4},{6,7},{7,6},{8,9},{9,8},{10,11... | collective-permute-start | bytes 2359304 | tf_op jit(solution)/shard_map/ppermute | solution.py:27
  80.5 14.0 %collective-permute-start.22 = (f32[192,256]{1,0:T(8,128)S(1)}, f32[192,256]{1,0:T(8,128)S(1)}, u32[]{:S(2)}, u32[]{:S(2)}) collective-permute-start(f32[192,256]{1,0:T(8,128)S(1)} %get-tuple-element.38), channel_id=1, source_target_pairs={{0,4},{1,5},{2,6},{3,7},{4,0},{5,1},{6,2},{7,3},{8,12},{9,13},{10,... | collective-permute-start | bytes 589832 | tf_op jit(solution)/shard_map/ppermute | solution.py:27
  82.8 13.4 %collective-permute-start.24 = (f32[192,256]{1,0:T(8,128)S(1)}, f32[192,256]{1,0:T(8,128)S(1)}, u32[]{:S(2)}, u32[]{:S(2)}) collective-permute-start(f32[192,256]{1,0:T(8,128)S(1)} %get-tuple-element.39), channel_id=1, source_target_pairs={{0,68},{1,69},{2,70},{3,71},{4,64},{5,65},{6,66},{7,67},{8,76},{9,... | collective-permute-start | bytes 589832 | tf_op jit(solution)/shard_map/ppermute | solution.py:27
  85.0 11.3 %collective-permute-start.23 = (f32[192,256]{1,0:T(8,128)S(1)}, f32[192,256]{1,0:T(8,128)S(1)}, u32[]{:S(2)}, u32[]{:S(2)}) collective-permute-start(f32[192,256]{1,0:T(8,128)S(1)} %get-tuple-element.40), channel_id=1, source_target_pairs={{0,64},{1,65},{2,66},{3,67},{4,68},{5,69},{6,70},{7,71},{8,72},{9,... | collective-permute-start | bytes 589832 | tf_op jit(solution)/shard_map/ppermute | solution.py:27
  89.8 11.4 %collective-permute-start.15 = (f32[320,256]{1,0:T(8,128)S(1)}, f32[320,256]{1,0:T(8,128)S(1)}, u32[]{:S(2)}, u32[]{:S(2)}) collective-permute-start(f32[320,256]{1,0:T(8,128)S(1)} %get-tuple-element.35), channel_id=1, source_target_pairs={{0,2},{1,3},{2,0},{3,1},{4,6},{5,7},{6,4},{7,5},{8,10},{9,11},{10,... | collective-permute-start | bytes 983048 | tf_op jit(solution)/shard_map/ppermute | solution.py:27
  93.8 10.9 %collective-permute-start.17 = (f32[320,256]{1,0:T(8,128)S(1)}, f32[320,256]{1,0:T(8,128)S(1)}, u32[]{:S(2)}, u32[]{:S(2)}) collective-permute-start(f32[320,256]{1,0:T(8,128)S(1)} %get-tuple-element.36), channel_id=1, source_target_pairs={{0,3},{1,2},{2,1},{3,0},{4,7},{5,6},{6,5},{7,4},{8,11},{9,10},{10,... | collective-permute-start | bytes 983048 | tf_op jit(solution)/shard_map/ppermute | solution.py:27
  94.5 11.0 %collective-permute-start.16 = (f32[320,256]{1,0:T(8,128)S(1)}, f32[320,256]{1,0:T(8,128)S(1)}, u32[]{:S(2)}, u32[]{:S(2)}) collective-permute-start(f32[320,256]{1,0:T(8,128)S(1)} %get-tuple-element.37), channel_id=1, source_target_pairs={{0,1},{1,0},{2,3},{3,2},{4,5},{5,4},{6,7},{7,6},{8,9},{9,8},{10,11... | collective-permute-start | bytes 983048 | tf_op jit(solution)/shard_map/ppermute | solution.py:27
  (5 other events, 20.1 us)

commit v3 on v2

--- a/solution.py
+++ b/solution.py
@@ -60,7 +60,7 @@
         in_specs=[VMEM],
         out_specs=[VMEM] * 2,
         compiler_params=pltpu.CompilerParams(vmem_limit_bytes=32 * 2**20),
-        cost_estimate=pl.CostEstimate(flops=3 * right.size, bytes_accessed=8 * right.size, transcendentals=0),
+        cost_estimate=pl.CostEstimate(flops=1, bytes_accessed=1, transcendentals=0),
     )(right)
 
 
@@ -121,7 +121,7 @@
         out_specs=[VMEM] * len(names),
         scratch_shapes=[pltpu.VMEM((pieces[0].shape[0], TILE), jnp.bfloat16)] * 2,
         compiler_params=pltpu.CompilerParams(vmem_limit_bytes=32 * 2**20),
-        cost_estimate=pl.CostEstimate(flops=work, bytes_accessed=4 * 2**20, transcendentals=0),
+        cost_estimate=pl.CostEstimate(flops=1, bytes_accessed=1, transcendentals=0),
     )(spots, *masks, *pieces, *right)
     return dict(zip(names, outs))
 
@@ -139,7 +139,7 @@
         out_specs=VMEM,
         input_output_aliases={0: 0},
         compiler_params=pltpu.CompilerParams(vmem_limit_bytes=32 * 2**20),
-        cost_estimate=pl.CostEstimate(flops=arrived.size, bytes_accessed=12 * arrived.size, transcendentals=0),
+        cost_estimate=pl.CostEstimate(flops=1, bytes_accessed=1, transcendentals=0),
     )(value, arrived)
 
 

time: 107 us -> 106 us (level)
  waiting for transfers between devices: 47 us -> 41.2 us
  local copies, waits for them, and re-layouts: 4.11 us -> 7.04 us
  starting transfers between devices: 47.4 us -> 49.8 us
  Pallas kernels: 5.32 us -> 3.84 us
    ppermute x25, waiting for transfers between devices: 47 us -> 41.2 us  [permute(): return lax.ppermute(value, AXES, pairs)]
    unnamed x8 -> x12, local copies, waits for them, and re-layouts: 2.2 us -> 5.13 us
    ppermute x25, starting transfers between devices: 47.4 us -> 49.8 us  [permute(): return lax.ppermute(value, AXES, pairs)]
    pallas_call x2, Pallas kernels: 4.27 us -> 2.79 us  [product(): pl.pallas_call(lambda *refs: product_kernel(rows, plan, *refs), out_shape...]
  transfers between devices with their start and end apart: 25 -> 25, of which waited for: 11 -> 11; matrix products, arithmetic and copies ran while one was open for 2% -> 3% of each run, Pallas kernels for 5% -> 4%
where the time goes in v3:
time: 106 us
  starting transfers between devices  49.8 us (47%)
  waiting for transfers between devices  41.2 us (39%)
  local copies, waits for them, and re-layouts  7.04 us (7%)
  Pallas kernels  3.84 us (4%)
  other arithmetic  3.41 us (3%)
    ppermute x25, starting transfers between devices, permute(): return lax.ppermute(value, AXES, pairs)  49.8 us
    ppermute x25, waiting for transfers between devices, permute(): return lax.ppermute(value, AXES, pairs)  41.2 us
    unnamed x12, local copies, waits for them, and re-layouts  5.13 us
    pallas_call x2, Pallas kernels, product(): pl.pallas_call(lambda *refs: product_kernel(rows, plan, *refs), out_shape...  2.79 us
  transfers between devices with their start and end apart: 25, of which 11 were waited for; matrix products, arithmetic and copies ran while one was open for 3% of the time, Pallas kernels for 4%

profile of v3, /device:TPU:0, one launch (start us, length us, event | category | flops | bytes accessed | tf_op | source)
XLA Modules:
  0.0 105.6 jit_solution(17996116758991861436)
XLA Ops:
  0.9 5.0 %collective-permute-start.6 = (f32[320,128]{1,0:T(8,128)S(1)}, f32[320,128]{1,0:T(8,128)S(1)}, u32[]{:S(2)}, u32[]{:S(2)}) collective-permute-start(f32[320,128]{1,0:T(8,128)S(1)} %slice.79), channel_id=1, source_target_pairs={{0,32},{1,33},{2,34},{3,35},{4,36},{5,37},{6,38},{7,39},{8,40},{9,... | collective-permute-start | bytes 491528 | tf_op jit(solution)/shard_map/ppermute | solution.py:27
  7.3 5.3 %collective-permute-start.5 = (f32[320,128]{1,0:T(8,128)S(1)}, f32[320,128]{1,0:T(8,128)S(1)}, u32[]{:S(2)}, u32[]{:S(2)}) collective-permute-start(f32[320,128]{1,0:T(8,128)S(1)} %slice.79), channel_id=1, source_target_pairs={{0,48},{1,49},{2,50},{3,51},{4,52},{5,53},{6,54},{7,55},{8,56},{9,... | collective-permute-start | bytes 491528 | tf_op jit(solution)/shard_map/ppermute | solution.py:27
  12.5 1.9 %collective-permute-start.4 = (f32[320,128]{1,0:T(8,128)S(1)}, f32[320,128]{1,0:T(8,128)S(1)}, u32[]{:S(2)}, u32[]{:S(2)}) collective-permute-start(f32[320,128]{1,0:T(8,128)S(1)} %slice.79), channel_id=1, source_target_pairs={{0,16},{1,17},{2,18},{3,19},{4,20},{5,21},{6,22},{7,23},{8,24},{9,... | collective-permute-start | bytes 491528 | tf_op jit(solution)/shard_map/ppermute | solution.py:27
  16.4 2.4 %collective-permute-start.2 = (f32[704,128]{1,0:T(8,128)S(1)}, f32[704,128]{1,0:T(8,128)}, u32[]{:S(2)}, u32[]{:S(2)}) collective-permute-start(f32[704,128]{1,0:T(8,128)S(1)} %pad_maximum_fusion.1), channel_id=1, source_target_pairs={{0,48},{1,49},{2,50},{3,51},{4,52},{5,53},{6,54},{7,55},{8,56},{9,... | collective-permute-start | bytes 1081352 | tf_op jit(solution)/shard_map/ppermute | solution.py:27
  18.9 3.5 %collective-permute-start.1 = (f32[704,128]{1,0:T(8,128)S(1)}, f32[704,128]{1,0:T(8,128)}, u32[]{:S(2)}, u32[]{:S(2)}) collective-permute-start(f32[704,128]{1,0:T(8,128)S(1)} %pad_maximum_fusion.1), channel_id=1, source_target_pairs={{0,16},{1,17},{2,18},{3,19},{4,20},{5,21},{6,22},{7,23},{8,24},{9,... | collective-permute-start | bytes 1081352 | tf_op jit(solution)/shard_map/ppermute | solution.py:27
  22.8 2.0 %collective-permute-start.3 = (f32[704,128]{1,0:T(8,128)S(1)}, f32[704,128]{1,0:T(8,128)}, u32[]{:S(2)}, u32[]{:S(2)}) collective-permute-start(f32[704,128]{1,0:T(8,128)S(1)} %pad_maximum_fusion.1), channel_id=1, source_target_pairs={{0,32},{1,33},{2,34},{3,35},{4,36},{5,37},{6,38},{7,39},{8,40},{9,... | collective-permute-start | bytes 1081352 | tf_op jit(solution)/shard_map/ppermute | solution.py:27
  24.8 2.2 %copy-done.2 = f32[512,2048]{1,0:T(8,128)S(1)} copy-done((f32[512,2048]{1,0:T(8,128)S(1)}, f32[512,2048]{1,0:T(8,128)}, u32[]{:S(2)}) %copy-start.2) | copy-done | bytes 4194328
  29.3 1.6 %copy-done.1 = bf16[512,2048]{1,0:T(8,128)(2,1)S(1)} copy-done((bf16[512,2048]{1,0:T(8,128)(2,1)S(1)}, bf16[512,2048]{1,0:T(8,128)(2,1)}, u32[]{:S(2)}) %copy-start.1) | copy-done | bytes 2097176
  32.2 2.8 %collective-permute-start.13 = (f32[2,320,256]{2,1,0:T(8,128)S(1)}, f32[2,320,256]{2,1,0:T(8,128)S(1)}, u32[]{:S(2)}, u32[]{:S(2)}) collective-permute-start(f32[2,320,256]{2,1,0:T(8,128)S(1)} %get-tuple-element.29), channel_id=1, source_target_pairs={{0,64},{1,65},{2,66},{3,67},{4,68},{5,69},{6,70},{7,71},{8,72},{9,... | collective-permute-start | bytes 1966088 | tf_op jit(solution)/shard_map/ppermute | solution.py:27
  36.0 2.4 %collective-permute-done.3 = f32[704,128]{1,0:T(8,128)} collective-permute-done((f32[704,128]{1,0:T(8,128)S(1)}, f32[704,128]{1,0:T(8,128)}, u32[]{:S(2)}, u32[]{:S(2)}) %collective-permute-start.3) | collective-permute-done | bytes 360480 | tf_op jit(solution)/shard_map/ppermute | solution.py:27
  40.8 1.7 %shard_map.57 = (f32[4,320,256]{2,1,0:T(8,128)S(1)}, f32[4,320,256]{2,1,0:T(8,128)S(1)}, f32[2,192,256]{2,1,0:T(8,128)S(1)}, f32[2,192,256]{2,1,0:T(8,128)S(1)},...) custom-call(s32[5]{0:T(128)S(1)} %stack.23.refs_0_, s32[2,16]{1,0:T(2,128)S(1)} %copy-done.4, ...), custom_call_target="tpu_custom_call" | custom-call | flops 1 | bytes 1 | tf_op jit(solution)/shard_map/pallas_call | solution.py:117
  42.4 2.6 %collective-permute-start.20 = (f32[2,192,256]{2,1,0:T(8,128)S(1)}, f32[2,192,256]{2,1,0:T(8,128)S(1)}, u32[]{:S(2)}, u32[]{:S(2)}) collective-permute-start(f32[2,192,256]{2,1,0:T(8,128)S(1)} %get-tuple-element.34), channel_id=1, source_target_pairs={{0,1},{1,0},{2,3},{3,2},{4,5},{5,4},{6,7},{7,6},{8,9},{9,8},{10,11... | collective-permute-start | bytes 1179656 | tf_op jit(solution)/shard_map/ppermute | solution.py:27
  45.1 1.9 %collective-permute-start.18 = (f32[2,192,256]{2,1,0:T(8,128)S(1)}, f32[2,192,256]{2,1,0:T(8,128)S(1)}, u32[]{:S(2)}, u32[]{:S(2)}) collective-permute-start(f32[2,192,256]{2,1,0:T(8,128)S(1)} %get-tuple-element.32), channel_id=1, source_target_pairs={{0,3},{1,2},{2,1},{3,0},{4,7},{5,6},{6,5},{7,4},{8,11},{9,10},{10,... | collective-permute-start | bytes 1179656 | tf_op jit(solution)/shard_map/ppermute | solution.py:27
  47.0 3.0 %collective-permute-done.13.arrived_ref = f32[2,320,256]{2,1,0:T(8,128)S(1)} collective-permute-done((f32[2,320,256]{2,1,0:T(8,128)S(1)}, f32[2,320,256]{2,1,0:T(8,128)S(1)}, u32[]{:S(2)}, u32[]{:S(2)}) %collective-permute-start.13) | collective-permute-done | bytes 655392 | tf_op jit(solution)/shard_map/ppermute | solution.py:27
  50.0 3.8 %collective-permute-start.14 = (f32[4,320,256]{2,1,0:T(8,128)S(1)}, f32[4,320,256]{2,1,0:T(8,128)S(1)}, u32[]{:S(2)}, u32[]{:S(2)}) collective-permute-start(f32[4,320,256]{2,1,0:T(8,128)S(1)} %shard_map.59), channel_id=1, source_target_pairs={{0,68},{1,69},{2,70},{3,71},{4,64},{5,65},{6,66},{7,67},{8,76},{9,... | collective-permute-start | bytes 3932168 | tf_op jit(solution)/shard_map/ppermute | solution.py:27
  54.3 4.0 %collective-permute-start.21 = (f32[4,192,256]{2,1,0:T(8,128)S(1)}, f32[4,192,256]{2,1,0:T(8,128)S(1)}, u32[]{:S(2)}, u32[]{:S(2)}) collective-permute-start(f32[4,192,256]{2,1,0:T(8,128)S(1)} %shard_map.61), channel_id=1, source_target_pairs={{0,3},{1,2},{2,1},{3,0},{4,7},{5,6},{6,5},{7,4},{8,11},{9,10},{10,... | collective-permute-start | bytes 2359304 | tf_op jit(solution)/shard_map/ppermute | solution.py:27
  58.4 18.2 %collective-permute-done.21 = f32[4,192,256]{2,1,0:T(8,128)S(1)} collective-permute-done((f32[4,192,256]{2,1,0:T(8,128)S(1)}, f32[4,192,256]{2,1,0:T(8,128)S(1)}, u32[]{:S(2)}, u32[]{:S(2)}) %collective-permute-start.21) | collective-permute-done | bytes 786464 | tf_op jit(solution)/shard_map/ppermute | solution.py:27
  76.6 1.5 %collective-permute-done.19 = f32[4,192,256]{2,1,0:T(8,128)S(1)} collective-permute-done((f32[4,192,256]{2,1,0:T(8,128)S(1)}, f32[4,192,256]{2,1,0:T(8,128)S(1)}, u32[]{:S(2)}, u32[]{:S(2)}) %collective-permute-start.19) | collective-permute-done | bytes 786464 | tf_op jit(solution)/shard_map/ppermute | solution.py:27
  78.2 3.7 %collective-permute-start.22 = (f32[192,256]{1,0:T(8,128)S(1)}, f32[192,256]{1,0:T(8,128)S(1)}, u32[]{:S(2)}, u32[]{:S(2)}) collective-permute-start(f32[192,256]{1,0:T(8,128)S(1)} %get-tuple-element.38), channel_id=1, source_target_pairs={{0,4},{1,5},{2,6},{3,7},{4,0},{5,1},{6,2},{7,3},{8,12},{9,13},{10,... | collective-permute-start | bytes 589832 | tf_op jit(solution)/shard_map/ppermute | solution.py:27
  81.9 4.2 %collective-permute-start.24 = (f32[192,256]{1,0:T(8,128)S(1)}, f32[192,256]{1,0:T(8,128)S(1)}, u32[]{:S(2)}, u32[]{:S(2)}) collective-permute-start(f32[192,256]{1,0:T(8,128)S(1)} %get-tuple-element.39), channel_id=1, source_target_pairs={{0,68},{1,69},{2,70},{3,71},{4,64},{5,65},{6,66},{7,67},{8,76},{9,... | collective-permute-start | bytes 589832 | tf_op jit(solution)/shard_map/ppermute | solution.py:27
  86.3 2.2 %collective-permute-start.15 = (f32[320,256]{1,0:T(8,128)S(1)}, f32[320,256]{1,0:T(8,128)S(1)}, u32[]{:S(2)}, u32[]{:S(2)}) collective-permute-start(f32[320,256]{1,0:T(8,128)S(1)} %get-tuple-element.35), channel_id=1, source_target_pairs={{0,2},{1,3},{2,0},{3,1},{4,6},{5,7},{6,4},{7,5},{8,10},{9,11},{10,... | collective-permute-start | bytes 983048 | tf_op jit(solution)/shard_map/ppermute | solution.py:27
  90.4 2.8 %collective-permute-done.24 = f32[192,256]{1,0:T(8,128)S(1)} collective-permute-done((f32[192,256]{1,0:T(8,128)S(1)}, f32[192,256]{1,0:T(8,128)S(1)}, u32[]{:S(2)}, u32[]{:S(2)}) %collective-permute-start.24) | collective-permute-done | bytes 196640 | tf_op jit(solution)/shard_map/ppermute | solution.py:27
  94.0 4.5 %collective-permute-done.15 = f32[320,256]{1,0:T(8,128)S(1)} collective-permute-done((f32[320,256]{1,0:T(8,128)S(1)}, f32[320,256]{1,0:T(8,128)S(1)}, u32[]{:S(2)}, u32[]{:S(2)}) %collective-permute-start.15) | collective-permute-done | bytes 327712 | tf_op jit(solution)/shard_map/ppermute | solution.py:27
  98.5 6.2 %collective-permute-done.17 = f32[320,256]{1,0:T(8,128)S(1)} collective-permute-done((f32[320,256]{1,0:T(8,128)S(1)}, f32[320,256]{1,0:T(8,128)S(1)}, u32[]{:S(2)}, u32[]{:S(2)}) %collective-permute-start.17) | collective-permute-done | bytes 327712 | tf_op jit(solution)/shard_map/ppermute | solution.py:27
  (58 shorter events, 16.0 us)
Async XLA Ops:
  0.9 14.4 %collective-permute-start.6 = (f32[320,128]{1,0:T(8,128)S(1)}, f32[320,128]{1,0:T(8,128)S(1)}, u32[]{:S(2)}, u32[]{:S(2)}) collective-permute-start(f32[320,128]{1,0:T(8,128)S(1)} %slice.79), channel_id=1, source_target_pairs={{0,32},{1,33},{2,34},{3,35},{4,36},{5,37},{6,38},{7,39},{8,40},{9,... | collective-permute-start | bytes 491528 | tf_op jit(solution)/shard_map/ppermute | solution.py:27
  6.0 10.4 %collective-permute-start = (f32[512,128]{1,0:T(8,128)}, f32[512,128]{1,0:T(8,128)S(1)}, u32[]{:S(2)}, u32[]{:S(2)}) collective-permute-start(f32[512,128]{1,0:T(8,128)} %param.5), channel_id=1, source_target_pairs={{32,96},{33,97},{34,98},{35,99},{36,100},{37,101},{38,102},{39,103... | collective-permute-start | bytes 786440 | tf_op jit(solution)/shard_map/ppermute | solution.py:27
  7.3 15.2 %collective-permute-start.5 = (f32[320,128]{1,0:T(8,128)S(1)}, f32[320,128]{1,0:T(8,128)S(1)}, u32[]{:S(2)}, u32[]{:S(2)}) collective-permute-start(f32[320,128]{1,0:T(8,128)S(1)} %slice.79), channel_id=1, source_target_pairs={{0,48},{1,49},{2,50},{3,51},{4,52},{5,53},{6,54},{7,55},{8,56},{9,... | collective-permute-start | bytes 491528 | tf_op jit(solution)/shard_map/ppermute | solution.py:27
  12.5 9.9 %collective-permute-start.4 = (f32[320,128]{1,0:T(8,128)S(1)}, f32[320,128]{1,0:T(8,128)S(1)}, u32[]{:S(2)}, u32[]{:S(2)}) collective-permute-start(f32[320,128]{1,0:T(8,128)S(1)} %slice.79), channel_id=1, source_target_pairs={{0,16},{1,17},{2,18},{3,19},{4,20},{5,21},{6,22},{7,23},{8,24},{9,... | collective-permute-start | bytes 491528 | tf_op jit(solution)/shard_map/ppermute | solution.py:27
  16.3 13.0 %collective-permute-start.8 = (f32[320,128]{1,0:T(8,128)S(1)}, f32[320,128]{1,0:T(8,128)S(1)}, u32[]{:S(2)}, u32[]{:S(2)}) collective-permute-start(f32[320,128]{1,0:T(8,128)S(1)} %broadcast_select_fusion.2.refs_5_), channel_id=1, source_target_pairs={{0,8},{1,9},{2,10},{3,11},{4,12},{5,13},{6,14},{7,15},{8,0},{9,1},... | collective-permute-start | bytes 491528 | tf_op jit(solution)/shard_map/ppermute | solution.py:27
  16.4 18.6 %collective-permute-start.2 = (f32[704,128]{1,0:T(8,128)S(1)}, f32[704,128]{1,0:T(8,128)}, u32[]{:S(2)}, u32[]{:S(2)}) collective-permute-start(f32[704,128]{1,0:T(8,128)S(1)} %pad_maximum_fusion.1), channel_id=1, source_target_pairs={{0,48},{1,49},{2,50},{3,51},{4,52},{5,53},{6,54},{7,55},{8,56},{9,... | collective-permute-start | bytes 1081352 | tf_op jit(solution)/shard_map/ppermute | solution.py:27
  18.9 16.1 %collective-permute-start.1 = (f32[704,128]{1,0:T(8,128)S(1)}, f32[704,128]{1,0:T(8,128)}, u32[]{:S(2)}, u32[]{:S(2)}) collective-permute-start(f32[704,128]{1,0:T(8,128)S(1)} %pad_maximum_fusion.1), channel_id=1, source_target_pairs={{0,16},{1,17},{2,18},{3,19},{4,20},{5,21},{6,22},{7,23},{8,24},{9,... | collective-permute-start | bytes 1081352 | tf_op jit(solution)/shard_map/ppermute | solution.py:27
  22.5 6.8 %collective-permute-start.7 = (f32[320,128]{1,0:T(8,128)S(1)}, f32[320,128]{1,0:T(8,128)S(1)}, u32[]{:S(2)}, u32[]{:S(2)}) collective-permute-start(f32[320,128]{1,0:T(8,128)S(1)} %broadcast_select_fusion.3.refs_4_), channel_id=1, source_target_pairs={{0,8},{1,9},{2,10},{3,11},{4,12},{5,13},{6,14},{7,15},{8,0},{9,1},... | collective-permute-start | bytes 491528 | tf_op jit(solution)/shard_map/ppermute | solution.py:27
  22.8 15.7 %collective-permute-start.3 = (f32[704,128]{1,0:T(8,128)S(1)}, f32[704,128]{1,0:T(8,128)}, u32[]{:S(2)}, u32[]{:S(2)}) collective-permute-start(f32[704,128]{1,0:T(8,128)S(1)} %pad_maximum_fusion.1), channel_id=1, source_target_pairs={{0,32},{1,33},{2,34},{3,35},{4,36},{5,37},{6,38},{7,39},{8,40},{9,... | collective-permute-start | bytes 1081352 | tf_op jit(solution)/shard_map/ppermute | solution.py:27
  32.1 21.7 %collective-permute-start.11 = (f32[2,320,256]{2,1,0:T(8,128)S(1)}, f32[2,320,256]{2,1,0:T(8,128)S(1)}, u32[]{:S(2)}, u32[]{:S(2)}) collective-permute-start(f32[2,320,256]{2,1,0:T(8,128)S(1)} %get-tuple-element.27), channel_id=1, source_target_pairs={{0,68},{1,69},{2,70},{3,71},{4,64},{5,65},{6,66},{7,67},{8,76},{9,... | collective-permute-start | bytes 1966088 | tf_op jit(solution)/shard_map/ppermute | solution.py:27
  32.2 17.8 %collective-permute-start.13 = (f32[2,320,256]{2,1,0:T(8,128)S(1)}, f32[2,320,256]{2,1,0:T(8,128)S(1)}, u32[]{:S(2)}, u32[]{:S(2)}) collective-permute-start(f32[2,320,256]{2,1,0:T(8,128)S(1)} %get-tuple-element.29), channel_id=1, source_target_pairs={{0,64},{1,65},{2,66},{3,67},{4,68},{5,69},{6,70},{7,71},{8,72},{9,... | collective-permute-start | bytes 1966088 | tf_op jit(solution)/shard_map/ppermute | solution.py:27
  38.6 2.2 %collective-permute-start.10 = (f32[704,128]{1,0:T(8,128)S(1)}, f32[704,128]{1,0:T(8,128)S(1)}, u32[]{:S(2)}, u32[]{:S(2)}) collective-permute-start(f32[704,128]{1,0:T(8,128)S(1)} %broadcast_select_fusion.refs_5_), channel_id=1, source_target_pairs={{0,8},{1,9},{2,10},{3,11},{4,12},{5,13},{6,14},{7,15},{8,0},{9,1},... | collective-permute-start | bytes 1081352 | tf_op jit(solution)/shard_map/ppermute | solution.py:27
  42.4 11.8 %collective-permute-start.20 = (f32[2,192,256]{2,1,0:T(8,128)S(1)}, f32[2,192,256]{2,1,0:T(8,128)S(1)}, u32[]{:S(2)}, u32[]{:S(2)}) collective-permute-start(f32[2,192,256]{2,1,0:T(8,128)S(1)} %get-tuple-element.34), channel_id=1, source_target_pairs={{0,1},{1,0},{2,3},{3,2},{4,5},{5,4},{6,7},{7,6},{8,9},{9,8},{10,11... | collective-permute-start | bytes 1179656 | tf_op jit(solution)/shard_map/ppermute | solution.py:27
  45.1 13.2 %collective-permute-start.18 = (f32[2,192,256]{2,1,0:T(8,128)S(1)}, f32[2,192,256]{2,1,0:T(8,128)S(1)}, u32[]{:S(2)}, u32[]{:S(2)}) collective-permute-start(f32[2,192,256]{2,1,0:T(8,128)S(1)} %get-tuple-element.32), channel_id=1, source_target_pairs={{0,3},{1,2},{2,1},{3,0},{4,7},{5,6},{6,5},{7,4},{8,11},{9,10},{10,... | collective-permute-start | bytes 1179656 | tf_op jit(solution)/shard_map/ppermute | solution.py:27
  50.0 36.1 %collective-permute-start.14 = (f32[4,320,256]{2,1,0:T(8,128)S(1)}, f32[4,320,256]{2,1,0:T(8,128)S(1)}, u32[]{:S(2)}, u32[]{:S(2)}) collective-permute-start(f32[4,320,256]{2,1,0:T(8,128)S(1)} %shard_map.59), channel_id=1, source_target_pairs={{0,68},{1,69},{2,70},{3,71},{4,64},{5,65},{6,66},{7,67},{8,76},{9,... | collective-permute-start | bytes 3932168 | tf_op jit(solution)/shard_map/ppermute | solution.py:27
  53.9 32.2 %collective-permute-start.12 = (f32[4,320,256]{2,1,0:T(8,128)S(1)}, f32[4,320,256]{2,1,0:T(8,128)S(1)}, u32[]{:S(2)}, u32[]{:S(2)}) collective-permute-start(f32[4,320,256]{2,1,0:T(8,128)S(1)} %shard_map.58), channel_id=1, source_target_pairs={{0,64},{1,65},{2,66},{3,67},{4,68},{5,69},{6,70},{7,71},{8,72},{9,... | collective-permute-start | bytes 3932168 | tf_op jit(solution)/shard_map/ppermute | solution.py:27
  54.3 22.3 %collective-permute-start.21 = (f32[4,192,256]{2,1,0:T(8,128)S(1)}, f32[4,192,256]{2,1,0:T(8,128)S(1)}, u32[]{:S(2)}, u32[]{:S(2)}) collective-permute-start(f32[4,192,256]{2,1,0:T(8,128)S(1)} %shard_map.61), channel_id=1, source_target_pairs={{0,3},{1,2},{2,1},{3,0},{4,7},{5,6},{6,5},{7,4},{8,11},{9,10},{10,... | collective-permute-start | bytes 2359304 | tf_op jit(solution)/shard_map/ppermute | solution.py:27
  58.3 19.8 %collective-permute-start.19 = (f32[4,192,256]{2,1,0:T(8,128)S(1)}, f32[4,192,256]{2,1,0:T(8,128)S(1)}, u32[]{:S(2)}, u32[]{:S(2)}) collective-permute-start(f32[4,192,256]{2,1,0:T(8,128)S(1)} %shard_map.60), channel_id=1, source_target_pairs={{0,1},{1,0},{2,3},{3,2},{4,5},{5,4},{6,7},{7,6},{8,9},{9,8},{10,11... | collective-permute-start | bytes 2359304 | tf_op jit(solution)/shard_map/ppermute | solution.py:27
  78.2 11.1 %collective-permute-start.22 = (f32[192,256]{1,0:T(8,128)S(1)}, f32[192,256]{1,0:T(8,128)S(1)}, u32[]{:S(2)}, u32[]{:S(2)}) collective-permute-start(f32[192,256]{1,0:T(8,128)S(1)} %get-tuple-element.38), channel_id=1, source_target_pairs={{0,4},{1,5},{2,6},{3,7},{4,0},{5,1},{6,2},{7,3},{8,12},{9,13},{10,... | collective-permute-start | bytes 589832 | tf_op jit(solution)/shard_map/ppermute | solution.py:27
  81.9 11.3 %collective-permute-start.24 = (f32[192,256]{1,0:T(8,128)S(1)}, f32[192,256]{1,0:T(8,128)S(1)}, u32[]{:S(2)}, u32[]{:S(2)}) collective-permute-start(f32[192,256]{1,0:T(8,128)S(1)} %get-tuple-element.39), channel_id=1, source_target_pairs={{0,68},{1,69},{2,70},{3,71},{4,64},{5,65},{6,66},{7,67},{8,76},{9,... | collective-permute-start | bytes 589832 | tf_op jit(solution)/shard_map/ppermute | solution.py:27
  86.1 7.8 %collective-permute-start.23 = (f32[192,256]{1,0:T(8,128)S(1)}, f32[192,256]{1,0:T(8,128)S(1)}, u32[]{:S(2)}, u32[]{:S(2)}) collective-permute-start(f32[192,256]{1,0:T(8,128)S(1)} %get-tuple-element.40), channel_id=1, source_target_pairs={{0,64},{1,65},{2,66},{3,67},{4,68},{5,69},{6,70},{7,71},{8,72},{9,... | collective-permute-start | bytes 589832 | tf_op jit(solution)/shard_map/ppermute | solution.py:27
  86.3 12.2 %collective-permute-start.15 = (f32[320,256]{1,0:T(8,128)S(1)}, f32[320,256]{1,0:T(8,128)S(1)}, u32[]{:S(2)}, u32[]{:S(2)}) collective-permute-start(f32[320,256]{1,0:T(8,128)S(1)} %get-tuple-element.35), channel_id=1, source_target_pairs={{0,2},{1,3},{2,0},{3,1},{4,6},{5,7},{6,4},{7,5},{8,10},{9,11},{10,... | collective-permute-start | bytes 983048 | tf_op jit(solution)/shard_map/ppermute | solution.py:27
  88.5 16.2 %collective-permute-start.17 = (f32[320,256]{1,0:T(8,128)S(1)}, f32[320,256]{1,0:T(8,128)S(1)}, u32[]{:S(2)}, u32[]{:S(2)}) collective-permute-start(f32[320,256]{1,0:T(8,128)S(1)} %get-tuple-element.36), channel_id=1, source_target_pairs={{0,3},{1,2},{2,1},{3,0},{4,7},{5,6},{6,5},{7,4},{8,11},{9,10},{10,... | collective-permute-start | bytes 983048 | tf_op jit(solution)/shard_map/ppermute | solution.py:27
  89.3 15.3 %collective-permute-start.16 = (f32[320,256]{1,0:T(8,128)S(1)}, f32[320,256]{1,0:T(8,128)S(1)}, u32[]{:S(2)}, u32[]{:S(2)}) collective-permute-start(f32[320,256]{1,0:T(8,128)S(1)} %get-tuple-element.37), channel_id=1, source_target_pairs={{0,1},{1,0},{2,3},{3,2},{4,5},{5,4},{6,7},{7,6},{8,9},{9,8},{10,11... | collective-permute-start | bytes 983048 | tf_op jit(solution)/shard_map/ppermute | solution.py:27
  (7 other events, 27.4 us)

commit v4 on v3

v4 whole, which is shorter than its diff:
```python
import jax
import jax.numpy as jnp
from jax import lax
from jax.experimental import pallas as pl
from jax.experimental.pallas import tpu as pltpu
from jax.sharding import Mesh
from jax.sharding import PartitionSpec as P

TILE = 512
WIDTH = 256
AXES = ("yl", "x", "c", "yh", "z")
SIZES = (2, 4, 2, 2, 4)
ROWS = {"A": 320, "B": 192}
COST = {"first": 1, "second": 1, "join_a": 1, "join_b": 1, "last": 1}
SMEM = pl.BlockSpec(memory_space=pltpu.SMEM)
VMEM = pl.BlockSpec(memory_space=pltpu.VMEM)


def permute(value, yl=0, x=0, c=0, yh=0, z=0):
    bits = (((yl * 4 + x) * 2 + c) * 2 + yh) * 4 + z
    return lax.ppermute(value, AXES, [(n, n ^ bits) for n in range(128)])


def along_y(value, bits):
    return permute(value, yl=bits % 2, yh=bits // 2)


def along_z(value, bits):
    return permute(value, z=bits)


def settings(cost):
    return dict(
        compiler_params=pltpu.CompilerParams(vmem_limit_bytes=16 * 2**20),
        cost_estimate=pl.CostEstimate(flops=1, bytes_accessed=COST[cost], transcendentals=0),
    )


def product_kernel(rows, plan, spots, left_mask, right_mask, result_mask, *rest):
    pieces, right, outs, (hi_ref, lo_ref, tiles, sems) = rest[:4], rest[4], rest[5:-4], rest[-4:]
    yl, x, c, yh, z = (spots[n] for n in range(5))
    k = (yh * 4 + z) * 2 + yl
    first = (x * 2 + c) * 4
    near = 1 - lax.rem(x, 2)

    def used(dy, chunk):
        i = lax.rem(yl + dy % 2, 2)
        j = first + lax.div(chunk, 2)
        return left_mask[i, k] * right_mask[k, j] * result_mask[i, j] > 0

    def fetch(n, chunk):
        where = pl.ds(pl.multiple_of(chunk * WIDTH, WIDTH), WIDTH)
        return pltpu.make_async_copy(right.at[:, where], tiles.at[n], sems.at[n])

    groups = [
        (n, lax.rem(yh + high, 2) * 4 + jnp.bitwise_xor(z, dz), [dy for dy in rows if dy // 2 == high], dz)
        for n, (high, dz) in enumerate((high, dz) for high in range(2) for dz in range(4))
    ]

    def wanted(chunk, turns):
        flag = used(turns[0], chunk)
        for dy in turns[1:]:
            flag = jnp.logical_or(flag, used(dy, chunk))
        return flag

    for n, chunk, turns, _ in groups:

        @pl.when(wanted(chunk, turns))
        def _():
            fetch(n, chunk).start()

    for piece, chip, core in zip(pieces, (near, 1 - near, near, 1 - near), (c, c, 1 - c, 1 - c)):
        value = piece[...]
        hi = value.astype(jnp.bfloat16)
        where = pl.ds(pl.multiple_of(chip * 256 + core * 128, 128), 128)
        hi_ref[:, where] = hi
        lo_ref[:, where] = (value - hi.astype(jnp.float32)).astype(jnp.bfloat16)
    for n, chunk, turns, dz in groups:

        @pl.when(wanted(chunk, turns))
        def _():
            fetch(n, chunk).wait()

        for dy in turns:
            start, stop = rows[dy]

            @pl.when(used(dy, chunk))
            def _():
                tile = tiles[n]
                hi = tile.astype(jnp.bfloat16)
                lo = (tile - hi.astype(jnp.float32)).astype(jnp.bfloat16)
                total = jnp.dot(hi_ref[start:stop], hi, preferred_element_type=jnp.float32)
                total += jnp.dot(hi_ref[start:stop], lo, preferred_element_type=jnp.float32)
                total += jnp.dot(lo_ref[start:stop], hi, preferred_element_type=jnp.float32)
                done = 0
                for half, out, slot in plan[dy, dz]:
                    outs[out][slot] = total[done : done + ROWS[half]]
                    done += ROWS[half]

            @pl.when(jnp.logical_not(used(dy, chunk)))
            def _():
                for half, out, slot in plan[dy, dz]:
                    outs[out][slot] = jnp.zeros((ROWS[half], WIDTH), jnp.float32)


def product(rows, names, spots, masks, pieces, right, cost):
    plan = {
        (dy, dz): [
            (half, n, blocks.index((half, dy, dz)))
            for half in "AB"
            for n, blocks in enumerate(names.values())
            if (half, dy, dz) in blocks
        ]
        for dy in rows
        for dz in range(4)
    }
    outs = pl.pallas_call(
        lambda *refs: product_kernel(rows, plan, *refs),
        out_shape=[jax.ShapeDtypeStruct((len(b), ROWS[b[0][0]], WIDTH), jnp.float32) for b in names.values()],
        in_specs=[SMEM] * 4 + [VMEM] * 4 + [pl.BlockSpec(memory_space=pltpu.HBM)],
        out_specs=[VMEM] * len(names),
        scratch_shapes=[pltpu.VMEM((pieces[0].shape[0], TILE), jnp.bfloat16)] * 2
        + [pltpu.VMEM((8, TILE, WIDTH), jnp.float32), pltpu.SemaphoreType.DMA((8,))],
        **settings(cost),
    )(spots, *masks, *pieces, right)
    return dict(zip(names, outs))


def join(value, first, arrived, cost):
    def kernel(value_ref, arrived_ref, out_ref):
        del value_ref
        for n in range(arrived.shape[0]):
            out_ref[first + n] += arrived_ref[n]

    return pl.pallas_call(
        kernel,
        out_shape=jax.ShapeDtypeStruct(value.shape, value.dtype),
        in_specs=[VMEM] * 2,
        out_specs=VMEM,
        input_output_aliases={0: 0},
        **settings(cost),
    )(value, arrived)


def total(top, bottom):
    def kernel(*refs):
        out_ref = refs[-1]
        out_ref[: ROWS["A"]] = sum(ref[...] for ref in refs[1 : len(top)]) + refs[0][...]
        out_ref[ROWS["A"] :] = sum(ref[...] for ref in refs[len(top) + 1 : -1]) + refs[len(top)][...]

    return pl.pallas_call(
        kernel,
        out_shape=jax.ShapeDtypeStruct((TILE, WIDTH), jnp.float32),
        in_specs=[VMEM] * (len(top) + len(bottom)),
        **settings("last"),
    )(*top, *bottom)


def gather(value, here):
    between, beside, across = (permute(value, x=bits) for bits in (1, 3, 2))
    near = jnp.where(here, between, beside)
    far = jnp.where(here, value, across)
    return near, far


def both_cores(near, far):
    return near, far, permute(near, c=1), permute(far, c=1)


def shards(left, right, left_mask, right_mask, result_mask):
    yl, x, c, yh, z = (lax.axis_index(a) for a in AXES)
    spots = jnp.stack([yl, x, c, yh, z]).astype(jnp.int32)
    masks = (left_mask, right_mask, result_mask)
    here = x // 2 == yl
    rows_a = ROWS["A"]

    left_a, left_b = lax.optimization_barrier((left[:rows_a], left[rows_a:]))
    own = gather(left_a, here)
    other_row = permute(left, yl=1)
    rest = gather(lax.optimization_barrier(jnp.concatenate([left_b, other_row])), here)
    p = product(
        {0: (0, rows_a), 2: (0, rows_a)},
        {
            "via1": [("A", 2, 0), ("A", 2, 1)],
            "via3": [("A", 2, 2), ("A", 2, 3)],
            "own": [("A", 0, d) for d in range(4)],
        },
        spots,
        masks,
        both_cores(*own),
        right,
        "first",
    )
    from1 = along_y(p["via1"], 1)
    from3 = along_y(p["via3"], 3)
    rest, a_own = lax.optimization_barrier((rest, p["own"]))
    own_rows, other_rows = (0, ROWS["B"]), (ROWS["B"], ROWS["B"] + TILE)
    q = product(
        {1: other_rows, 3: other_rows, 0: own_rows, 2: own_rows},
        {
            "a1": [("A", 1, d) for d in range(4)],
            "a3": [("A", 3, d) for d in range(4)],
            "via1": [("B", 0, 2), ("B", 1, 2)],
            "via3": [("B", 2, 2), ("B", 3, 2)],
            "b1": [("B", d, 1) for d in range(4)],
            "b3": [("B", d, 3) for d in range(4)],
            "own": [("B", d, 0) for d in range(4)],
        },
        spots,
        masks,
        both_cores(*rest),
        right,
        "second",
    )
    top_parts = (
        along_y(join(q["a1"], 2, from3, "join_a"), 1),
        along_y(join(q["a3"], 0, from1, "join_a"), 3),
    )
    from1 = along_z(q["via1"], 1)
    from3 = along_z(q["via3"], 3)
    bottom_parts = (
        along_z(join(q["b1"], 2, from3, "join_b"), 1),
        along_z(join(q["b3"], 0, from1, "join_b"), 3),
    )
    a = [a_own[d] + top_parts[0][d] + top_parts[1][d] for d in range(4)]
    _, b_own = lax.optimization_barrier((a[2], q["own"]))
    b = [b_own[d] + bottom_parts[0][d] + bottom_parts[1][d] for d in range(4)]
    return total(
        [a[0], along_z(a[2], 2), along_z(a[1], 1), along_z(a[3], 3)],
        [b[0], along_y(b[2], 2), along_y(b[1], 1), along_y(b[3], 3)],
    )


def solution(mesh):
    torus = Mesh(mesh.devices.reshape(SIZES), AXES)
    in_specs = (
        P("yl", ("yh", "z", "x", "c")),
        P(("yh", "z", "yl"), ("x", "c")),
        P(),
        P(),
        P(),
    )
    return jax.shard_map(
        shards, mesh=torus, in_specs=in_specs, out_specs=P("yl", ("x", "c", "yh", "z")), check_vma=False
    )
```

time: 106 us -> 94.1 us (0.89)
  starting transfers between devices: 49.8 us -> 31.5 us
  waiting for transfers between devices: 41.2 us -> 52 us
  local copies, waits for them, and re-layouts: 7.04 us -> 4.15 us
  other arithmetic: 3.41 us -> 0.55 us
    ppermute x25, starting transfers between devices: 49.8 us -> 31.5 us  [permute(): return lax.ppermute(value, AXES, [(n, n ^ bits) for n in range(128)])]
    ppermute x25, waiting for transfers between devices: 41.2 us -> 52 us  [permute(): return lax.ppermute(value, AXES, [(n, n ^ bits) for n in range(128)])]
    unnamed x12 -> x10, local copies, waits for them, and re-layouts: 5.13 us -> 2.2 us
  transfers between devices with their start and end apart: 25 -> 25, of which waited for: 11 -> 16; matrix products, arithmetic and copies ran while one was open for 3% -> 1% of each run, Pallas kernels for 4% -> 4%
where the time goes in v4:
time: 94.1 us; the launch traced here: 93.2 us
  waiting for transfers between devices  52 us (55%)
  starting transfers between devices  31.5 us (33%)
  Pallas kernels  4.84 us (5%)
  local copies, waits for them, and re-layouts  4.15 us (4%)
    ppermute x25, waiting for transfers between devices, permute(): return lax.ppermute(value, AXES, [(n, n ^ bits) for n in range(128)])  52 us
    ppermute x25, starting transfers between devices, permute(): return lax.ppermute(value, AXES, [(n, n ^ bits) for n in range(128)])  31.5 us
    pallas_call x2, Pallas kernels, product(): pl.pallas_call(lambda *refs: product_kernel(rows, plan, *refs), out_shape...  3.7 us
    unnamed x10, local copies, waits for them, and re-layouts  2.2 us
  transfers between devices with their start and end apart: 25, of which 16 were waited for; matrix products, arithmetic and copies ran while one was open for 1% of the time, Pallas kernels for 4%

profile of v4, /device:TPU:0, one launch (start us, length us, event | category | flops | bytes accessed | tf_op | source)
XLA Modules:
  0.0 93.2 jit_solution(16132997707016992458)
XLA Ops:
  1.9 3.2 %collective-permute-start.6 = (f32[320,128]{1,0:T(8,128)S(1)}, f32[320,128]{1,0:T(8,128)S(1)}, u32[]{:S(2)}, u32[]{:S(2)}) collective-permute-start(f32[320,128]{1,0:T(8,128)S(1)} %slice.78), channel_id=1, source_target_pairs={{0,32},{1,33},{2,34},{3,35},{4,36},{5,37},{6,38},{7,39},{8,40},{9,... | collective-permute-start | bytes 491528 | tf_op jit(solution)/shard_map/ppermute | solution.py:21
  5.1 1.6 %collective-permute-start = (f32[512,128]{1,0:T(8,128)}, f32[512,128]{1,0:T(8,128)S(1)}, u32[]{:S(2)}, u32[]{:S(2)}) collective-permute-start(f32[512,128]{1,0:T(8,128)} %param.5), channel_id=1, source_target_pairs={{0,64},{1,65},{2,66},{3,67},{4,68},{5,69},{6,70},{7,71},{8,72},{9,... | collective-permute-start | bytes 786440 | tf_op jit(solution)/shard_map/ppermute | solution.py:21
  7.8 1.9 %collective-permute-done.6 = f32[320,128]{1,0:T(8,128)S(1)} collective-permute-done((f32[320,128]{1,0:T(8,128)S(1)}, f32[320,128]{1,0:T(8,128)S(1)}, u32[]{:S(2)}, u32[]{:S(2)}) %collective-permute-start.6) | collective-permute-done | bytes 163872 | tf_op jit(solution)/shard_map/ppermute | solution.py:21
  9.8 3.2 %collective-permute-done = f32[512,128]{1,0:T(8,128)S(1)} collective-permute-done((f32[512,128]{1,0:T(8,128)}, f32[512,128]{1,0:T(8,128)S(1)}, u32[]{:S(2)}, u32[]{:S(2)}) %collective-permute-start) | collective-permute-done | bytes 262176 | tf_op jit(solution)/shard_map/ppermute | solution.py:21
  14.3 2.4 %collective-permute-start.2 = (f32[704,128]{1,0:T(8,128)S(1)}, f32[704,128]{1,0:T(8,128)S(1)}, u32[]{:S(2)}, u32[]{:S(2)}) collective-permute-start(f32[704,128]{1,0:T(8,128)S(1)} %pad_maximum_fusion), channel_id=1, source_target_pairs={{0,48},{1,49},{2,50},{3,51},{4,52},{5,53},{6,54},{7,55},{8,56},{9,... | collective-permute-start | bytes 1081352 | tf_op jit(solution)/shard_map/ppermute | solution.py:21
  17.0 2.2 %copy-done = f32[512,2048]{1,0:T(8,128)S(1)} copy-done((f32[512,2048]{1,0:T(8,128)S(1)}, f32[512,2048]{1,0:T(8,128)}, u32[]{:S(2)}) %copy-start) | copy-done | bytes 4194328
  19.2 1.4 %shard_map.55 = (f32[2,320,256]{2,1,0:T(8,128)S(1)}, f32[2,320,256]{2,1,0:T(8,128)S(1)}, f32[4,320,256]{2,1,0:T(8,128)S(1)}) custom-call(s32[5]{0:T(128)S(1)} %stack.23.refs_0_, s32[2,16]{1,0:T(2,128)S(1)} %copy-done.3, s32[16,32]{1,0:T(8,128)S(1)} %copy-done.2, s32[2,32]{1,0:T(2,128)S(1)} %copy-done.4, f32[320,128]{1,0:T(8,128)S(1)} %broadcast_select_fusion.3.refs_4_, ...), custom_call_target="tpu_custom_call" | custom-call | flops 1 | bytes 1 | tf_op jit(solution)/shard_map/pallas_call | solution.py:117
  20.6 3.1 %collective-permute-start.11 = (f32[2,320,256]{2,1,0:T(8,128)S(1)}, f32[2,320,256]{2,1,0:T(8,128)S(1)}, u32[]{:S(2)}, u32[]{:S(2)}) collective-permute-start(f32[2,320,256]{2,1,0:T(8,128)S(1)} %get-tuple-element.28), channel_id=1, source_target_pairs={{0,68},{1,69},{2,70},{3,71},{4,64},{5,65},{6,66},{7,67},{8,76},{9,... | collective-permute-start | bytes 1966088 | tf_op jit(solution)/shard_map/ppermute | solution.py:21
  23.8 2.2 %collective-permute-done.3 = f32[704,128]{1,0:T(8,128)S(1)} collective-permute-done((f32[704,128]{1,0:T(8,128)S(1)}, f32[704,128]{1,0:T(8,128)S(1)}, u32[]{:S(2)}, u32[]{:S(2)}) %collective-permute-start.3) | collective-permute-done | bytes 360480 | tf_op jit(solution)/shard_map/ppermute | solution.py:21
  26.1 5.3 %collective-permute-done.2 = f32[704,128]{1,0:T(8,128)S(1)} collective-permute-done((f32[704,128]{1,0:T(8,128)S(1)}, f32[704,128]{1,0:T(8,128)S(1)}, u32[]{:S(2)}, u32[]{:S(2)}) %collective-permute-start.2) | collective-permute-done | bytes 360480 | tf_op jit(solution)/shard_map/ppermute | solution.py:21
  33.7 2.3 %shard_map.56 = (f32[4,320,256]{2,1,0:T(8,128)S(1)}, f32[4,320,256]{2,1,0:T(8,128)S(1)}, f32[2,192,256]{2,1,0:T(8,128)S(1)}, f32[2,192,256]{2,1,0:T(8,128)S(1)},...) custom-call(s32[5]{0:T(128)S(1)} %stack.23.refs_0_, s32[2,16]{1,0:T(2,128)S(1)} %copy-done.3, ...), custom_call_target="tpu_custom_call" | custom-call | flops 1 | bytes 1 | tf_op jit(solution)/shard_map/pallas_call | solution.py:117
  35.9 4.0 %collective-permute-done.13.arrived_ref = f32[2,320,256]{2,1,0:T(8,128)S(1)} collective-permute-done((f32[2,320,256]{2,1,0:T(8,128)S(1)}, f32[2,320,256]{2,1,0:T(8,128)S(1)}, u32[]{:S(2)}, u32[]{:S(2)}) %collective-permute-start.13) | collective-permute-done | bytes 655392 | tf_op jit(solution)/shard_map/ppermute | solution.py:21
  41.7 2.2 %collective-permute-start.20 = (f32[2,192,256]{2,1,0:T(8,128)S(1)}, f32[2,192,256]{2,1,0:T(8,128)S(1)}, u32[]{:S(2)}, u32[]{:S(2)}) collective-permute-start(f32[2,192,256]{2,1,0:T(8,128)S(1)} %get-tuple-element.36), channel_id=1, source_target_pairs={{0,1},{1,0},{2,3},{3,2},{4,5},{5,4},{6,7},{7,6},{8,9},{9,8},{10,11... | collective-permute-start | bytes 1179656 | tf_op jit(solution)/shard_map/ppermute | solution.py:21
  43.9 1.7 %collective-permute-start.18 = (f32[2,192,256]{2,1,0:T(8,128)S(1)}, f32[2,192,256]{2,1,0:T(8,128)S(1)}, u32[]{:S(2)}, u32[]{:S(2)}) collective-permute-start(f32[2,192,256]{2,1,0:T(8,128)S(1)} %get-tuple-element.34), channel_id=1, source_target_pairs={{0,3},{1,2},{2,1},{3,0},{4,7},{5,6},{6,5},{7,4},{8,11},{9,10},{10,... | collective-permute-start | bytes 1179656 | tf_op jit(solution)/shard_map/ppermute | solution.py:21
  45.7 7.0 %collective-permute-done.20.arrived_ref = f32[2,192,256]{2,1,0:T(8,128)S(1)} collective-permute-done((f32[2,192,256]{2,1,0:T(8,128)S(1)}, f32[2,192,256]{2,1,0:T(8,128)S(1)}, u32[]{:S(2)}, u32[]{:S(2)}) %collective-permute-start.20) | collective-permute-done | bytes 393248 | tf_op jit(solution)/shard_map/ppermute | solution.py:21
  52.7 3.6 %collective-permute-start.21 = (f32[4,192,256]{2,1,0:T(8,128)S(1)}, f32[4,192,256]{2,1,0:T(8,128)S(1)}, u32[]{:S(2)}, u32[]{:S(2)}) collective-permute-start(f32[4,192,256]{2,1,0:T(8,128)S(1)} %shard_map.60), channel_id=1, source_target_pairs={{0,3},{1,2},{2,1},{3,0},{4,7},{5,6},{6,5},{7,4},{8,11},{9,10},{10,... | collective-permute-start | bytes 2359304 | tf_op jit(solution)/shard_map/ppermute | solution.py:21
  56.4 14.4 %collective-permute-done.14 = f32[4,320,256]{2,1,0:T(8,128)S(1)} collective-permute-done((f32[4,320,256]{2,1,0:T(8,128)S(1)}, f32[4,320,256]{2,1,0:T(8,128)S(1)}, u32[]{:S(2)}, u32[]{:S(2)}) %collective-permute-start.14) | collective-permute-done | bytes 1310752 | tf_op jit(solution)/shard_map/ppermute | solution.py:21
  72.6 1.6 %collective-permute-done.19 = f32[4,192,256]{2,1,0:T(8,128)S(1)} collective-permute-done((f32[4,192,256]{2,1,0:T(8,128)S(1)}, f32[4,192,256]{2,1,0:T(8,128)S(1)}, u32[]{:S(2)}, u32[]{:S(2)}) %collective-permute-start.19) | collective-permute-done | bytes 786464 | tf_op jit(solution)/shard_map/ppermute | solution.py:21
  74.4 3.1 %collective-permute-start.17 = (f32[320,256]{1,0:T(8,128)S(1)}, f32[320,256]{1,0:T(8,128)S(1)}, u32[]{:S(2)}, u32[]{:S(2)}) collective-permute-start(f32[320,256]{1,0:T(8,128)S(1)} %get-tuple-element.37), channel_id=1, source_target_pairs={{0,3},{1,2},{2,1},{3,0},{4,7},{5,6},{6,5},{7,4},{8,11},{9,10},{10,... | collective-permute-start | bytes 983048 | tf_op jit(solution)/shard_map/ppermute | solution.py:21
  77.6 1.6 %collective-permute-start.15 = (f32[320,256]{1,0:T(8,128)S(1)}, f32[320,256]{1,0:T(8,128)S(1)}, u32[]{:S(2)}, u32[]{:S(2)}) collective-permute-start(f32[320,256]{1,0:T(8,128)S(1)} %get-tuple-element.39), channel_id=1, source_target_pairs={{0,2},{1,3},{2,0},{3,1},{4,6},{5,7},{6,4},{7,5},{8,10},{9,11},{10,... | collective-permute-start | bytes 983048 | tf_op jit(solution)/shard_map/ppermute | solution.py:21
  81.3 2.5 %collective-permute-start.22 = (f32[192,256]{1,0:T(8,128)S(1)}, f32[192,256]{1,0:T(8,128)S(1)}, u32[]{:S(2)}, u32[]{:S(2)}) collective-permute-start(f32[192,256]{1,0:T(8,128)S(1)} %get-tuple-element.43), channel_id=1, source_target_pairs={{0,4},{1,5},{2,6},{3,7},{4,0},{5,1},{6,2},{7,3},{8,12},{9,13},{10,... | collective-permute-start | bytes 589832 | tf_op jit(solution)/shard_map/ppermute | solution.py:21
  83.8 2.2 %collective-permute-done.23.refs_6_ = f32[192,256]{1,0:T(8,128)S(1)} collective-permute-done((f32[192,256]{1,0:T(8,128)S(1)}, f32[192,256]{1,0:T(8,128)S(1)}, u32[]{:S(2)}, u32[]{:S(2)}) %collective-permute-start.23) | collective-permute-done | bytes 196640 | tf_op jit(solution)/shard_map/ppermute | solution.py:21
  86.1 3.5 %collective-permute-done.22.refs_5_ = f32[192,256]{1,0:T(8,128)S(1)} collective-permute-done((f32[192,256]{1,0:T(8,128)S(1)}, f32[192,256]{1,0:T(8,128)S(1)}, u32[]{:S(2)}, u32[]{:S(2)}) %collective-permute-start.22) | collective-permute-done | bytes 196640 | tf_op jit(solution)/shard_map/ppermute | solution.py:21
  89.6 2.7 %collective-permute-done.15.refs_1_ = f32[320,256]{1,0:T(8,128)S(1)} collective-permute-done((f32[320,256]{1,0:T(8,128)S(1)}, f32[320,256]{1,0:T(8,128)S(1)}, u32[]{:S(2)}, u32[]{:S(2)}) %collective-permute-start.15) | collective-permute-done | bytes 327712 | tf_op jit(solution)/shard_map/ppermute | solution.py:21
  (53 shorter events, 14.1 us)
Async XLA Ops:
  1.9 7.8 %collective-permute-start.6 = (f32[320,128]{1,0:T(8,128)S(1)}, f32[320,128]{1,0:T(8,128)S(1)}, u32[]{:S(2)}, u32[]{:S(2)}) collective-permute-start(f32[320,128]{1,0:T(8,128)S(1)} %slice.78), channel_id=1, source_target_pairs={{0,32},{1,33},{2,34},{3,35},{4,36},{5,37},{6,38},{7,39},{8,40},{9,... | collective-permute-start | bytes 491528 | tf_op jit(solution)/shard_map/ppermute | solution.py:21
  5.1 8.0 %collective-permute-start = (f32[512,128]{1,0:T(8,128)}, f32[512,128]{1,0:T(8,128)S(1)}, u32[]{:S(2)}, u32[]{:S(2)}) collective-permute-start(f32[512,128]{1,0:T(8,128)} %param.5), channel_id=1, source_target_pairs={{0,64},{1,65},{2,66},{3,67},{4,68},{5,69},{6,70},{7,71},{8,72},{9,... | collective-permute-start | bytes 786440 | tf_op jit(solution)/shard_map/ppermute | solution.py:21
  6.6 7.3 %collective-permute-start.5 = (f32[320,128]{1,0:T(8,128)S(1)}, f32[320,128]{1,0:T(8,128)S(1)}, u32[]{:S(2)}, u32[]{:S(2)}) collective-permute-start(f32[320,128]{1,0:T(8,128)S(1)} %slice.78), channel_id=1, source_target_pairs={{0,48},{1,49},{2,50},{3,51},{4,52},{5,53},{6,54},{7,55},{8,56},{9,... | collective-permute-start | bytes 491528 | tf_op jit(solution)/shard_map/ppermute | solution.py:21
  7.8 6.2 %collective-permute-start.4 = (f32[320,128]{1,0:T(8,128)S(1)}, f32[320,128]{1,0:T(8,128)S(1)}, u32[]{:S(2)}, u32[]{:S(2)}) collective-permute-start(f32[320,128]{1,0:T(8,128)S(1)} %slice.78), channel_id=1, source_target_pairs={{0,16},{1,17},{2,18},{3,19},{4,20},{5,21},{6,22},{7,23},{8,24},{9,... | collective-permute-start | bytes 491528 | tf_op jit(solution)/shard_map/ppermute | solution.py:21
  9.7 7.2 %collective-permute-start.8 = (f32[320,128]{1,0:T(8,128)S(1)}, f32[320,128]{1,0:T(8,128)S(1)}, u32[]{:S(2)}, u32[]{:S(2)}) collective-permute-start(f32[320,128]{1,0:T(8,128)S(1)} %broadcast_select_fusion.2.refs_5_), channel_id=1, source_target_pairs={{0,8},{1,9},{2,10},{3,11},{4,12},{5,13},{6,14},{7,15},{8,0},{9,1},... | collective-permute-start | bytes 491528 | tf_op jit(solution)/shard_map/ppermute | solution.py:21
  13.1 13.0 %collective-permute-start.3 = (f32[704,128]{1,0:T(8,128)S(1)}, f32[704,128]{1,0:T(8,128)S(1)}, u32[]{:S(2)}, u32[]{:S(2)}) collective-permute-start(f32[704,128]{1,0:T(8,128)S(1)} %pad_maximum_fusion), channel_id=1, source_target_pairs={{0,32},{1,33},{2,34},{3,35},{4,36},{5,37},{6,38},{7,39},{8,40},{9,... | collective-permute-start | bytes 1081352 | tf_op jit(solution)/shard_map/ppermute | solution.py:21
  14.0 3.0 %collective-permute-start.7 = (f32[320,128]{1,0:T(8,128)S(1)}, f32[320,128]{1,0:T(8,128)S(1)}, u32[]{:S(2)}, u32[]{:S(2)}) collective-permute-start(f32[320,128]{1,0:T(8,128)S(1)} %broadcast_select_fusion.3.refs_4_), channel_id=1, source_target_pairs={{0,8},{1,9},{2,10},{3,11},{4,12},{5,13},{6,14},{7,15},{8,0},{9,1},... | collective-permute-start | bytes 491528 | tf_op jit(solution)/shard_map/ppermute | solution.py:21
  14.3 17.1 %collective-permute-start.2 = (f32[704,128]{1,0:T(8,128)S(1)}, f32[704,128]{1,0:T(8,128)S(1)}, u32[]{:S(2)}, u32[]{:S(2)}) collective-permute-start(f32[704,128]{1,0:T(8,128)S(1)} %pad_maximum_fusion), channel_id=1, source_target_pairs={{0,48},{1,49},{2,50},{3,51},{4,52},{5,53},{6,54},{7,55},{8,56},{9,... | collective-permute-start | bytes 1081352 | tf_op jit(solution)/shard_map/ppermute | solution.py:21
  16.6 14.7 %collective-permute-start.1 = (f32[704,128]{1,0:T(8,128)S(1)}, f32[704,128]{1,0:T(8,128)S(1)}, u32[]{:S(2)}, u32[]{:S(2)}) collective-permute-start(f32[704,128]{1,0:T(8,128)S(1)} %pad_maximum_fusion), channel_id=1, source_target_pairs={{0,16},{1,17},{2,18},{3,19},{4,20},{5,21},{6,22},{7,23},{8,24},{9,... | collective-permute-start | bytes 1081352 | tf_op jit(solution)/shard_map/ppermute | solution.py:21
  20.6 20.9 %collective-permute-start.11 = (f32[2,320,256]{2,1,0:T(8,128)S(1)}, f32[2,320,256]{2,1,0:T(8,128)S(1)}, u32[]{:S(2)}, u32[]{:S(2)}) collective-permute-start(f32[2,320,256]{2,1,0:T(8,128)S(1)} %get-tuple-element.28), channel_id=1, source_target_pairs={{0,68},{1,69},{2,70},{3,71},{4,64},{5,65},{6,66},{7,67},{8,76},{9,... | collective-permute-start | bytes 1966088 | tf_op jit(solution)/shard_map/ppermute | solution.py:21
  23.7 16.3 %collective-permute-start.13 = (f32[2,320,256]{2,1,0:T(8,128)S(1)}, f32[2,320,256]{2,1,0:T(8,128)S(1)}, u32[]{:S(2)}, u32[]{:S(2)}) collective-permute-start(f32[2,320,256]{2,1,0:T(8,128)S(1)} %get-tuple-element.30), channel_id=1, source_target_pairs={{0,64},{1,65},{2,66},{3,67},{4,68},{5,69},{6,70},{7,71},{8,72},{9,... | collective-permute-start | bytes 1966088 | tf_op jit(solution)/shard_map/ppermute | solution.py:21
  31.5 2.1 %collective-permute-start.10 = (f32[704,128]{1,0:T(8,128)S(1)}, f32[704,128]{1,0:T(8,128)S(1)}, u32[]{:S(2)}, u32[]{:S(2)}) collective-permute-start(f32[704,128]{1,0:T(8,128)S(1)} %broadcast_select_fusion.refs_5_), channel_id=1, source_target_pairs={{0,8},{1,9},{2,10},{3,11},{4,12},{5,13},{6,14},{7,15},{8,0},{9,1},... | collective-permute-start | bytes 1081352 | tf_op jit(solution)/shard_map/ppermute | solution.py:21
  40.0 30.7 %collective-permute-start.14 = (f32[4,320,256]{2,1,0:T(8,128)S(1)}, f32[4,320,256]{2,1,0:T(8,128)S(1)}, u32[]{:S(2)}, u32[]{:S(2)}) collective-permute-start(f32[4,320,256]{2,1,0:T(8,128)S(1)} %shard_map.58), channel_id=1, source_target_pairs={{0,68},{1,69},{2,70},{3,71},{4,64},{5,65},{6,66},{7,67},{8,76},{9,... | collective-permute-start | bytes 3932168 | tf_op jit(solution)/shard_map/ppermute | solution.py:21
  41.5 30.4 %collective-permute-start.12 = (f32[4,320,256]{2,1,0:T(8,128)S(1)}, f32[4,320,256]{2,1,0:T(8,128)S(1)}, u32[]{:S(2)}, u32[]{:S(2)}) collective-permute-start(f32[4,320,256]{2,1,0:T(8,128)S(1)} %shard_map.57), channel_id=1, source_target_pairs={{0,64},{1,65},{2,66},{3,67},{4,68},{5,69},{6,70},{7,71},{8,72},{9,... | collective-permute-start | bytes 3932168 | tf_op jit(solution)/shard_map/ppermute | solution.py:21
  41.7 10.9 %collective-permute-start.20 = (f32[2,192,256]{2,1,0:T(8,128)S(1)}, f32[2,192,256]{2,1,0:T(8,128)S(1)}, u32[]{:S(2)}, u32[]{:S(2)}) collective-permute-start(f32[2,192,256]{2,1,0:T(8,128)S(1)} %get-tuple-element.36), channel_id=1, source_target_pairs={{0,1},{1,0},{2,3},{3,2},{4,5},{5,4},{6,7},{7,6},{8,9},{9,8},{10,11... | collective-permute-start | bytes 1179656 | tf_op jit(solution)/shard_map/ppermute | solution.py:21
  43.9 12.3 %collective-permute-start.18 = (f32[2,192,256]{2,1,0:T(8,128)S(1)}, f32[2,192,256]{2,1,0:T(8,128)S(1)}, u32[]{:S(2)}, u32[]{:S(2)}) collective-permute-start(f32[2,192,256]{2,1,0:T(8,128)S(1)} %get-tuple-element.34), channel_id=1, source_target_pairs={{0,3},{1,2},{2,1},{3,0},{4,7},{5,6},{6,5},{7,4},{8,11},{9,10},{10,... | collective-permute-start | bytes 1179656 | tf_op jit(solution)/shard_map/ppermute | solution.py:21
  52.7 19.9 %collective-permute-start.21 = (f32[4,192,256]{2,1,0:T(8,128)S(1)}, f32[4,192,256]{2,1,0:T(8,128)S(1)}, u32[]{:S(2)}, u32[]{:S(2)}) collective-permute-start(f32[4,192,256]{2,1,0:T(8,128)S(1)} %shard_map.60), channel_id=1, source_target_pairs={{0,3},{1,2},{2,1},{3,0},{4,7},{5,6},{6,5},{7,4},{8,11},{9,10},{10,... | collective-permute-start | bytes 2359304 | tf_op jit(solution)/shard_map/ppermute | solution.py:21
  56.3 17.9 %collective-permute-start.19 = (f32[4,192,256]{2,1,0:T(8,128)S(1)}, f32[4,192,256]{2,1,0:T(8,128)S(1)}, u32[]{:S(2)}, u32[]{:S(2)}) collective-permute-start(f32[4,192,256]{2,1,0:T(8,128)S(1)} %shard_map.59), channel_id=1, source_target_pairs={{0,1},{1,0},{2,3},{3,2},{4,5},{5,4},{6,7},{7,6},{8,9},{9,8},{10,11... | collective-permute-start | bytes 2359304 | tf_op jit(solution)/shard_map/ppermute | solution.py:21
  74.3 7.0 %collective-permute-start.24 = (f32[192,256]{1,0:T(8,128)S(1)}, f32[192,256]{1,0:T(8,128)S(1)}, u32[]{:S(2)}, u32[]{:S(2)}) collective-permute-start(f32[192,256]{1,0:T(8,128)S(1)} %get-tuple-element.41), channel_id=1, source_target_pairs={{0,68},{1,69},{2,70},{3,71},{4,64},{5,65},{6,66},{7,67},{8,76},{9,... | collective-permute-start | bytes 589832 | tf_op jit(solution)/shard_map/ppermute | solution.py:21
  74.4 15.1 %collective-permute-start.17 = (f32[320,256]{1,0:T(8,128)S(1)}, f32[320,256]{1,0:T(8,128)S(1)}, u32[]{:S(2)}, u32[]{:S(2)}) collective-permute-start(f32[320,256]{1,0:T(8,128)S(1)} %get-tuple-element.37), channel_id=1, source_target_pairs={{0,3},{1,2},{2,1},{3,0},{4,7},{5,6},{6,5},{7,4},{8,11},{9,10},{10,... | collective-permute-start | bytes 983048 | tf_op jit(solution)/shard_map/ppermute | solution.py:21
  77.6 12.0 %collective-permute-start.16 = (f32[320,256]{1,0:T(8,128)S(1)}, f32[320,256]{1,0:T(8,128)S(1)}, u32[]{:S(2)}, u32[]{:S(2)}) collective-permute-start(f32[320,256]{1,0:T(8,128)S(1)} %get-tuple-element.38), channel_id=1, source_target_pairs={{0,1},{1,0},{2,3},{3,2},{4,5},{5,4},{6,7},{7,6},{8,9},{9,8},{10,11... | collective-permute-start | bytes 983048 | tf_op jit(solution)/shard_map/ppermute | solution.py:21
  77.6 14.7 %collective-permute-start.15 = (f32[320,256]{1,0:T(8,128)S(1)}, f32[320,256]{1,0:T(8,128)S(1)}, u32[]{:S(2)}, u32[]{:S(2)}) collective-permute-start(f32[320,256]{1,0:T(8,128)S(1)} %get-tuple-element.39), channel_id=1, source_target_pairs={{0,2},{1,3},{2,0},{3,1},{4,6},{5,7},{6,4},{7,5},{8,10},{9,11},{10,... | collective-permute-start | bytes 983048 | tf_op jit(solution)/shard_map/ppermute | solution.py:21
  79.2 6.8 %collective-permute-start.23 = (f32[192,256]{1,0:T(8,128)S(1)}, f32[192,256]{1,0:T(8,128)S(1)}, u32[]{:S(2)}, u32[]{:S(2)}) collective-permute-start(f32[192,256]{1,0:T(8,128)S(1)} %get-tuple-element.42), channel_id=1, source_target_pairs={{0,64},{1,65},{2,66},{3,67},{4,68},{5,69},{6,70},{7,71},{8,72},{9,... | collective-permute-start | bytes 589832 | tf_op jit(solution)/shard_map/ppermute | solution.py:21
  81.3 8.3 %collective-permute-start.22 = (f32[192,256]{1,0:T(8,128)S(1)}, f32[192,256]{1,0:T(8,128)S(1)}, u32[]{:S(2)}, u32[]{:S(2)}) collective-permute-start(f32[192,256]{1,0:T(8,128)S(1)} %get-tuple-element.43), channel_id=1, source_target_pairs={{0,4},{1,5},{2,6},{3,7},{4,0},{5,1},{6,2},{7,3},{8,12},{9,13},{10,... | collective-permute-start | bytes 589832 | tf_op jit(solution)/shard_map/ppermute | solution.py:21
  (6 other events, 69.3 us)

commit v5 on v4

v5 whole, which is shorter than its diff:
```python
import jax
import jax.numpy as jnp
from jax import lax
from jax.experimental import pallas as pl
from jax.experimental.pallas import tpu as pltpu
from jax.sharding import Mesh
from jax.sharding import PartitionSpec as P

TILE = 512
WIDTH = 256
AXES = ("yl", "x", "c", "yh", "z")
SIZES = (2, 4, 2, 2, 4)
ROWS = {"A": 256, "B": 256}
COST = {"first": 1, "second": 1, "join_a": 1, "join_b": 1, "last": 1}
SMEM = pl.BlockSpec(memory_space=pltpu.SMEM)
VMEM = pl.BlockSpec(memory_space=pltpu.VMEM)


def permute(value, yl=0, x=0, c=0, yh=0, z=0):
    bits = (((yl * 4 + x) * 2 + c) * 2 + yh) * 4 + z
    return lax.ppermute(value, AXES, [(n, n ^ bits) for n in range(128)])


def along_y(value, bits):
    return permute(value, yl=bits % 2, yh=bits // 2)


def along_z(value, bits):
    return permute(value, z=bits)


def settings(cost):
    size = 48 if cost in ("first", "second") else 8
    return dict(
        compiler_params=pltpu.CompilerParams(vmem_limit_bytes=size * 2**20),
        cost_estimate=pl.CostEstimate(flops=1, bytes_accessed=COST[cost], transcendentals=0),
    )


def product_kernel(turns_all, plan, blocks, spots, left_mask, right_mask, result_mask, *rest):
    pieces, right, outs, (hi_ref, lo_ref, tiles, sems) = rest[:blocks], rest[blocks], rest[blocks + 1 : -4], rest[-4:]
    yl, x, c, yh, z = (spots[n] for n in range(5))
    k = (yh * 4 + z) * 2 + yl
    first = (x * 2 + c) * 4
    near = 1 - lax.rem(x, 2)

    def used(dy, chunk):
        i = lax.rem(yl + dy % 2, 2)
        j = first + lax.div(chunk, 2)
        return left_mask[i, k] * right_mask[k, j] * result_mask[i, j] > 0

    def fetch(n, chunk):
        where = pl.ds(pl.multiple_of(chunk * WIDTH, WIDTH), WIDTH)
        return pltpu.make_async_copy(right.at[:, where], tiles.at[n], sems.at[n])

    groups = [
        (n, lax.rem(yh + high, 2) * 4 + jnp.bitwise_xor(z, dz), [dy for dy in turns_all if dy // 2 == high], dz)
        for n, (high, dz) in enumerate((high, dz) for high in range(2) for dz in range(4))
    ]

    def wanted(chunk, turns):
        flag = used(turns[0], chunk)
        for dy in turns[1:]:
            flag = jnp.logical_or(flag, used(dy, chunk))
        return flag

    for n, chunk, turns, _ in groups:

        @pl.when(wanted(chunk, turns))
        def _():
            fetch(n, chunk).start()

    if blocks == 2:
        cores = [(c, pieces[0]), (1 - c, pieces[1])]
    else:
        cores = [(core, pieces[0].at[core]) for core in range(2)]
    for core, piece in cores:
        for n, chip in enumerate((near, 1 - near)):
            value = piece[n]
            hi = value.astype(jnp.bfloat16)
            where = pl.ds(pl.multiple_of(chip * 256 + core * 128, 128), 128)
            hi_ref[:, where] = hi
            lo_ref[:, where] = (value - hi.astype(jnp.float32)).astype(jnp.bfloat16)
    for n, chunk, turns, dz in groups:

        @pl.when(wanted(chunk, turns))
        def _():
            fetch(n, chunk).wait()

        for dy in turns:

            @pl.when(used(dy, chunk))
            def _():
                tile = tiles[n]
                hi = tile.astype(jnp.bfloat16)
                lo = (tile - hi.astype(jnp.float32)).astype(jnp.bfloat16)
                total = jnp.dot(hi_ref[...], hi, preferred_element_type=jnp.float32)
                total += jnp.dot(hi_ref[...], lo, preferred_element_type=jnp.float32)
                total += jnp.dot(lo_ref[...], hi, preferred_element_type=jnp.float32)
                done = 0
                for half, out, slot in plan[dy, dz]:
                    outs[out][slot] = total[done : done + ROWS[half]]
                    done += ROWS[half]

            @pl.when(jnp.logical_not(used(dy, chunk)))
            def _():
                for half, out, slot in plan[dy, dz]:
                    outs[out][slot] = jnp.zeros((ROWS[half], WIDTH), jnp.float32)


def product(turns, names, spots, masks, pieces, right, cost):
    plan = {
        (dy, dz): [
            (half, n, blocks.index((half, dy, dz)))
            for half in "AB"
            for n, blocks in enumerate(names.values())
            if (half, dy, dz) in blocks
        ]
        for dy in turns
        for dz in range(4)
    }
    outs = pl.pallas_call(
        lambda *refs: product_kernel(turns, plan, len(pieces), *refs),
        out_shape=[jax.ShapeDtypeStruct((len(b), ROWS[b[0][0]], WIDTH), jnp.float32) for b in names.values()],
        in_specs=[SMEM] * 4 + [VMEM] * len(pieces) + [pl.BlockSpec(memory_space=pltpu.HBM)],
        out_specs=[VMEM] * len(names),
        scratch_shapes=[pltpu.VMEM((TILE, TILE), jnp.bfloat16)] * 2
        + [pltpu.VMEM((8, TILE, WIDTH), jnp.float32), pltpu.SemaphoreType.DMA((8,))],
        **settings(cost),
    )(spots, *masks, *pieces, right)
    return dict(zip(names, outs))


def join(value, first, arrived, cost, kept=None):
    def kernel(value_ref, arrived_ref, *rest):
        out_ref = rest[-1]
        del value_ref
        for n in range(count):
            out_ref[first + n] = (rest[0][n] if kept is not None else out_ref[first + n]) + arrived_ref[n]

    count = min(value.shape[0] - first, arrived.shape[0])
    operands = [value, arrived] + ([] if kept is None else [kept])
    return pl.pallas_call(
        kernel,
        out_shape=jax.ShapeDtypeStruct(value.shape, value.dtype),
        in_specs=[VMEM] * len(operands),
        out_specs=VMEM,
        input_output_aliases={0: 0},
        **settings(cost),
    )(*operands)


def total(top, bottom):
    def kernel(*refs):
        out_ref = refs[-1]
        out_ref[: ROWS["A"]] = sum(ref[...] for ref in refs[1 : len(top)]) + refs[0][...]
        out_ref[ROWS["A"] :] = sum(ref[...] for ref in refs[len(top) + 1 : -1]) + refs[len(top)][...]

    return pl.pallas_call(
        kernel,
        out_shape=jax.ShapeDtypeStruct((TILE, WIDTH), jnp.float32),
        in_specs=[VMEM] * (len(top) + len(bottom)),
        **settings("last"),
    )(*top, *bottom)


def both_cores(value):
    return lax.all_to_all(jnp.broadcast_to(value[None], (2, *value.shape)), "c", 0, 0, tiled=True)


def shards(left, right, left_mask, right_mask, result_mask):
    yl, x, c, yh, z = (lax.axis_index(a) for a in AXES)
    spots = jnp.stack([yl, x, c, yh, z]).astype(jnp.int32)
    masks = (left_mask, right_mask, result_mask)

    here = x // 2 == yl
    across, beside, between = (permute(left, x=bits) for bits in (2, 3, 1))
    mine = jnp.stack([jnp.where(here, between, beside), jnp.where(here, left, across)])
    others = jnp.stack([jnp.where(here, beside, between), jnp.where(here, across, left)])
    others = along_y(others, 1)
    p = product(
        (0, 2),
        {
            "y1": [("A", 2, 0), ("A", 2, 1)],
            "y3": [("A", 2, 2), ("A", 2, 3)],
            "z1": [("B", 0, 2), ("B", 0, 1)],
            "z3": [("B", 2, 2), ("B", 2, 3)],
            "z1_kept": [("B", 2, 1)],
            "z3_kept": [("B", 0, 3)],
            "a": [("A", 0, d) for d in range(4)],
            "b": [("B", 0, 0), ("B", 2, 0)],
        },
        spots,
        masks,
        (mine, permute(mine, c=1)),
        right,
        "first",
    )
    from_y1 = along_y(p["y1"], 1)
    from_y3 = along_y(p["y3"], 3)
    from_z1 = along_z(p["z1"], 1)
    from_z3 = along_z(p["z3"], 3)
    others, a_own = lax.optimization_barrier((others, p["a"]))
    q = product(
        (1, 3),
        {
            "y1": [("A", 1, d) for d in range(4)],
            "y3": [("A", 3, d) for d in range(4)],
            "z1": [("B", 1, 2), ("B", 1, 1), ("B", 1, 1)],
            "z3": [("B", 3, 2), ("B", 3, 3), ("B", 3, 3)],
            "z1_last": [("B", 3, 1)],
            "z3_last": [("B", 1, 3)],
            "b": [("B", 1, 0), ("B", 3, 0)],
        },
        spots,
        masks,
        (both_cores(others),),
        right,
        "second",
    )
    sum_y1 = along_y(join(q["y1"], 2, from_y3, "join_a"), 1)
    sum_y3 = along_y(join(q["y3"], 0, from_y1, "join_a"), 3)
    next_z1 = along_z(join(q["z1"], 2, from_z3, "join_b", p["z1_kept"]), 1)
    next_z3 = along_z(join(q["z3"], 2, from_z1, "join_b", p["z3_kept"]), 3)
    last_z1 = along_z(join(q["z1_last"], 0, next_z3, "join_b"), 1)
    last_z3 = along_z(join(q["z3_last"], 0, next_z1, "join_b"), 3)
    a = [a_own[d] + sum_y1[d] + sum_y3[d] for d in range(4)]
    b = [
        p["b"][0] + from_z1[1] + next_z3[2],
        q["b"][0] + next_z1[1] + last_z3[0],
        p["b"][1] + next_z1[2] + from_z3[1],
        q["b"][1] + last_z1[0] + next_z3[1],
    ]
    return total(
        [a[0], along_z(a[2], 2), along_z(a[1], 1), along_z(a[3], 3)],
        [b[0], along_y(b[2], 2), along_y(b[1], 1), along_y(b[3], 3)],
    )


def solution(mesh):
    torus = Mesh(mesh.devices.reshape(SIZES), AXES)
    in_specs = (
        P("yl", ("yh", "z", "x", "c")),
        P(("yh", "z", "yl"), ("x", "c")),
        P(),
        P(),
        P(),
    )
    return jax.shard_map(
        shards, mesh=torus, in_specs=in_specs, out_specs=P("yl", ("x", "c", "yh", "z")), check_vma=False
    )
```

time: 94.1 us -> 92.7 us (0.985)
  waiting for transfers between devices: 52 us -> 45.4 us
  starting transfers between devices: 31.5 us -> 36.6 us
  blocking collectives: 0 us -> 4.58 us
  local copies, waits for them, and re-layouts: 4.15 us -> 0.16 us
  other arithmetic: 0.55 us -> 1.54 us
    ppermute x25 -> x21, waiting for transfers between devices: 52 us -> 45.4 us  [permute(): return lax.ppermute(value, AXES, [(n, n ^ bits) for n in range(128)])]
    ppermute x25 -> x21, starting transfers between devices: 31.5 us -> 36.6 us  [permute(): return lax.ppermute(value, AXES, [(n, n ^ bits) for n in range(128)])]
    all_to_all x0 -> x1, blocking collectives: none -> 4.58 us  [both_cores(): lax.all_to_all(jnp.broadcast_to(value[None], (2, *value.shape)), 'c', 0,...]
    unnamed x10 -> x6, local copies, waits for them, and re-layouts: 2.2 us -> 0.01 us
    slice x2 -> x0, local copies, waits for them, and re-layouts: 1.87 us -> none  [shards(): left_a, left_b = lax.optimization_barrier((left[:rows_a], left[rows_a:]))]
    another operation x0 -> x4, other arithmetic: none -> 1.1 us  [the longest x3 1.06 us: shards(): jnp.stack([jnp.where(here, between, beside), jnp.where(here, left, across)])]
  transfers between devices with their start and end apart: 25 -> 21, of which waited for: 16 -> 13; matrix products, arithmetic and copies ran while one was open for 1% -> 2% of each run, Pallas kernels for 4% -> 3%
where the time goes in v5:
time: 92.7 us; the launch traced here: 92.6 us
  waiting for transfers between devices  45.4 us (49%)
  starting transfers between devices  36.6 us (39%)
  blocking collectives  4.58 us (5%)
  Pallas kernels  4.13 us (4%)
  other arithmetic  1.54 us (2%)
    ppermute x21, waiting for transfers between devices, permute(): return lax.ppermute(value, AXES, [(n, n ^ bits) for n in range(128)])  45.4 us
    ppermute x21, starting transfers between devices, permute(): return lax.ppermute(value, AXES, [(n, n ^ bits) for n in range(128)])  36.6 us
    all_to_all x1, blocking collectives, both_cores(): lax.all_to_all(jnp.broadcast_to(value[None], (2, *value.shape)), 'c', 0,...  4.58 us
    pallas_call x2, Pallas kernels, product(): pl.pallas_call(lambda *refs: product_kernel(turns, plan, len(pieces), *re...  2.98 us
  transfers between devices with their start and end apart: 21, of which 13 were waited for; matrix products, arithmetic and copies ran while one was open for 2% of the time, Pallas kernels for 3%

profile of v5, /device:TPU:0, one launch (start us, length us, event | category | flops | bytes accessed | tf_op | source)
XLA Modules:
  0.0 92.6 jit_solution(13582089778908901647)
XLA Ops:
  0.0 3.2 %collective-permute-start.2 = (f32[512,128]{1,0:T(8,128)}, f32[512,128]{1,0:T(8,128)S(1)}, u32[]{:S(2)}, u32[]{:S(2)}) collective-permute-start(f32[512,128]{1,0:T(8,128)} %param.5), channel_id=1, source_target_pairs={{0,32},{1,33},{2,34},{3,35},{4,36},{5,37},{6,38},{7,39},{8,40},{9,... | collective-permute-start | bytes 786440 | tf_op jit(solution)/shard_map/ppermute | solution.py:21
  4.3 6.6 %collective-permute-done.2 = f32[512,128]{1,0:T(8,128)S(1)} collective-permute-done((f32[512,128]{1,0:T(8,128)}, f32[512,128]{1,0:T(8,128)S(1)}, u32[]{:S(2)}, u32[]{:S(2)}) %collective-permute-start.2) | collective-permute-done | bytes 262176 | tf_op jit(solution)/shard_map/ppermute | solution.py:21
  11.9 3.8 %collective-permute-done.1 = f32[512,128]{1,0:T(8,128)S(1)} collective-permute-done((f32[512,128]{1,0:T(8,128)}, f32[512,128]{1,0:T(8,128)S(1)}, u32[]{:S(2)}, u32[]{:S(2)}) %collective-permute-start.1) | collective-permute-done | bytes 262176 | tf_op jit(solution)/shard_map/ppermute | solution.py:21
  15.9 1.7 %collective-permute-start.3 = (f32[2,512,128]{2,1,0:T(8,128)S(1)}, f32[2,512,128]{2,1,0:T(8,128)S(1)}, u32[]{:S(2)}, u32[]{:S(2)}) collective-permute-start(f32[2,512,128]{2,1,0:T(8,128)S(1)} %pad_maximum_fusion), channel_id=1, source_target_pairs={{0,64},{1,65},{2,66},{3,67},{4,68},{5,69},{6,70},{7,71},{8,72},{9,... | collective-permute-start | bytes 1572872 | tf_op jit(solution)/shard_map/ppermute | solution.py:21
  17.8 1.5 %shard_map.55 = (f32[2,256,256]{2,1,0:T(8,128)S(1)}, f32[2,256,256]{2,1,0:T(8,128)S(1)}, f32[2,256,256]{2,1,0:T(8,128)S(1)}, f32[2,256,256]{2,1,0:T(8,128)S(1)},...) custom-call(s32[5]{0:T(128)S(1)} %stack.44.refs_0_, ...), custom_call_target="tpu_custom_call" | custom-call | flops 1 | bytes 1 | tf_op jit(solution)/shard_map/pallas_call | solution.py:122
  19.3 6.1 %collective-permute-start.14 = (f32[2,256,256]{2,1,0:T(8,128)S(1)}, f32[2,256,256]{2,1,0:T(8,128)S(1)}, u32[]{:S(2)}, u32[]{:S(2)}) collective-permute-start(f32[2,256,256]{2,1,0:T(8,128)S(1)} %get-tuple-element.34), channel_id=1, source_target_pairs={{0,3},{1,2},{2,1},{3,0},{4,7},{5,6},{6,5},{7,4},{8,11},{9,10},{10,... | collective-permute-start | bytes 1572872 | tf_op jit(solution)/shard_map/ppermute | solution.py:21
  25.4 3.3 %collective-permute-start.5 = (f32[2,256,256]{2,1,0:T(8,128)S(1)}, f32[2,256,256]{2,1,0:T(8,128)S(1)}, u32[]{:S(2)}, u32[]{:S(2)}) collective-permute-start(f32[2,256,256]{2,1,0:T(8,128)S(1)} %get-tuple-element.26), channel_id=1, source_target_pairs={{0,68},{1,69},{2,70},{3,71},{4,64},{5,65},{6,66},{7,67},{8,76},{9,... | collective-permute-start | bytes 1572872 | tf_op jit(solution)/shard_map/ppermute | solution.py:21
  28.7 2.0 %collective-permute-done.3 = f32[2,512,128]{2,1,0:T(8,128)S(1)} collective-permute-done((f32[2,512,128]{2,1,0:T(8,128)S(1)}, f32[2,512,128]{2,1,0:T(8,128)S(1)}, u32[]{:S(2)}, u32[]{:S(2)}) %collective-permute-start.3) | collective-permute-done | bytes 524320 | tf_op jit(solution)/shard_map/ppermute | solution.py:21
  30.8 4.6 %all_to_all.5.refs_4_ = f32[2,2,512,128]{3,2,1,0:T(8,128)S(1)} all-to-all(f32[2,2,512,128]{3,2,1,0:T(8,128)S(1)} %broadcast_in_dim.2), channel_id=1, replica_groups=mesh['yl'=2,'x'=4,'c'=2,'yh'=2,'z'=4] {'c'}, dimensions={0} | all-to-all | bytes 2097152 | tf_op jit(solution)/shard_map/all_to_all | solution.py:168
  35.4 1.5 %shard_map.56 = (f32[4,256,256]{2,1,0:T(8,128)S(1)}, f32[4,256,256]{2,1,0:T(8,128)S(1)}, f32[3,256,256]{2,1,0:T(8,128)S(1)}, f32[3,256,256]{2,1,0:T(8,128)S(1)},...) custom-call(s32[5]{0:T(128)S(1)} %stack.44.refs_0_, s32[2,16]{1,0:T(2,128)S(1)} %copy-done.1, ...), custom_call_target="tpu_custom_call" | custom-call | flops 1 | bytes 1 | tf_op jit(solution)/shard_map/pallas_call | solution.py:122
  40.1 3.1 %collective-permute-start.13 = (f32[3,256,256]{2,1,0:T(8,128)S(1)}, f32[3,256,256]{2,1,0:T(8,128)S(1)}, u32[]{:S(2)}, u32[]{:S(2)}) collective-permute-start(f32[3,256,256]{2,1,0:T(8,128)S(1)} %shard_map.59), channel_id=1, source_target_pairs={{0,3},{1,2},{2,1},{3,0},{4,7},{5,6},{6,5},{7,4},{8,11},{9,10},{10,... | collective-permute-start | bytes 2359304 | tf_op jit(solution)/shard_map/ppermute | solution.py:21
  43.3 3.4 %collective-permute-start.8 = (f32[4,256,256]{2,1,0:T(8,128)S(1)}, f32[4,256,256]{2,1,0:T(8,128)S(1)}, u32[]{:S(2)}, u32[]{:S(2)}) collective-permute-start(f32[4,256,256]{2,1,0:T(8,128)S(1)} %shard_map.58), channel_id=1, source_target_pairs={{0,68},{1,69},{2,70},{3,71},{4,64},{5,65},{6,66},{7,67},{8,76},{9,... | collective-permute-start | bytes 3145736 | tf_op jit(solution)/shard_map/ppermute | solution.py:21
  46.8 11.0 %collective-permute-done.15.arrived_ref = f32[3,256,256]{2,1,0:T(8,128)S(1)} collective-permute-done((f32[3,256,256]{2,1,0:T(8,128)S(1)}, f32[3,256,256]{2,1,0:T(8,128)S(1)}, u32[]{:S(2)}, u32[]{:S(2)}) %collective-permute-start.15) | collective-permute-done | bytes 786464 | tf_op jit(solution)/shard_map/ppermute | solution.py:21
  57.8 4.9 %collective-permute-start.17 = (f32[1,256,256]{2,1,0:T(8,128)S(1)}, f32[1,256,256]{2,1,0:T(8,128)S(1)}, u32[]{:S(2)}, u32[]{:S(2)}) collective-permute-start(f32[1,256,256]{2,1,0:T(8,128)S(1)} %shard_map.61), channel_id=1, source_target_pairs={{0,3},{1,2},{2,1},{3,0},{4,7},{5,6},{6,5},{7,4},{8,11},{9,10},{10,... | collective-permute-start | bytes 786440 | tf_op jit(solution)/shard_map/ppermute | solution.py:21
  62.8 7.0 %collective-permute-done.17 = f32[1,256,256]{2,1,0:T(8,128)S(1)} collective-permute-done((f32[1,256,256]{2,1,0:T(8,128)S(1)}, f32[1,256,256]{2,1,0:T(8,128)S(1)}, u32[]{:S(2)}, u32[]{:S(2)}) %collective-permute-start.17) | collective-permute-done | bytes 262176 | tf_op jit(solution)/shard_map/ppermute | solution.py:21
  69.8 1.6 %collective-permute-done.19 = f32[1,256,256]{2,1,0:T(8,128)S(1)} collective-permute-done((f32[1,256,256]{2,1,0:T(8,128)S(1)}, f32[1,256,256]{2,1,0:T(8,128)S(1)}, u32[]{:S(2)}, u32[]{:S(2)}) %collective-permute-start.19) | collective-permute-done | bytes 262176 | tf_op jit(solution)/shard_map/ppermute | solution.py:21
  71.7 3.2 %collective-permute-start.16 = (f32[256,256]{1,0:T(8,128)S(1)}, f32[256,256]{1,0:T(8,128)S(1)}, u32[]{:S(2)}, u32[]{:S(2)}) collective-permute-start(f32[256,256]{1,0:T(8,128)S(1)} %get-tuple-element.46), channel_id=1, source_target_pairs={{0,4},{1,5},{2,6},{3,7},{4,0},{5,1},{6,2},{7,3},{8,12},{9,13},{10,... | collective-permute-start | bytes 786440 | tf_op jit(solution)/shard_map/ppermute | solution.py:21
  75.0 1.4 %collective-permute-start.20 = (f32[256,256]{1,0:T(8,128)S(1)}, f32[256,256]{1,0:T(8,128)S(1)}, u32[]{:S(2)}, u32[]{:S(2)}) collective-permute-start(f32[256,256]{1,0:T(8,128)S(1)} %get-tuple-element.48), channel_id=1, source_target_pairs={{0,68},{1,69},{2,70},{3,71},{4,64},{5,65},{6,66},{7,67},{8,76},{9,... | collective-permute-start | bytes 786440 | tf_op jit(solution)/shard_map/ppermute | solution.py:21
  76.6 2.0 %collective-permute-start.11 = (f32[256,256]{1,0:T(8,128)S(1)}, f32[256,256]{1,0:T(8,128)S(1)}, u32[]{:S(2)}, u32[]{:S(2)}) collective-permute-start(f32[256,256]{1,0:T(8,128)S(1)} %get-tuple-element.39), channel_id=1, source_target_pairs={{0,3},{1,2},{2,1},{3,0},{4,7},{5,6},{6,5},{7,4},{8,11},{9,10},{10,... | collective-permute-start | bytes 786440 | tf_op jit(solution)/shard_map/ppermute | solution.py:21
  78.6 2.3 %collective-permute-done.18.refs_6_ = f32[256,256]{1,0:T(8,128)S(1)} collective-permute-done((f32[256,256]{1,0:T(8,128)S(1)}, f32[256,256]{1,0:T(8,128)S(1)}, u32[]{:S(2)}, u32[]{:S(2)}) %collective-permute-start.18) | collective-permute-done | bytes 262176 | tf_op jit(solution)/shard_map/ppermute | solution.py:21
  80.9 1.7 %collective-permute-start.9 = (f32[256,256]{1,0:T(8,128)S(1)}, f32[256,256]{1,0:T(8,128)S(1)}, u32[]{:S(2)}, u32[]{:S(2)}) collective-permute-start(f32[256,256]{1,0:T(8,128)S(1)} %get-tuple-element.41), channel_id=1, source_target_pairs={{0,2},{1,3},{2,0},{3,1},{4,6},{5,7},{6,4},{7,5},{8,10},{9,11},{10,... | collective-permute-start | bytes 786440 | tf_op jit(solution)/shard_map/ppermute | solution.py:21
  82.7 3.9 %collective-permute-done.16.refs_5_ = f32[256,256]{1,0:T(8,128)S(1)} collective-permute-done((f32[256,256]{1,0:T(8,128)S(1)}, f32[256,256]{1,0:T(8,128)S(1)}, u32[]{:S(2)}, u32[]{:S(2)}) %collective-permute-start.16) | collective-permute-done | bytes 262176 | tf_op jit(solution)/shard_map/ppermute | solution.py:21
  86.6 2.6 %collective-permute-done.20.refs_7_ = f32[256,256]{1,0:T(8,128)S(1)} collective-permute-done((f32[256,256]{1,0:T(8,128)S(1)}, f32[256,256]{1,0:T(8,128)S(1)}, u32[]{:S(2)}, u32[]{:S(2)}) %collective-permute-start.20) | collective-permute-done | bytes 262176 | tf_op jit(solution)/shard_map/ppermute | solution.py:21
  89.2 2.5 %collective-permute-done.9.refs_1_ = f32[256,256]{1,0:T(8,128)S(1)} collective-permute-done((f32[256,256]{1,0:T(8,128)S(1)}, f32[256,256]{1,0:T(8,128)S(1)}, u32[]{:S(2)}, u32[]{:S(2)}) %collective-permute-start.9) | collective-permute-done | bytes 262176 | tf_op jit(solution)/shard_map/ppermute | solution.py:21
  (42 shorter events, 7.7 us)
Async XLA Ops:
  0.0 17.8 %copy-start.2 = (s32[2,32]{1,0:T(2,128)S(1)}, s32[2,32]{1,0:T(2,128)}, u32[]{:S(2)}) copy-start(s32[2,32]{1,0:T(2,128)} %refs_3_.3) | copy-start | bytes 772
  0.0 17.8 %copy-start = (s32[16,32]{1,0:T(8,128)S(1)}, s32[16,32]{1,0:T(8,128)}, u32[]{:S(2)}) copy-start(s32[16,32]{1,0:T(8,128)} %refs_2_.3) | copy-start | bytes 6148
  0.0 17.8 %copy-start.1 = (s32[2,16]{1,0:T(2,128)S(1)}, s32[2,16]{1,0:T(2,128)}, u32[]{:S(2)}) copy-start(s32[2,16]{1,0:T(2,128)} %refs_1_.3) | copy-start | bytes 388
  0.0 10.9 %collective-permute-start.2 = (f32[512,128]{1,0:T(8,128)}, f32[512,128]{1,0:T(8,128)S(1)}, u32[]{:S(2)}, u32[]{:S(2)}) collective-permute-start(f32[512,128]{1,0:T(8,128)} %param.5), channel_id=1, source_target_pairs={{0,32},{1,33},{2,34},{3,35},{4,36},{5,37},{6,38},{7,39},{8,40},{9,... | collective-permute-start | bytes 786440 | tf_op jit(solution)/shard_map/ppermute | solution.py:21
  3.2 12.5 %collective-permute-start.1 = (f32[512,128]{1,0:T(8,128)}, f32[512,128]{1,0:T(8,128)S(1)}, u32[]{:S(2)}, u32[]{:S(2)}) collective-permute-start(f32[512,128]{1,0:T(8,128)} %param.5), channel_id=1, source_target_pairs={{0,16},{1,17},{2,18},{3,19},{4,20},{5,21},{6,22},{7,23},{8,24},{9,... | collective-permute-start | bytes 786440 | tf_op jit(solution)/shard_map/ppermute | solution.py:21
  3.8 11.9 %collective-permute-start = (f32[512,128]{1,0:T(8,128)}, f32[512,128]{1,0:T(8,128)S(1)}, u32[]{:S(2)}, u32[]{:S(2)}) collective-permute-start(f32[512,128]{1,0:T(8,128)} %param.5), channel_id=1, source_target_pairs={{0,48},{1,49},{2,50},{3,51},{4,52},{5,53},{6,54},{7,55},{8,56},{9,... | collective-permute-start | bytes 786440 | tf_op jit(solution)/shard_map/ppermute | solution.py:21
  15.8 2.0 %collective-permute-start.4 = (f32[2,512,128]{2,1,0:T(8,128)S(1)}, f32[2,512,128]{2,1,0:T(8,128)S(1)}, u32[]{:S(2)}, u32[]{:S(2)}) collective-permute-start(f32[2,512,128]{2,1,0:T(8,128)S(1)} %pad_maximum_fusion.1.refs_4_), channel_id=1, source_target_pairs={{0,8},{1,9},{2,10},{3,11},{4,12},{5,13},{6,14},{7,15},{8,0},{9,1},... | collective-permute-start | bytes 1572872 | tf_op jit(solution)/shard_map/ppermute | solution.py:21
  15.9 14.8 %collective-permute-start.3 = (f32[2,512,128]{2,1,0:T(8,128)S(1)}, f32[2,512,128]{2,1,0:T(8,128)S(1)}, u32[]{:S(2)}, u32[]{:S(2)}) collective-permute-start(f32[2,512,128]{2,1,0:T(8,128)S(1)} %pad_maximum_fusion), channel_id=1, source_target_pairs={{0,64},{1,65},{2,66},{3,67},{4,68},{5,69},{6,70},{7,71},{8,72},{9,... | collective-permute-start | bytes 1572872 | tf_op jit(solution)/shard_map/ppermute | solution.py:21
  19.3 18.4 %collective-permute-start.14 = (f32[2,256,256]{2,1,0:T(8,128)S(1)}, f32[2,256,256]{2,1,0:T(8,128)S(1)}, u32[]{:S(2)}, u32[]{:S(2)}) collective-permute-start(f32[2,256,256]{2,1,0:T(8,128)S(1)} %get-tuple-element.34), channel_id=1, source_target_pairs={{0,3},{1,2},{2,1},{3,0},{4,7},{5,6},{6,5},{7,4},{8,11},{9,10},{10,... | collective-permute-start | bytes 1572872 | tf_op jit(solution)/shard_map/ppermute | solution.py:21
  25.3 14.8 %collective-permute-start.12 = (f32[2,256,256]{2,1,0:T(8,128)S(1)}, f32[2,256,256]{2,1,0:T(8,128)S(1)}, u32[]{:S(2)}, u32[]{:S(2)}) collective-permute-start(f32[2,256,256]{2,1,0:T(8,128)S(1)} %get-tuple-element.30), channel_id=1, source_target_pairs={{0,1},{1,0},{2,3},{3,2},{4,5},{5,4},{6,7},{7,6},{8,9},{9,8},{10,11... | collective-permute-start | bytes 1572872 | tf_op jit(solution)/shard_map/ppermute | solution.py:21
  25.3 17.9 %collective-permute-start.7 = (f32[2,256,256]{2,1,0:T(8,128)S(1)}, f32[2,256,256]{2,1,0:T(8,128)S(1)}, u32[]{:S(2)}, u32[]{:S(2)}) collective-permute-start(f32[2,256,256]{2,1,0:T(8,128)S(1)} %get-tuple-element.28), channel_id=1, source_target_pairs={{0,64},{1,65},{2,66},{3,67},{4,68},{5,69},{6,70},{7,71},{8,72},{9,... | collective-permute-start | bytes 1572872 | tf_op jit(solution)/shard_map/ppermute | solution.py:21
  25.4 21.3 %collective-permute-start.5 = (f32[2,256,256]{2,1,0:T(8,128)S(1)}, f32[2,256,256]{2,1,0:T(8,128)S(1)}, u32[]{:S(2)}, u32[]{:S(2)}) collective-permute-start(f32[2,256,256]{2,1,0:T(8,128)S(1)} %get-tuple-element.26), channel_id=1, source_target_pairs={{0,68},{1,69},{2,70},{3,71},{4,64},{5,65},{6,66},{7,67},{8,76},{9,... | collective-permute-start | bytes 1572872 | tf_op jit(solution)/shard_map/ppermute | solution.py:21
  37.7 20.1 %collective-permute-start.15 = (f32[3,256,256]{2,1,0:T(8,128)S(1)}, f32[3,256,256]{2,1,0:T(8,128)S(1)}, u32[]{:S(2)}, u32[]{:S(2)}) collective-permute-start(f32[3,256,256]{2,1,0:T(8,128)S(1)} %shard_map.60), channel_id=1, source_target_pairs={{0,1},{1,0},{2,3},{3,2},{4,5},{5,4},{6,7},{7,6},{8,9},{9,8},{10,11... | collective-permute-start | bytes 2359304 | tf_op jit(solution)/shard_map/ppermute | solution.py:21
  40.1 22.6 %collective-permute-start.13 = (f32[3,256,256]{2,1,0:T(8,128)S(1)}, f32[3,256,256]{2,1,0:T(8,128)S(1)}, u32[]{:S(2)}, u32[]{:S(2)}) collective-permute-start(f32[3,256,256]{2,1,0:T(8,128)S(1)} %shard_map.59), channel_id=1, source_target_pairs={{0,3},{1,2},{2,1},{3,0},{4,7},{5,6},{6,5},{7,4},{8,11},{9,10},{10,... | collective-permute-start | bytes 2359304 | tf_op jit(solution)/shard_map/ppermute | solution.py:21
  43.3 33.1 %collective-permute-start.8 = (f32[4,256,256]{2,1,0:T(8,128)S(1)}, f32[4,256,256]{2,1,0:T(8,128)S(1)}, u32[]{:S(2)}, u32[]{:S(2)}) collective-permute-start(f32[4,256,256]{2,1,0:T(8,128)S(1)} %shard_map.58), channel_id=1, source_target_pairs={{0,68},{1,69},{2,70},{3,71},{4,64},{5,65},{6,66},{7,67},{8,76},{9,... | collective-permute-start | bytes 3145736 | tf_op jit(solution)/shard_map/ppermute | solution.py:21
  46.7 29.7 %collective-permute-start.6 = (f32[4,256,256]{2,1,0:T(8,128)S(1)}, f32[4,256,256]{2,1,0:T(8,128)S(1)}, u32[]{:S(2)}, u32[]{:S(2)}) collective-permute-start(f32[4,256,256]{2,1,0:T(8,128)S(1)} %shard_map.57), channel_id=1, source_target_pairs={{0,64},{1,65},{2,66},{3,67},{4,68},{5,69},{6,70},{7,71},{8,72},{9,... | collective-permute-start | bytes 3145736 | tf_op jit(solution)/shard_map/ppermute | solution.py:21
  57.8 12.0 %collective-permute-start.17 = (f32[1,256,256]{2,1,0:T(8,128)S(1)}, f32[1,256,256]{2,1,0:T(8,128)S(1)}, u32[]{:S(2)}, u32[]{:S(2)}) collective-permute-start(f32[1,256,256]{2,1,0:T(8,128)S(1)} %shard_map.61), channel_id=1, source_target_pairs={{0,3},{1,2},{2,1},{3,0},{4,7},{5,6},{6,5},{7,4},{8,11},{9,10},{10,... | collective-permute-start | bytes 786440 | tf_op jit(solution)/shard_map/ppermute | solution.py:21
  62.7 8.7 %collective-permute-start.19 = (f32[1,256,256]{2,1,0:T(8,128)S(1)}, f32[1,256,256]{2,1,0:T(8,128)S(1)}, u32[]{:S(2)}, u32[]{:S(2)}) collective-permute-start(f32[1,256,256]{2,1,0:T(8,128)S(1)} %shard_map.62), channel_id=1, source_target_pairs={{0,1},{1,0},{2,3},{3,2},{4,5},{5,4},{6,7},{7,6},{8,9},{9,8},{10,11... | collective-permute-start | bytes 786440 | tf_op jit(solution)/shard_map/ppermute | solution.py:21
  71.6 9.3 %collective-permute-start.18 = (f32[256,256]{1,0:T(8,128)S(1)}, f32[256,256]{1,0:T(8,128)S(1)}, u32[]{:S(2)}, u32[]{:S(2)}) collective-permute-start(f32[256,256]{1,0:T(8,128)S(1)} %get-tuple-element.45), channel_id=1, source_target_pairs={{0,64},{1,65},{2,66},{3,67},{4,68},{5,69},{6,70},{7,71},{8,72},{9,... | collective-permute-start | bytes 786440 | tf_op jit(solution)/shard_map/ppermute | solution.py:21
  71.7 14.9 %collective-permute-start.16 = (f32[256,256]{1,0:T(8,128)S(1)}, f32[256,256]{1,0:T(8,128)S(1)}, u32[]{:S(2)}, u32[]{:S(2)}) collective-permute-start(f32[256,256]{1,0:T(8,128)S(1)} %get-tuple-element.46), channel_id=1, source_target_pairs={{0,4},{1,5},{2,6},{3,7},{4,0},{5,1},{6,2},{7,3},{8,12},{9,13},{10,... | collective-permute-start | bytes 786440 | tf_op jit(solution)/shard_map/ppermute | solution.py:21
  75.0 14.2 %collective-permute-start.20 = (f32[256,256]{1,0:T(8,128)S(1)}, f32[256,256]{1,0:T(8,128)S(1)}, u32[]{:S(2)}, u32[]{:S(2)}) collective-permute-start(f32[256,256]{1,0:T(8,128)S(1)} %get-tuple-element.48), channel_id=1, source_target_pairs={{0,68},{1,69},{2,70},{3,71},{4,64},{5,65},{6,66},{7,67},{8,76},{9,... | collective-permute-start | bytes 786440 | tf_op jit(solution)/shard_map/ppermute | solution.py:21
  76.6 12.6 %collective-permute-start.11 = (f32[256,256]{1,0:T(8,128)S(1)}, f32[256,256]{1,0:T(8,128)S(1)}, u32[]{:S(2)}, u32[]{:S(2)}) collective-permute-start(f32[256,256]{1,0:T(8,128)S(1)} %get-tuple-element.39), channel_id=1, source_target_pairs={{0,3},{1,2},{2,1},{3,0},{4,7},{5,6},{6,5},{7,4},{8,11},{9,10},{10,... | collective-permute-start | bytes 786440 | tf_op jit(solution)/shard_map/ppermute | solution.py:21
  78.6 10.6 %collective-permute-start.10 = (f32[256,256]{1,0:T(8,128)S(1)}, f32[256,256]{1,0:T(8,128)S(1)}, u32[]{:S(2)}, u32[]{:S(2)}) collective-permute-start(f32[256,256]{1,0:T(8,128)S(1)} %get-tuple-element.40), channel_id=1, source_target_pairs={{0,1},{1,0},{2,3},{3,2},{4,5},{5,4},{6,7},{7,6},{8,9},{9,8},{10,11... | collective-permute-start | bytes 786440 | tf_op jit(solution)/shard_map/ppermute | solution.py:21
  80.9 10.7 %collective-permute-start.9 = (f32[256,256]{1,0:T(8,128)S(1)}, f32[256,256]{1,0:T(8,128)S(1)}, u32[]{:S(2)}, u32[]{:S(2)}) collective-permute-start(f32[256,256]{1,0:T(8,128)S(1)} %get-tuple-element.41), channel_id=1, source_target_pairs={{0,2},{1,3},{2,0},{3,1},{4,6},{5,7},{6,4},{7,5},{8,10},{9,11},{10,... | collective-permute-start | bytes 786440 | tf_op jit(solution)/shard_map/ppermute | solution.py:21

commit v6 on v5

--- a/solution.py
+++ b/solution.py
@@ -181,8 +181,8 @@
     p = product(
         (0, 2),
         {
-            "y1": [("A", 2, 0), ("A", 2, 1)],
-            "y3": [("A", 2, 2), ("A", 2, 3)],
+            "y1": [("A", 2, 0)],
+            "y3": [("A", 2, 1), ("A", 2, 2), ("A", 2, 3)],
             "z1": [("B", 0, 2), ("B", 0, 1)],
             "z3": [("B", 2, 2), ("B", 2, 3)],
             "z1_kept": [("B", 2, 1)],
@@ -201,6 +201,7 @@
     from_z1 = along_z(p["z1"], 1)
     from_z3 = along_z(p["z3"], 3)
     others, a_own = lax.optimization_barrier((others, p["a"]))
+    others, from_y1 = lax.optimization_barrier((both_cores(others), from_y1))
     q = product(
         (1, 3),
         {
@@ -214,11 +215,11 @@
         },
         spots,
         masks,
-        (both_cores(others),),
+        (others,),
         right,
         "second",
     )
-    sum_y1 = along_y(join(q["y1"], 2, from_y3, "join_a"), 1)
+    sum_y1 = along_y(join(q["y1"], 1, from_y3, "join_a"), 1)
     sum_y3 = along_y(join(q["y3"], 0, from_y1, "join_a"), 3)
     next_z1 = along_z(join(q["z1"], 2, from_z3, "join_b", p["z1_kept"]), 1)
     next_z3 = along_z(join(q["z3"], 2, from_z1, "join_b", p["z3_kept"]), 3)
@@ -232,7 +233,7 @@
         q["b"][1] + last_z1[0] + next_z3[1],
     ]
     return total(
-        [a[0], along_z(a[2], 2), along_z(a[1], 1), along_z(a[3], 3)],
+        [a[0], along_z(a[1], 1), along_z(a[3], 3), along_z(a[2], 2)],
         [b[0], along_y(b[2], 2), along_y(b[1], 1), along_y(b[3], 3)],
     )
 

time: 92.7 us -> 91.4 us (0.986)
  starting transfers between devices: 36.6 us -> 32.9 us
  Pallas kernels: 4.13 us -> 6.16 us
    ppermute x21, starting transfers between devices: 36.6 us -> 32.9 us  [permute(): return lax.ppermute(value, AXES, [(n, n ^ bits) for n in range(128)])]
    pallas_call x2, Pallas kernels: 2.98 us -> 5.01 us  [product(): pl.pallas_call(lambda *refs: product_kernel(turns, plan, len(pieces), *re...]
  transfers between devices with their start and end apart: 21 -> 21, of which waited for: 13 -> 13; matrix products, arithmetic and copies ran while one was open for 2% -> 2% of each run, Pallas kernels for 3% -> 6%
where the time goes in v6:
time: 91.4 us; the launch traced here: 91.1 us
  waiting for transfers between devices  45.7 us (50%)
  starting transfers between devices  32.9 us (36%)
  Pallas kernels  6.16 us (7%)
  blocking collectives  4.58 us (5%)
  other arithmetic  1.54 us (2%)
    ppermute x21, waiting for transfers between devices, permute(): return lax.ppermute(value, AXES, [(n, n ^ bits) for n in range(128)])  45.7 us
    ppermute x21, starting transfers between devices, permute(): return lax.ppermute(value, AXES, [(n, n ^ bits) for n in range(128)])  32.9 us
    pallas_call x2, Pallas kernels, product(): pl.pallas_call(lambda *refs: product_kernel(turns, plan, len(pieces), *re...  5.01 us
    all_to_all x1, blocking collectives, both_cores(): lax.all_to_all(jnp.broadcast_to(value[None], (2, *value.shape)), 'c', 0,...  4.58 us
  transfers between devices with their start and end apart: 21, of which 13 were waited for; matrix products, arithmetic and copies ran while one was open for 2% of the time, Pallas kernels for 6%

profile of v6, /device:TPU:0, one launch (start us, length us, event | category | flops | bytes accessed | tf_op | source)
XLA Modules:
  0.0 91.1 jit_solution(11365574322281142486)
XLA Ops:
  0.0 3.2 %collective-permute-start.2 = (f32[512,128]{1,0:T(8,128)}, f32[512,128]{1,0:T(8,128)S(1)}, u32[]{:S(2)}, u32[]{:S(2)}) collective-permute-start(f32[512,128]{1,0:T(8,128)} %param.5), channel_id=1, source_target_pairs={{0,32},{1,33},{2,34},{3,35},{4,36},{5,37},{6,38},{7,39},{8,40},{9,... | collective-permute-start | bytes 786440 | tf_op jit(solution)/shard_map/ppermute | solution.py:21
  4.3 6.6 %collective-permute-done.2 = f32[512,128]{1,0:T(8,128)S(1)} collective-permute-done((f32[512,128]{1,0:T(8,128)}, f32[512,128]{1,0:T(8,128)S(1)}, u32[]{:S(2)}, u32[]{:S(2)}) %collective-permute-start.2) | collective-permute-done | bytes 262176 | tf_op jit(solution)/shard_map/ppermute | solution.py:21
  10.9 1.0 %select_bitcast_fusion = (f32[1,512,128]{2,1,0:T(8,128)S(1)}, f32[1,512,128]{2,1,0:T(8,128)S(1)}) fusion(f32[512,128]{1,0:T(8,128)} %param.5, f32[512,128]{1,0:T(8,128)S(1)} %collective-permute-done.2, pred[]{:T(512)S(6)} %eq.3), kind=kLoop, calls=%fused_computation.25 | loop fusion | flops 131072 | bytes 1048577 | tf_op jit(solution)/shard_map/stack | solution.py:178
  11.9 3.8 %collective-permute-done.1 = f32[512,128]{1,0:T(8,128)S(1)} collective-permute-done((f32[512,128]{1,0:T(8,128)}, f32[512,128]{1,0:T(8,128)S(1)}, u32[]{:S(2)}, u32[]{:S(2)}) %collective-permute-start.1) | collective-permute-done | bytes 262176 | tf_op jit(solution)/shard_map/ppermute | solution.py:21
  15.9 1.7 %collective-permute-start.3 = (f32[2,512,128]{2,1,0:T(8,128)S(1)}, f32[2,512,128]{2,1,0:T(8,128)S(1)}, u32[]{:S(2)}, u32[]{:S(2)}) collective-permute-start(f32[2,512,128]{2,1,0:T(8,128)S(1)} %pad_maximum_fusion), channel_id=1, source_target_pairs={{0,64},{1,65},{2,66},{3,67},{4,68},{5,69},{6,70},{7,71},{8,72},{9,... | collective-permute-start | bytes 1572872 | tf_op jit(solution)/shard_map/ppermute | solution.py:21
  17.8 1.5 %shard_map.55 = (f32[1,256,256]{2,1,0:T(8,128)S(1)}, f32[3,256,256]{2,1,0:T(8,128)S(1)}, f32[2,256,256]{2,1,0:T(8,128)S(1)}, f32[2,256,256]{2,1,0:T(8,128)S(1)},...) custom-call(s32[5]{0:T(128)S(1)} %stack.44.refs_0_, ...), custom_call_target="tpu_custom_call" | custom-call | flops 1 | bytes 1 | tf_op jit(solution)/shard_map/pallas_call | solution.py:122
  19.3 6.9 %collective-permute-start.14 = (f32[2,256,256]{2,1,0:T(8,128)S(1)}, f32[2,256,256]{2,1,0:T(8,128)S(1)}, u32[]{:S(2)}, u32[]{:S(2)}) collective-permute-start(f32[2,256,256]{2,1,0:T(8,128)S(1)} %get-tuple-element.38), channel_id=1, source_target_pairs={{0,3},{1,2},{2,1},{3,0},{4,7},{5,6},{6,5},{7,4},{8,11},{9,10},{10,... | collective-permute-start | bytes 1572872 | tf_op jit(solution)/shard_map/ppermute | solution.py:21
  26.6 3.7 %collective-permute-done.3 = f32[2,512,128]{2,1,0:T(8,128)S(1)} collective-permute-done((f32[2,512,128]{2,1,0:T(8,128)S(1)}, f32[2,512,128]{2,1,0:T(8,128)S(1)}, u32[]{:S(2)}, u32[]{:S(2)}) %collective-permute-start.3) | collective-permute-done | bytes 524320 | tf_op jit(solution)/shard_map/ppermute | solution.py:21
  30.4 4.6 %all_to_all.5.refs_4_ = f32[2,2,512,128]{3,2,1,0:T(8,128)S(1)} all-to-all(f32[2,2,512,128]{3,2,1,0:T(8,128)S(1)} %broadcast_in_dim.2), channel_id=1, replica_groups=mesh['yl'=2,'x'=4,'c'=2,'yh'=2,'z'=4] {'c'}, dimensions={0} | all-to-all | bytes 2097152 | tf_op jit(solution)/shard_map/all_to_all | solution.py:168
  35.0 3.5 %shard_map.56 = (f32[4,256,256]{2,1,0:T(8,128)S(1)}, f32[4,256,256]{2,1,0:T(8,128)S(1)}, f32[3,256,256]{2,1,0:T(8,128)S(1)}, f32[3,256,256]{2,1,0:T(8,128)S(1)},...) custom-call(s32[5]{0:T(128)S(1)} %stack.44.refs_0_, s32[2,16]{1,0:T(2,128)S(1)} %copy-done.1, ...), custom_call_target="tpu_custom_call" | custom-call | flops 1 | bytes 1 | tf_op jit(solution)/shard_map/pallas_call | solution.py:122
  38.6 2.9 %collective-permute-start.15 = (f32[3,256,256]{2,1,0:T(8,128)S(1)}, f32[3,256,256]{2,1,0:T(8,128)S(1)}, u32[]{:S(2)}, u32[]{:S(2)}) collective-permute-start(f32[3,256,256]{2,1,0:T(8,128)S(1)} %shard_map.60), channel_id=1, source_target_pairs={{0,1},{1,0},{2,3},{3,2},{4,5},{5,4},{6,7},{7,6},{8,9},{9,8},{10,11... | collective-permute-start | bytes 2359304 | tf_op jit(solution)/shard_map/ppermute | solution.py:21
  42.1 5.2 %collective-permute-start.8 = (f32[4,256,256]{2,1,0:T(8,128)S(1)}, f32[4,256,256]{2,1,0:T(8,128)S(1)}, u32[]{:S(2)}, u32[]{:S(2)}) collective-permute-start(f32[4,256,256]{2,1,0:T(8,128)S(1)} %shard_map.58), channel_id=1, source_target_pairs={{0,68},{1,69},{2,70},{3,71},{4,64},{5,65},{6,66},{7,67},{8,76},{9,... | collective-permute-start | bytes 3145736 | tf_op jit(solution)/shard_map/ppermute | solution.py:21
  47.5 12.4 %collective-permute-done.15.arrived_ref = f32[3,256,256]{2,1,0:T(8,128)S(1)} collective-permute-done((f32[3,256,256]{2,1,0:T(8,128)S(1)}, f32[3,256,256]{2,1,0:T(8,128)S(1)}, u32[]{:S(2)}, u32[]{:S(2)}) %collective-permute-start.15) | collective-permute-done | bytes 786464 | tf_op jit(solution)/shard_map/ppermute | solution.py:21
  59.9 1.7 %collective-permute-start.17 = (f32[1,256,256]{2,1,0:T(8,128)S(1)}, f32[1,256,256]{2,1,0:T(8,128)S(1)}, u32[]{:S(2)}, u32[]{:S(2)}) collective-permute-start(f32[1,256,256]{2,1,0:T(8,128)S(1)} %shard_map.61), channel_id=1, source_target_pairs={{0,3},{1,2},{2,1},{3,0},{4,7},{5,6},{6,5},{7,4},{8,11},{9,10},{10,... | collective-permute-start | bytes 786440 | tf_op jit(solution)/shard_map/ppermute | solution.py:21
  61.6 1.1 %collective-permute-done.13.arrived_ref = f32[3,256,256]{2,1,0:T(8,128)S(1)} collective-permute-done((f32[3,256,256]{2,1,0:T(8,128)S(1)}, f32[3,256,256]{2,1,0:T(8,128)S(1)}, u32[]{:S(2)}, u32[]{:S(2)}) %collective-permute-start.13) | collective-permute-done | bytes 786464 | tf_op jit(solution)/shard_map/ppermute | solution.py:21
  62.8 6.7 %collective-permute-done.17 = f32[1,256,256]{2,1,0:T(8,128)S(1)} collective-permute-done((f32[1,256,256]{2,1,0:T(8,128)S(1)}, f32[1,256,256]{2,1,0:T(8,128)S(1)}, u32[]{:S(2)}, u32[]{:S(2)}) %collective-permute-start.17) | collective-permute-done | bytes 262176 | tf_op jit(solution)/shard_map/ppermute | solution.py:21
  69.5 1.1 %collective-permute-done.19 = f32[1,256,256]{2,1,0:T(8,128)S(1)} collective-permute-done((f32[1,256,256]{2,1,0:T(8,128)S(1)}, f32[1,256,256]{2,1,0:T(8,128)S(1)}, u32[]{:S(2)}, u32[]{:S(2)}) %collective-permute-start.19) | collective-permute-done | bytes 262176 | tf_op jit(solution)/shard_map/ppermute | solution.py:21
  70.9 2.2 %collective-permute-start.18 = (f32[256,256]{1,0:T(8,128)S(1)}, f32[256,256]{1,0:T(8,128)S(1)}, u32[]{:S(2)}, u32[]{:S(2)}) collective-permute-start(f32[256,256]{1,0:T(8,128)S(1)} %get-tuple-element.49), channel_id=1, source_target_pairs={{0,64},{1,65},{2,66},{3,67},{4,68},{5,69},{6,70},{7,71},{8,72},{9,... | collective-permute-start | bytes 786440 | tf_op jit(solution)/shard_map/ppermute | solution.py:21
  73.0 3.5 %collective-permute-start.16 = (f32[256,256]{1,0:T(8,128)S(1)}, f32[256,256]{1,0:T(8,128)S(1)}, u32[]{:S(2)}, u32[]{:S(2)}) collective-permute-start(f32[256,256]{1,0:T(8,128)S(1)} %get-tuple-element.50), channel_id=1, source_target_pairs={{0,4},{1,5},{2,6},{3,7},{4,0},{5,1},{6,2},{7,3},{8,12},{9,13},{10,... | collective-permute-start | bytes 786440 | tf_op jit(solution)/shard_map/ppermute | solution.py:21
  76.7 1.6 %collective-permute-start.11 = (f32[256,256]{1,0:T(8,128)S(1)}, f32[256,256]{1,0:T(8,128)S(1)}, u32[]{:S(2)}, u32[]{:S(2)}) collective-permute-start(f32[256,256]{1,0:T(8,128)S(1)} %get-tuple-element.43), channel_id=1, source_target_pairs={{0,2},{1,3},{2,0},{3,1},{4,6},{5,7},{6,4},{7,5},{8,10},{9,11},{10,... | collective-permute-start | bytes 786440 | tf_op jit(solution)/shard_map/ppermute | solution.py:21
  78.3 1.5 %collective-permute-start.10 = (f32[256,256]{1,0:T(8,128)S(1)}, f32[256,256]{1,0:T(8,128)S(1)}, u32[]{:S(2)}, u32[]{:S(2)}) collective-permute-start(f32[256,256]{1,0:T(8,128)S(1)} %get-tuple-element.44), channel_id=1, source_target_pairs={{0,3},{1,2},{2,1},{3,0},{4,7},{5,6},{6,5},{7,4},{8,11},{9,10},{10,... | collective-permute-start | bytes 786440 | tf_op jit(solution)/shard_map/ppermute | solution.py:21
  80.5 6.5 %collective-permute-done.16.refs_5_ = f32[256,256]{1,0:T(8,128)S(1)} collective-permute-done((f32[256,256]{1,0:T(8,128)S(1)}, f32[256,256]{1,0:T(8,128)S(1)}, u32[]{:S(2)}, u32[]{:S(2)}) %collective-permute-start.16) | collective-permute-done | bytes 262176 | tf_op jit(solution)/shard_map/ppermute | solution.py:21
  87.0 2.6 %collective-permute-done.20.refs_7_ = f32[256,256]{1,0:T(8,128)S(1)} collective-permute-done((f32[256,256]{1,0:T(8,128)S(1)}, f32[256,256]{1,0:T(8,128)S(1)}, u32[]{:S(2)}, u32[]{:S(2)}) %collective-permute-start.20) | collective-permute-done | bytes 262176 | tf_op jit(solution)/shard_map/ppermute | solution.py:21
  90.2 0.9 %shard_map.63 = f32[512,256]{1,0:T(8,128)} custom-call(f32[256,256]{1,0:T(8,128)S(1)} %get-tuple-element.46.refs_0_, f32[256,256]{1,0:T(8,128)S(1)} %collective-permute-done.9.refs_1_, f32[256,256]{1,0:T(8,128)S(1)} %collective-permute-done.10.refs_2_, f32[256,256]{1,0:T(8,128)S(1)} %collective-permute-done.11.refs_3_, ...), custom_call_target="tpu_custom_call" | custom-call | flops 1 | bytes 1 | tf_op jit(solution)/shard_map/pallas_call | solution.py:159
  (42 shorter events, 4.8 us)
Async XLA Ops:
  0.0 17.8 %copy-start.2 = (s32[2,32]{1,0:T(2,128)S(1)}, s32[2,32]{1,0:T(2,128)}, u32[]{:S(2)}) copy-start(s32[2,32]{1,0:T(2,128)} %refs_3_.3) | copy-start | bytes 772
  0.0 17.8 %copy-start = (s32[16,32]{1,0:T(8,128)S(1)}, s32[16,32]{1,0:T(8,128)}, u32[]{:S(2)}) copy-start(s32[16,32]{1,0:T(8,128)} %refs_2_.3) | copy-start | bytes 6148
  0.0 17.8 %copy-start.1 = (s32[2,16]{1,0:T(2,128)S(1)}, s32[2,16]{1,0:T(2,128)}, u32[]{:S(2)}) copy-start(s32[2,16]{1,0:T(2,128)} %refs_1_.3) | copy-start | bytes 388
  0.0 10.9 %collective-permute-start.2 = (f32[512,128]{1,0:T(8,128)}, f32[512,128]{1,0:T(8,128)S(1)}, u32[]{:S(2)}, u32[]{:S(2)}) collective-permute-start(f32[512,128]{1,0:T(8,128)} %param.5), channel_id=1, source_target_pairs={{0,32},{1,33},{2,34},{3,35},{4,36},{5,37},{6,38},{7,39},{8,40},{9,... | collective-permute-start | bytes 786440 | tf_op jit(solution)/shard_map/ppermute | solution.py:21
  3.2 12.5 %collective-permute-start.1 = (f32[512,128]{1,0:T(8,128)}, f32[512,128]{1,0:T(8,128)S(1)}, u32[]{:S(2)}, u32[]{:S(2)}) collective-permute-start(f32[512,128]{1,0:T(8,128)} %param.5), channel_id=1, source_target_pairs={{0,16},{1,17},{2,18},{3,19},{4,20},{5,21},{6,22},{7,23},{8,24},{9,... | collective-permute-start | bytes 786440 | tf_op jit(solution)/shard_map/ppermute | solution.py:21
  3.8 11.9 %collective-permute-start = (f32[512,128]{1,0:T(8,128)}, f32[512,128]{1,0:T(8,128)S(1)}, u32[]{:S(2)}, u32[]{:S(2)}) collective-permute-start(f32[512,128]{1,0:T(8,128)} %param.5), channel_id=1, source_target_pairs={{0,48},{1,49},{2,50},{3,51},{4,52},{5,53},{6,54},{7,55},{8,56},{9,... | collective-permute-start | bytes 786440 | tf_op jit(solution)/shard_map/ppermute | solution.py:21
  15.8 2.0 %collective-permute-start.4 = (f32[2,512,128]{2,1,0:T(8,128)S(1)}, f32[2,512,128]{2,1,0:T(8,128)S(1)}, u32[]{:S(2)}, u32[]{:S(2)}) collective-permute-start(f32[2,512,128]{2,1,0:T(8,128)S(1)} %pad_maximum_fusion.1.refs_4_), channel_id=1, source_target_pairs={{0,8},{1,9},{2,10},{3,11},{4,12},{5,13},{6,14},{7,15},{8,0},{9,1},... | collective-permute-start | bytes 1572872 | tf_op jit(solution)/shard_map/ppermute | solution.py:21
  15.9 14.4 %collective-permute-start.3 = (f32[2,512,128]{2,1,0:T(8,128)S(1)}, f32[2,512,128]{2,1,0:T(8,128)S(1)}, u32[]{:S(2)}, u32[]{:S(2)}) collective-permute-start(f32[2,512,128]{2,1,0:T(8,128)S(1)} %pad_maximum_fusion), channel_id=1, source_target_pairs={{0,64},{1,65},{2,66},{3,67},{4,68},{5,69},{6,70},{7,71},{8,72},{9,... | collective-permute-start | bytes 1572872 | tf_op jit(solution)/shard_map/ppermute | solution.py:21
  19.3 19.2 %collective-permute-start.14 = (f32[2,256,256]{2,1,0:T(8,128)S(1)}, f32[2,256,256]{2,1,0:T(8,128)S(1)}, u32[]{:S(2)}, u32[]{:S(2)}) collective-permute-start(f32[2,256,256]{2,1,0:T(8,128)S(1)} %get-tuple-element.38), channel_id=1, source_target_pairs={{0,3},{1,2},{2,1},{3,0},{4,7},{5,6},{6,5},{7,4},{8,11},{9,10},{10,... | collective-permute-start | bytes 1572872 | tf_op jit(solution)/shard_map/ppermute | solution.py:21
  26.2 15.2 %collective-permute-start.12 = (f32[2,256,256]{2,1,0:T(8,128)S(1)}, f32[2,256,256]{2,1,0:T(8,128)S(1)}, u32[]{:S(2)}, u32[]{:S(2)}) collective-permute-start(f32[2,256,256]{2,1,0:T(8,128)S(1)} %get-tuple-element.34), channel_id=1, source_target_pairs={{0,1},{1,0},{2,3},{3,2},{4,5},{5,4},{6,7},{7,6},{8,9},{9,8},{10,11... | collective-permute-start | bytes 1572872 | tf_op jit(solution)/shard_map/ppermute | solution.py:21
  26.2 21.1 %collective-permute-start.6 = (f32[3,256,256]{2,1,0:T(8,128)S(1)}, f32[3,256,256]{2,1,0:T(8,128)S(1)}, u32[]{:S(2)}, u32[]{:S(2)}) collective-permute-start(f32[3,256,256]{2,1,0:T(8,128)S(1)} %get-tuple-element.30), channel_id=1, source_target_pairs={{0,68},{1,69},{2,70},{3,71},{4,64},{5,65},{6,66},{7,67},{8,76},{9,... | collective-permute-start | bytes 2359304 | tf_op jit(solution)/shard_map/ppermute | solution.py:21
  26.4 8.6 %collective-permute-start.5 = (f32[1,256,256]{2,1,0:T(8,128)S(1)}, f32[1,256,256]{2,1,0:T(8,128)S(1)}, u32[]{:S(2)}, u32[]{:S(2)}) collective-permute-start(f32[1,256,256]{2,1,0:T(8,128)S(1)} %get-tuple-element.27), channel_id=1, source_target_pairs={{0,64},{1,65},{2,66},{3,67},{4,68},{5,69},{6,70},{7,71},{8,72},{9,... | collective-permute-start | bytes 786440 | tf_op jit(solution)/shard_map/ppermute | solution.py:21
  38.6 21.3 %collective-permute-start.15 = (f32[3,256,256]{2,1,0:T(8,128)S(1)}, f32[3,256,256]{2,1,0:T(8,128)S(1)}, u32[]{:S(2)}, u32[]{:S(2)}) collective-permute-start(f32[3,256,256]{2,1,0:T(8,128)S(1)} %shard_map.60), channel_id=1, source_target_pairs={{0,1},{1,0},{2,3},{3,2},{4,5},{5,4},{6,7},{7,6},{8,9},{9,8},{10,11... | collective-permute-start | bytes 2359304 | tf_op jit(solution)/shard_map/ppermute | solution.py:21
  41.5 21.2 %collective-permute-start.13 = (f32[3,256,256]{2,1,0:T(8,128)S(1)}, f32[3,256,256]{2,1,0:T(8,128)S(1)}, u32[]{:S(2)}, u32[]{:S(2)}) collective-permute-start(f32[3,256,256]{2,1,0:T(8,128)S(1)} %shard_map.59), channel_id=1, source_target_pairs={{0,3},{1,2},{2,1},{3,0},{4,7},{5,6},{6,5},{7,4},{8,11},{9,10},{10,... | collective-permute-start | bytes 2359304 | tf_op jit(solution)/shard_map/ppermute | solution.py:21
  42.1 34.4 %collective-permute-start.8 = (f32[4,256,256]{2,1,0:T(8,128)S(1)}, f32[4,256,256]{2,1,0:T(8,128)S(1)}, u32[]{:S(2)}, u32[]{:S(2)}) collective-permute-start(f32[4,256,256]{2,1,0:T(8,128)S(1)} %shard_map.58), channel_id=1, source_target_pairs={{0,68},{1,69},{2,70},{3,71},{4,64},{5,65},{6,66},{7,67},{8,76},{9,... | collective-permute-start | bytes 3145736 | tf_op jit(solution)/shard_map/ppermute | solution.py:21
  47.4 29.1 %collective-permute-start.7 = (f32[4,256,256]{2,1,0:T(8,128)S(1)}, f32[4,256,256]{2,1,0:T(8,128)S(1)}, u32[]{:S(2)}, u32[]{:S(2)}) collective-permute-start(f32[4,256,256]{2,1,0:T(8,128)S(1)} %shard_map.57), channel_id=1, source_target_pairs={{0,64},{1,65},{2,66},{3,67},{4,68},{5,69},{6,70},{7,71},{8,72},{9,... | collective-permute-start | bytes 3145736 | tf_op jit(solution)/shard_map/ppermute | solution.py:21
  59.9 9.6 %collective-permute-start.17 = (f32[1,256,256]{2,1,0:T(8,128)S(1)}, f32[1,256,256]{2,1,0:T(8,128)S(1)}, u32[]{:S(2)}, u32[]{:S(2)}) collective-permute-start(f32[1,256,256]{2,1,0:T(8,128)S(1)} %shard_map.61), channel_id=1, source_target_pairs={{0,3},{1,2},{2,1},{3,0},{4,7},{5,6},{6,5},{7,4},{8,11},{9,10},{10,... | collective-permute-start | bytes 786440 | tf_op jit(solution)/shard_map/ppermute | solution.py:21
  62.7 7.9 %collective-permute-start.19 = (f32[1,256,256]{2,1,0:T(8,128)S(1)}, f32[1,256,256]{2,1,0:T(8,128)S(1)}, u32[]{:S(2)}, u32[]{:S(2)}) collective-permute-start(f32[1,256,256]{2,1,0:T(8,128)S(1)} %shard_map.62), channel_id=1, source_target_pairs={{0,1},{1,0},{2,3},{3,2},{4,5},{5,4},{6,7},{7,6},{8,9},{9,8},{10,11... | collective-permute-start | bytes 786440 | tf_op jit(solution)/shard_map/ppermute | solution.py:21
  70.9 9.4 %collective-permute-start.18 = (f32[256,256]{1,0:T(8,128)S(1)}, f32[256,256]{1,0:T(8,128)S(1)}, u32[]{:S(2)}, u32[]{:S(2)}) collective-permute-start(f32[256,256]{1,0:T(8,128)S(1)} %get-tuple-element.49), channel_id=1, source_target_pairs={{0,64},{1,65},{2,66},{3,67},{4,68},{5,69},{6,70},{7,71},{8,72},{9,... | collective-permute-start | bytes 786440 | tf_op jit(solution)/shard_map/ppermute | solution.py:21
  73.0 14.0 %collective-permute-start.16 = (f32[256,256]{1,0:T(8,128)S(1)}, f32[256,256]{1,0:T(8,128)S(1)}, u32[]{:S(2)}, u32[]{:S(2)}) collective-permute-start(f32[256,256]{1,0:T(8,128)S(1)} %get-tuple-element.50), channel_id=1, source_target_pairs={{0,4},{1,5},{2,6},{3,7},{4,0},{5,1},{6,2},{7,3},{8,12},{9,13},{10,... | collective-permute-start | bytes 786440 | tf_op jit(solution)/shard_map/ppermute | solution.py:21
  76.5 13.1 %collective-permute-start.20 = (f32[256,256]{1,0:T(8,128)S(1)}, f32[256,256]{1,0:T(8,128)S(1)}, u32[]{:S(2)}, u32[]{:S(2)}) collective-permute-start(f32[256,256]{1,0:T(8,128)S(1)} %get-tuple-element.52), channel_id=1, source_target_pairs={{0,68},{1,69},{2,70},{3,71},{4,64},{5,65},{6,66},{7,67},{8,76},{9,... | collective-permute-start | bytes 786440 | tf_op jit(solution)/shard_map/ppermute | solution.py:21
  76.7 12.9 %collective-permute-start.11 = (f32[256,256]{1,0:T(8,128)S(1)}, f32[256,256]{1,0:T(8,128)S(1)}, u32[]{:S(2)}, u32[]{:S(2)}) collective-permute-start(f32[256,256]{1,0:T(8,128)S(1)} %get-tuple-element.43), channel_id=1, source_target_pairs={{0,2},{1,3},{2,0},{3,1},{4,6},{5,7},{6,4},{7,5},{8,10},{9,11},{10,... | collective-permute-start | bytes 786440 | tf_op jit(solution)/shard_map/ppermute | solution.py:21
  78.3 11.9 %collective-permute-start.10 = (f32[256,256]{1,0:T(8,128)S(1)}, f32[256,256]{1,0:T(8,128)S(1)}, u32[]{:S(2)}, u32[]{:S(2)}) collective-permute-start(f32[256,256]{1,0:T(8,128)S(1)} %get-tuple-element.44), channel_id=1, source_target_pairs={{0,3},{1,2},{2,1},{3,0},{4,7},{5,6},{6,5},{7,4},{8,11},{9,10},{10,... | collective-permute-start | bytes 786440 | tf_op jit(solution)/shard_map/ppermute | solution.py:21
  80.2 10.0 %collective-permute-start.9 = (f32[256,256]{1,0:T(8,128)S(1)}, f32[256,256]{1,0:T(8,128)S(1)}, u32[]{:S(2)}, u32[]{:S(2)}) collective-permute-start(f32[256,256]{1,0:T(8,128)S(1)} %get-tuple-element.45), channel_id=1, source_target_pairs={{0,1},{1,0},{2,3},{3,2},{4,5},{5,4},{6,7},{7,6},{8,9},{9,8},{10,11... | collective-permute-start | bytes 786440 | tf_op jit(solution)/shard_map/ppermute | solution.py:21
